TPU v7x, 256 devices: a whole 4x4x8 slice. The times are simulated.
256 devices in a mesh: section: 32 (over y, z_lo, core), dp: 8 (over x, z_hi).
Axes of the slice: x: 4, y: 4, z: 8 (z_hi: 2, z_lo: 4; z = z_hi * 4 + z_lo), core: 2. Of those that a mesh axis runs over, the one named last changes fastest.
Arguments:
- section_states: bfloat16 [32, 4, 8, 16, 16, 512], P('section', None, 'dp'), may hold values from -6 to 6
- conv_kernels: bfloat16 [32, 2, 1152, 512], P('section'), may hold values from -0.1875 to 0.1875
- top_feed: bfloat16 [3, 4, 8, 16, 16, 512], P(None, None, 'dp'), may hold values from -6 to 6
Outputs:
- final_states: bfloat16 [32, 4, 8, 16, 16, 512], P('section', None, 'dp')
- kernel_grads: float32 [32, 2, 1152, 512], P('section', None, 'dp')
All inputs are finite; a program needn't handle non-finite values.
Results may differ from a plain program's by a relative error of at most 0.024.
Values may be sent and summed in bfloat16 or wider, within the bound.
No kernel may reach another device: no remote copies, remote signals or barrier semaphores. Data moves between devices by JAX's collectives and lax.ppermute only.
A program may use at most 128 MiB of HBM per device.

v0:
```python
import functools

import jax
import jax.numpy as jnp
from jax import lax
from jax.experimental import pallas as pl
from jax.experimental.pallas import tpu as pltpu
from jax.sharding import Mesh
from jax.sharding import PartitionSpec as P

GW = 128
HW = 16
TICKS = 4
CELLS = HW * HW
ROWS = 9 * GW
HALVES = 2
VMEM_LIMIT = 24 * 1024 * 1024


def column_shifts(field, at_left, at_right):
    before = jnp.where(at_left, 0.0, pltpu.roll(field, 1, 0))
    after = jnp.where(at_right, 0.0, pltpu.roll(field, CELLS - 1, 0))
    return jnp.concatenate(
        [before.astype(jnp.bfloat16), field.astype(jnp.bfloat16), after.astype(jnp.bfloat16)], axis=1
    )


def row_shifts(field):
    edge = jnp.zeros((HW, GW), field.dtype)
    up = jnp.concatenate([field[HW:], edge], axis=0)
    down = jnp.concatenate([edge, field[:-HW]], axis=0)
    return jnp.concatenate([up, field, down], axis=1)


def taps_by_row(kernel_ref, branch, lanes):
    return jnp.concatenate(
        [kernel_ref[branch, pl.ds(a * 3 * GW, 3 * GW), lanes] for a in range(3)], axis=1
    )


def conv(stack, kernel):
    parts = jnp.dot(stack, kernel, preferred_element_type=jnp.float32)
    edge = jnp.zeros((HW, GW), jnp.float32)
    above = jnp.concatenate([edge, parts[:-HW, :GW]], axis=0)
    below = jnp.concatenate([parts[HW:, 2 * GW :], edge], axis=0)
    return parts[:, GW : 2 * GW] + above + below


def conv_back(stack, kernel, at_left, at_right):
    parts = lax.dot_general(
        stack, kernel, (((1,), (1,)), ((), ())), preferred_element_type=jnp.float32
    )
    before = jnp.where(at_right, 0.0, pltpu.roll(parts[:, :GW], CELLS - 1, 0))
    after = jnp.where(at_left, 0.0, pltpu.roll(parts[:, 2 * GW :], 1, 0))
    return parts[:, GW : 2 * GW] + before + after


def correlate(columns, rows):
    return lax.dot_general(
        columns, rows, (((0,), (0,)), ((), ())), preferred_element_type=jnp.float32
    )


def masks():
    column = lax.rem(lax.broadcasted_iota(jnp.int32, (CELLS, GW), 0), HW)
    return column == 0, column == HW - 1


def section_back(state_ref, lanes, kernel_g, kernel_f, store, keep):
    edges = masks()
    grad_two = state_ref[3, :, lanes]
    out_one = state_ref[0, :, lanes].astype(jnp.float32)
    sigma_one = jax.nn.sigmoid(out_one)
    slope_one = sigma_one * (1.0 + out_one * (1.0 - sigma_one))
    act_one = out_one * sigma_one
    columns_one = column_shifts(act_one, *edges)
    rows_two = row_shifts(grad_two)

    weights = kernel_g()
    in_two = (state_ref[1, :, lanes].astype(jnp.float32) - conv(columns_one, weights)).astype(
        jnp.bfloat16
    )
    total_one = (
        state_ref[2, :, lanes].astype(jnp.float32)
        + conv_back(rows_two, weights, *edges) * slope_one
    ).astype(jnp.bfloat16)
    rows_one = row_shifts(total_one)

    wide_two = in_two.astype(jnp.float32)
    sigma_two = jax.nn.sigmoid(wide_two)
    slope_two = sigma_two * (1.0 + wide_two * (1.0 - sigma_two))
    act_two = wide_two * sigma_two
    columns_two = column_shifts(act_two, *edges)

    weights = kernel_f()
    in_one = (out_one - conv(columns_two, weights)).astype(jnp.bfloat16)
    total_two = (
        grad_two.astype(jnp.float32) + conv_back(rows_one, weights, *edges) * slope_two
    ).astype(jnp.bfloat16)
    for at, stream in enumerate((in_one, in_two, total_one, total_two)):
        store(at, stream)
    keep(act_one, act_two, grad_two, total_one, columns_one, columns_two, rows_two, rows_one)


def group_lanes(group):
    return pl.ds(group * GW, GW)


def kernel_loads(half, width, kernels, held, sems):
    copies = {}
    for group in range(width // GW):
        wide = pl.ds(half * width + group * GW, GW)
        for branch in (1, 0):
            copies[group, branch] = pltpu.make_async_copy(
                kernels.at[branch, :, wide],
                held.at[branch, :, group_lanes(group)],
                sems.at[branch, group],
            )
            copies[group, branch].start()

    def loaded(group, branch):
        copies[group, branch].wait()
        return taps_by_row(held, branch, group_lanes(group))

    return loaded


def take_top(is_top, tick, half, width, top, made, sem):
    @pl.when(is_top[0] == 1)
    def _():
        copy = pltpu.make_async_copy(
            top.at[tick - 1, :, :, pl.ds(half * width, width)], made, sem
        )
        copy.start()
        copy.wait()


def early_tick(tick, half, width, *refs):
    if tick:
        is_top, received, top, kernels, earlier, made, kept, turn, held, sent, sems, sem, out_sems = refs
    else:
        states, kernels, earlier, made, kept, turn, held, sent, sems, sem, out_sems = refs
    if not tick:
        copies = []
        for group in range(width // GW):
            lanes = group_lanes(group)
            wide = pl.ds(half * width + group * GW, GW)
            copies.append(
                pltpu.make_async_copy(states.at[:, :, wide], made.at[:, :, lanes], sem.at[group])
            )
            copies[-1].start()
    loaded = kernel_loads(half, width, kernels, held, sems)
    turn[...] = jnp.zeros_like(turn)
    if tick:
        take_top(is_top, tick, half, width, top, made, sem.at[0])
    outgoing = []
    for group in range(width // GW):
        lanes = group_lanes(group)
        if not tick:
            copies[group].wait()

        def store(at, stream):
            made[at, :, lanes] = stream

        def keep(act_one, act_two, grad_two, total_one, *stacks):
            sent[0, :, lanes] = act_two.astype(jnp.bfloat16)
            sent[1, :, lanes] = act_one.astype(jnp.bfloat16)
            sent[2, :, lanes] = total_one
            sent[3, :, lanes] = grad_two
            copy = pltpu.make_async_copy(
                sent.at[:, :, lanes], kept.at[:, :, lanes], out_sems.at[group]
            )
            copy.start()
            outgoing.append(copy)

        section_back(
            made,
            lanes,
            functools.partial(loaded, group, 1),
            functools.partial(loaded, group, 0),
            store,
            keep,
        )
    for copy in outgoing:
        copy.wait()


def early_terms(width, *refs):
    kept = refs[: TICKS - 1]
    earlier, total, turn, fields, summed, sems, out_sems = refs[TICKS - 1 :]
    turn[...] = jnp.zeros_like(turn)
    edges = masks()
    copies = {}
    for group in range(width // GW):
        lanes = group_lanes(group)
        for tick in range(TICKS - 1):
            copies[group, tick] = pltpu.make_async_copy(
                kept[tick].at[:, :, lanes], fields.at[tick, :, :, lanes], sems.at[tick, group]
            )
            copies[group, tick].start()
    outgoing = []
    for group in range(width // GW):
        lanes = group_lanes(group)
        for tick in range(TICKS - 1):
            copies[group, tick].wait()
        for branch in range(2):
            columns = jnp.concatenate(
                [
                    column_shifts(fields[tick, branch, :, lanes].astype(jnp.float32), *edges)
                    for tick in range(TICKS - 1)
                ],
                axis=0,
            )
            rows = jnp.concatenate(
                [row_shifts(fields[tick, 2 + branch, :, lanes]) for tick in range(TICKS - 1)], axis=0
            )
            term = correlate(columns, rows)
            for a in range(3):
                summed[branch, pl.ds(a * 3 * GW, 3 * GW), lanes] = term[:, a * GW : (a + 1) * GW]
            copy = pltpu.make_async_copy(
                summed.at[branch, :, lanes], total.at[branch, :, lanes], out_sems.at[branch, group]
            )
            copy.start()
            outgoing.append(copy)
    for copy in outgoing:
        copy.wait()


def last_tick(half, width, is_top, received, top, kernels, total, earlier, *rest):
    made, final, share, turn, held, summed, sent, sems, sem, total_sem, final_sem, share_sems = rest[-12:]
    loaded = kernel_loads(half, width, kernels, held, sems)
    total_copy = pltpu.make_async_copy(total, summed, total_sem)
    total_copy.start()
    turn[...] = jnp.zeros_like(turn)
    take_top(is_top, TICKS - 1, half, width, top, made, sem)
    outgoing = []
    for group in range(width // GW):
        lanes = group_lanes(group)

        def store(at, stream):
            made[at, :, lanes] = stream

        def keep(act_one, act_two, grad_two, total_one, columns_one, columns_two, rows_two, rows_one):
            if not group:
                total_copy.wait()
            for branch, pair in ((1, (columns_one, rows_two)), (0, (columns_two, rows_one))):
                term = correlate(*pair)
                for a in range(3):
                    rows = pl.ds(a * 3 * GW, 3 * GW)
                    sent[branch, rows, lanes] = (
                        summed[branch, rows, lanes] + term[:, a * GW : (a + 1) * GW]
                    ).astype(jnp.bfloat16)
                copy = pltpu.make_async_copy(
                    sent.at[branch, :, lanes], share.at[branch, :, lanes], share_sems.at[branch, group]
                )
                copy.start()
                outgoing.append(copy)

        section_back(
            made,
            lanes,
            functools.partial(loaded, group, 1),
            functools.partial(loaded, group, 0),
            store,
            keep,
        )
    copy = pltpu.make_async_copy(made, final.at[:, :, pl.ds(half * width, width)], final_sem)
    copy.start()
    outgoing.append(copy)
    for copy in outgoing:
        copy.wait()


ANY_REF = pl.BlockSpec(memory_space=pl.ANY)
VMEM_REF = pl.BlockSpec(memory_space=pltpu.VMEM)
SMEM_REF = pl.BlockSpec(memory_space=pltpu.SMEM)


def in_vmem(array):
    return pltpu.with_memory_space_constraint(array, pltpu.VMEM)


def in_hbm(array):
    return pltpu.with_memory_space_constraint(array, pltpu.HBM)


def params():
    return pltpu.CompilerParams(vmem_limit_bytes=VMEM_LIMIT)


def cost(products, width):
    groups = width // GW
    return pl.CostEstimate(
        flops=products * 2 * CELLS * ROWS * GW * groups,
        bytes_accessed=4 * 4 * CELLS * width,
        transcendentals=2 * CELLS * width,
    )


def passed_down(value):
    count = lax.axis_size("section")
    return lax.ppermute(value, "section", [(source, source - 1) for source in range(1, count)])


def on_device(section_states, conv_kernels, top_feed):
    chans = section_states.shape[-1]
    width = chans // HALVES
    states = in_hbm(section_states.reshape(4, CELLS, chans))
    kernels = in_hbm(conv_kernels[0])
    top = in_hbm(top_feed.reshape(TICKS - 1, 4, CELLS, chans))
    is_top = (lax.axis_index("section") == lax.axis_size("section") - 1).astype(jnp.int32)[None]

    groups = width // GW
    state_type = pltpu.VMEM((4, CELLS, width), jnp.bfloat16)
    kept_type = pltpu.HBM((4, CELLS, width), jnp.bfloat16)
    turn_type = pltpu.VMEM((8, 128), jnp.float32)
    held_scratch = pltpu.VMEM((2, ROWS, width), jnp.bfloat16)
    turn = jnp.zeros((8, 128), jnp.float32)
    made, kept = [None] * HALVES, [[] for _ in range(HALVES)]
    for tick in range(TICKS - 1):
        for half in range(HALVES):
            operands, specs = [states, kernels, turn], [ANY_REF] * 3
            if tick:
                operands = [is_top, in_vmem(made[half]), top, kernels, turn]
                specs = [SMEM_REF, VMEM_REF, ANY_REF, ANY_REF, ANY_REF]
            out, fields, turn = pl.pallas_call(
                functools.partial(early_tick, tick, half, width),
                out_shape=(state_type, kept_type, turn_type),
                in_specs=specs,
                out_specs=(VMEM_REF, ANY_REF, VMEM_REF),
                scratch_shapes=[
                    held_scratch,
                    pltpu.VMEM((4, CELLS, width), jnp.bfloat16),
                    pltpu.SemaphoreType.DMA((2, groups)),
                    pltpu.SemaphoreType.DMA((groups,)),
                    pltpu.SemaphoreType.DMA((groups,)),
                ],
                input_output_aliases={1: 0} if tick else {},
                compiler_params=params(),
                cost_estimate=cost(4, width),
                name=f"tick_{tick}_{half}",
            )(*operands)
            made[half] = passed_down(out)
            kept[half].append(in_hbm(fields))

    total = []
    for half in range(HALVES):
        summed, turn = pl.pallas_call(
            functools.partial(early_terms, width),
            out_shape=(pltpu.HBM((2, ROWS, width), jnp.float32), turn_type),
            in_specs=[ANY_REF] * TICKS,
            out_specs=(ANY_REF, VMEM_REF),
            scratch_shapes=[
                pltpu.VMEM((TICKS - 1, 4, CELLS, width), jnp.bfloat16),
                pltpu.VMEM((2, ROWS, width), jnp.float32),
                pltpu.SemaphoreType.DMA((TICKS - 1, groups)),
                pltpu.SemaphoreType.DMA((2, groups)),
            ],
            compiler_params=params(),
            cost_estimate=cost(2 * (TICKS - 1), width),
            name=f"early_terms_{half}",
        )(*kept[half], turn)
        total.append(in_hbm(summed))

    final = None
    shares = []
    for half in range(HALVES):
        operands = [is_top, in_vmem(made[half]), top, kernels, total[half], turn]
        specs = [SMEM_REF, VMEM_REF, ANY_REF, ANY_REF, ANY_REF, ANY_REF]
        aliases = {1: 0}
        if half:
            operands.append(in_hbm(final))
            specs.append(ANY_REF)
            aliases[6] = 1
        _, final, share, turn = pl.pallas_call(
            functools.partial(last_tick, half, width),
            out_shape=(
                state_type,
                pltpu.HBM((4, CELLS, chans), jnp.bfloat16),
                pltpu.HBM((2, ROWS, width), jnp.bfloat16),
                turn_type,
            ),
            in_specs=specs,
            out_specs=(VMEM_REF, ANY_REF, ANY_REF, VMEM_REF),
            scratch_shapes=[
                held_scratch,
                pltpu.VMEM((2, ROWS, width), jnp.float32),
                pltpu.VMEM((2, ROWS, width), jnp.bfloat16),
                pltpu.SemaphoreType.DMA((2, groups)),
                pltpu.SemaphoreType.DMA(()),
                pltpu.SemaphoreType.DMA(()),
                pltpu.SemaphoreType.DMA(()),
                pltpu.SemaphoreType.DMA((2, groups)),
            ],
            input_output_aliases=aliases,
            compiler_params=params(),
            cost_estimate=cost(6, width),
            name=f"last_tick_{half}",
        )(*operands)
        for axis in ("dp_0", "dp_1"):
            share = lax.psum_scatter(share, axis, scatter_dimension=1, tiled=True)
        shares.append(share)
    grads = jnp.concatenate(shares, axis=2).astype(jnp.float32) * (1.0 / (HW * HW))
    return (final.reshape(1, 4, 1, HW, HW, chans), grads[None])


def solution(mesh):
    finer = Mesh(mesh.devices.reshape(mesh.shape["section"], 4, 2), ("section", "dp_0", "dp_1"))
    images = ("dp_0", "dp_1")
    in_specs = (
        P("section", None, images, None, None, None),
        P("section", None, None, None),
        P(None, None, images, None, None, None),
    )
    out_specs = (P("section", None, images, None, None, None), P("section", None, images, None))
    return jax.shard_map(
        on_device, mesh=finer, in_specs=in_specs, out_specs=out_specs, check_vma=False
    )
```

profile of v0, /device:TPU:24, one launch (start us, length us, event | category | flops | bytes accessed | tf_op | source)
XLA Modules:
  0.0 188.9 jit_solution(11128915790139596059)
XLA Ops:
  7.2 0.0 reduce-scatter.9.cloned.1.call-start
  7.2 3.9 %tick_0_0.1 = (bf16[4,256,256]{2,1,0:T(8,128)(2,1)S(1)}, bf16[4,256,256]{2,1,0:T(8,128)(2,1)}, f32[8,128]{1,0:T(8,128)S(1)}) custom-call(bf16[4,256,512]{2,1,0:T(8,128)(2,1)} %bitcast.23, bf16[2,1152,512]{2,1,0:T(8,128)(2,1)} %bitcast.9, f32[8,128]{1,0:T(8,128)S(1)} %broadcast_in_dim.11.refs_2_), custom_call_target="tpu_custom_call" | custom-call | flops 603979776 | bytes 1048576 | tf_op jit(solution)/shard_map/tick_0_0/pallas_call | solution.py:326
  11.1 6.2 %collective-permute-start.1 = (bf16[4,256,256]{2,1,0:T(8,128)(2,1)S(1)}, bf16[4,256,256]{2,1,0:T(8,128)(2,1)S(1)}, u32[]{:S(2)}, u32[]{:S(2)}) collective-permute-start(bf16[4,256,256]{2,1,0:T(8,128)(2,1)S(1)} %get-tuple-element.31), channel_id=1, source_target_pairs={{8,0},{16,8},{24,16},{32,24},{40,32},{48,40},{56,48},{64,56},{72,6... | collective-permute-start | bytes 1572872 | tf_op jit(solution)/shard_map/ppermute | solution.py:302
  17.3 3.9 %tick_0_1.1 = (bf16[4,256,256]{2,1,0:T(8,128)(2,1)S(1)}, bf16[4,256,256]{2,1,0:T(8,128)(2,1)}, f32[8,128]{1,0:T(8,128)S(1)}) custom-call(bf16[4,256,512]{2,1,0:T(8,128)(2,1)} %bitcast.24, bf16[2,1152,512]{2,1,0:T(8,128)(2,1)} %bitcast.10, f32[8,128]{1,0:T(8,128)S(1)} %get-tuple-element.29.refs_2_), custom_call_target="tpu_custom_call" | custom-call | flops 603979776 | bytes 1048576 | tf_op jit(solution)/shard_map/tick_0_1/pallas_call | solution.py:326
  21.1 2.6 %collective-permute-start = (bf16[4,256,256]{2,1,0:T(8,128)(2,1)S(1)}, bf16[4,256,256]{2,1,0:T(8,128)(2,1)S(1)}, u32[]{:S(2)}, u32[]{:S(2)}) collective-permute-start(bf16[4,256,256]{2,1,0:T(8,128)(2,1)S(1)} %get-tuple-element.30), channel_id=1, source_target_pairs={{8,0},{16,8},{24,16},{32,24},{40,32},{48,40},{56,48},{64,56},{72,6... | collective-permute-start | bytes 1572872 | tf_op jit(solution)/shard_map/ppermute | solution.py:302
  23.7 0.2 collective-permute-done.1.refs_1_
  23.9 3.6 %tick_1_0.1 = (bf16[4,256,256]{2,1,0:T(8,128)(2,1)S(1)}, bf16[4,256,256]{2,1,0:T(8,128)(2,1)}, f32[8,128]{1,0:T(8,128)S(1)}) custom-call(s32[1]{0:T(128)} %bitcast.refs_0_.is_top, bf16[4,256,256]{2,1,0:T(8,128)(2,1)S(1)} %collective-permute-done.1.refs_1_, bf16[3,4,256,512]{3,2,1,0:T(8,128)(2,1)} %bitcast.17, ...), custom_call_target="tpu_custom_call", output_to_operand_aliasing={{0}: (1, {})} | custom-call | flops 603979776 | bytes 1048576 | tf_op jit(solution)/shard_map/tick_1_0/pallas_call | solution.py:326
  27.5 6.5 %collective-permute-start.3 = (bf16[4,256,256]{2,1,0:T(8,128)(2,1)S(1)}, bf16[4,256,256]{2,1,0:T(8,128)(2,1)S(1)}, u32[]{:S(2)}, u32[]{:S(2)}) collective-permute-start(bf16[4,256,256]{2,1,0:T(8,128)(2,1)S(1)} %get-tuple-element.35), channel_id=1, source_target_pairs={{8,0},{16,8},{24,16},{32,24},{40,32},{48,40},{56,48},{64,56},{72,6... | collective-permute-start | bytes 1572872 | tf_op jit(solution)/shard_map/ppermute | solution.py:302
  34.0 0.0 collective-permute-done.refs_1_
  34.0 3.6 %tick_1_1.1 = (bf16[4,256,256]{2,1,0:T(8,128)(2,1)S(1)}, bf16[4,256,256]{2,1,0:T(8,128)(2,1)}, f32[8,128]{1,0:T(8,128)S(1)}) custom-call(s32[1]{0:T(128)} %bitcast.refs_0_.is_top, bf16[4,256,256]{2,1,0:T(8,128)(2,1)S(1)} %collective-permute-done.refs_1_, bf16[3,4,256,512]{3,2,1,0:T(8,128)(2,1)} %bitcast.18, ...), custom_call_target="tpu_custom_call", output_to_operand_aliasing={{0}: (1, {})} | custom-call | flops 603979776 | bytes 1048576 | tf_op jit(solution)/shard_map/tick_1_1/pallas_call | solution.py:326
  37.6 2.9 %collective-permute-start.2 = (bf16[4,256,256]{2,1,0:T(8,128)(2,1)S(1)}, bf16[4,256,256]{2,1,0:T(8,128)(2,1)S(1)}, u32[]{:S(2)}, u32[]{:S(2)}) collective-permute-start(bf16[4,256,256]{2,1,0:T(8,128)(2,1)S(1)} %get-tuple-element.34), channel_id=1, source_target_pairs={{8,0},{16,8},{24,16},{32,24},{40,32},{48,40},{56,48},{64,56},{72,6... | collective-permute-start | bytes 1572872 | tf_op jit(solution)/shard_map/ppermute | solution.py:302
  40.5 0.2 collective-permute-done.3.refs_1_
  40.7 3.6 %tick_2_0.1 = (bf16[4,256,256]{2,1,0:T(8,128)(2,1)S(1)}, bf16[4,256,256]{2,1,0:T(8,128)(2,1)}, f32[8,128]{1,0:T(8,128)S(1)}) custom-call(s32[1]{0:T(128)} %bitcast.refs_0_.is_top, bf16[4,256,256]{2,1,0:T(8,128)(2,1)S(1)} %collective-permute-done.3.refs_1_, bf16[3,4,256,512]{3,2,1,0:T(8,128)(2,1)} %bitcast.19, ...), custom_call_target="tpu_custom_call", output_to_operand_aliasing={{0}: (1, {})} | custom-call | flops 603979776 | bytes 1048576 | tf_op jit(solution)/shard_map/tick_2_0/pallas_call | solution.py:326
  44.3 6.5 %collective-permute-start.5 = (bf16[4,256,256]{2,1,0:T(8,128)(2,1)S(1)}, bf16[4,256,256]{2,1,0:T(8,128)(2,1)S(1)}, u32[]{:S(2)}, u32[]{:S(2)}) collective-permute-start(bf16[4,256,256]{2,1,0:T(8,128)(2,1)S(1)} %get-tuple-element.48), channel_id=1, source_target_pairs={{8,0},{16,8},{24,16},{32,24},{40,32},{48,40},{56,48},{64,56},{72,6... | collective-permute-start | bytes 1572872 | tf_op jit(solution)/shard_map/ppermute | solution.py:302
  50.8 0.0 collective-permute-done.2.refs_1_
  50.8 3.6 %tick_2_1.1 = (bf16[4,256,256]{2,1,0:T(8,128)(2,1)S(1)}, bf16[4,256,256]{2,1,0:T(8,128)(2,1)}, f32[8,128]{1,0:T(8,128)S(1)}) custom-call(s32[1]{0:T(128)} %bitcast.refs_0_.is_top, bf16[4,256,256]{2,1,0:T(8,128)(2,1)S(1)} %collective-permute-done.2.refs_1_, bf16[3,4,256,512]{3,2,1,0:T(8,128)(2,1)} %bitcast.20, ...), custom_call_target="tpu_custom_call", output_to_operand_aliasing={{0}: (1, {})} | custom-call | flops 603979776 | bytes 1048576 | tf_op jit(solution)/shard_map/tick_2_1/pallas_call | solution.py:326
  54.4 3.0 %collective-permute-start.4 = (bf16[4,256,256]{2,1,0:T(8,128)(2,1)S(1)}, bf16[4,256,256]{2,1,0:T(8,128)(2,1)S(1)}, u32[]{:S(2)}, u32[]{:S(2)}) collective-permute-start(bf16[4,256,256]{2,1,0:T(8,128)(2,1)S(1)} %get-tuple-element.38), channel_id=1, source_target_pairs={{8,0},{16,8},{24,16},{32,24},{40,32},{48,40},{56,48},{64,56},{72,6... | collective-permute-start | bytes 1572872 | tf_op jit(solution)/shard_map/ppermute | solution.py:302
  57.5 3.7 %early_terms_0.1 = (f32[2,1152,256]{2,1,0:T(8,128)}, f32[8,128]{1,0:T(8,128)S(1)}) custom-call(bf16[4,256,256]{2,1,0:T(8,128)(2,1)} %get-tuple-element.42.refs_0_, bf16[4,256,256]{2,1,0:T(8,128)(2,1)} %get-tuple-element.43.refs_1_, bf16[4,256,256]{2,1,0:T(8,128)(2,1)} %get-tuple-element.44.refs_2_, f32[8,128]{1,0:T(8,128)S(1)} %get-tuple-element.45.refs_3_), custom_call_target="tpu_custom_call" | custom-call | flops 905969664 | bytes 1048576 | tf_op jit(solution)/shard_map/early_terms_0/pallas_call | solution.py:348
  61.2 3.7 %early_terms_1.1 = (f32[2,1152,256]{2,1,0:T(8,128)}, f32[8,128]{1,0:T(8,128)S(1)}) custom-call(bf16[4,256,256]{2,1,0:T(8,128)(2,1)} %get-tuple-element.39.refs_0_, bf16[4,256,256]{2,1,0:T(8,128)(2,1)} %get-tuple-element.40.refs_1_, bf16[4,256,256]{2,1,0:T(8,128)(2,1)} %get-tuple-element.41.refs_2_, f32[8,128]{1,0:T(8,128)S(1)} %get-tuple-element.46.refs_3_), custom_call_target="tpu_custom_call" | custom-call | flops 905969664 | bytes 1048576 | tf_op jit(solution)/shard_map/early_terms_1/pallas_call | solution.py:348
  64.9 0.0 collective-permute-done.5.received
  64.9 4.6 %last_tick_0.1 = (bf16[4,256,256]{2,1,0:T(8,128)(2,1)S(1)}, bf16[4,256,512]{2,1,0:T(8,128)(2,1)}, bf16[2,1152,256]{2,1,0:T(8,128)(2,1)}, f32[8,128]{1,0:T(8,128)S(1)}) custom-call(s32[1]{0:T(128)} %bitcast.refs_0_.is_top, bf16[4,256,256]{2,1,0:T(8,128)(2,1)S(1)} %collective-permute-done.5.received, ...), custom_call_target="tpu_custom_call", output_to_operand_aliasing={{0}: (1, {})} | custom-call | flops 905969664 | bytes 1048576 | tf_op jit(solution)/shard_map/last_tick_0/pallas_call | solution.py:375
  69.5 0.0 collective-permute-done.4.received
  69.5 5.2 %last_tick_1.1 = (bf16[4,256,256]{2,1,0:T(8,128)(2,1)S(1)}, bf16[4,256,512]{2,1,0:T(8,128)(2,1)}, bf16[2,1152,256]{2,1,0:T(8,128)(2,1)}, f32[8,128]{1,0:T(8,128)}) custom-call(s32[1]{0:T(128)} %bitcast.refs_0_.is_top, bf16[4,256,256]{2,1,0:T(8,128)(2,1)S(1)} %collective-permute-done.4.received, ...), custom_call_target="tpu_custom_call", output_to_operand_aliasing={{0}: (1, {}), {1}: (6, {})} | custom-call | flops 905969664 | bytes 1048576 | tf_op jit(solution)/shard_map/last_tick_1/pallas_call | solution.py:375
  74.7 0.0 reduce-scatter.9.cloned.1.call-update
  74.8 0.0 reduce-scatter.5.cloned.1.call-start
  74.8 0.7 reduce-scatter.5.cloned.1.call-update
  75.5 0.0 reduce-scatter.11.cloned.1.call-start
  75.6 25.8 %reduce-scatter.9.cloned.1.call-done = bf16[2,288,256]{2,1,0:T(8,128)(2,1)} async-done(((bf16[2,1152,256]{2,1,0:T(8,128)(2,1)}), bf16[2,288,256]{2,1,0:T(8,128)(2,1)}) %reduce-scatter.9.cloned.1.call-update) | async-done | bytes 294928 | tf_op jit(solution)/shard_map/reduce_scatter | solution.py:401
  101.3 0.0 reduce-scatter.11.cloned.1.call-update
  101.3 0.0 reduce-scatter.7.cloned.1.call-start
  101.4 28.9 %reduce-scatter.5.cloned.1.call-done = bf16[2,288,256]{2,1,0:T(8,128)(2,1)} async-done(((bf16[2,1152,256]{2,1,0:T(8,128)(2,1)}), bf16[2,288,256]{2,1,0:T(8,128)(2,1)}) %reduce-scatter.5.cloned.1.call-update) | async-done | bytes 294928 | tf_op jit(solution)/shard_map/reduce_scatter | solution.py:401
  130.3 0.0 reduce-scatter.7.cloned.1.call-update
  130.3 26.8 %reduce-scatter.11.cloned.1.call-done = bf16[2,144,256]{2,1,0:T(8,128)(2,1)} async-done(((bf16[2,288,256]{2,1,0:T(8,128)(2,1)}), bf16[2,144,256]{2,1,0:T(8,128)(2,1)}) %reduce-scatter.11.cloned.1.call-update) | async-done | bytes 147472 | tf_op jit(solution)/shard_map/reduce_scatter | solution.py:401
  157.1 23.4 %reduce-scatter.7.cloned.1.call-done = bf16[2,144,256]{2,1,0:T(8,128)(2,1)} async-done(((bf16[2,288,256]{2,1,0:T(8,128)(2,1)}), bf16[2,144,256]{2,1,0:T(8,128)(2,1)}) %reduce-scatter.7.cloned.1.call-update) | async-done | bytes 147472 | tf_op jit(solution)/shard_map/reduce_scatter | solution.py:401
  180.5 1.9 convert_multiply_fusion
  (1 shorter events, 0.0 us)
Async XLA Ops:
  7.2 94.2 %reduce-scatter.9.cloned.1.call-start = ((), (), s32[]{:S(2)}) async-start(), calls=%async_computation.6 | async-start | bytes 1474560 | tf_op jit(solution)/shard_map/reduce_scatter | solution.py:401
  11.1 12.8 %collective-permute-start.1 = (bf16[4,256,256]{2,1,0:T(8,128)(2,1)S(1)}, bf16[4,256,256]{2,1,0:T(8,128)(2,1)S(1)}, u32[]{:S(2)}, u32[]{:S(2)}) collective-permute-start(bf16[4,256,256]{2,1,0:T(8,128)(2,1)S(1)} %get-tuple-element.31), channel_id=1, source_target_pairs={{8,0},{16,8},{24,16},{32,24},{40,32},{48,40},{56,48},{64,56},{72,6... | collective-permute-start | bytes 1572872 | tf_op jit(solution)/shard_map/ppermute | solution.py:302
  21.1 12.9 %collective-permute-start = (bf16[4,256,256]{2,1,0:T(8,128)(2,1)S(1)}, bf16[4,256,256]{2,1,0:T(8,128)(2,1)S(1)}, u32[]{:S(2)}, u32[]{:S(2)}) collective-permute-start(bf16[4,256,256]{2,1,0:T(8,128)(2,1)S(1)} %get-tuple-element.30), channel_id=1, source_target_pairs={{8,0},{16,8},{24,16},{32,24},{40,32},{48,40},{56,48},{64,56},{72,6... | collective-permute-start | bytes 1572872 | tf_op jit(solution)/shard_map/ppermute | solution.py:302
  27.5 13.2 %collective-permute-start.3 = (bf16[4,256,256]{2,1,0:T(8,128)(2,1)S(1)}, bf16[4,256,256]{2,1,0:T(8,128)(2,1)S(1)}, u32[]{:S(2)}, u32[]{:S(2)}) collective-permute-start(bf16[4,256,256]{2,1,0:T(8,128)(2,1)S(1)} %get-tuple-element.35), channel_id=1, source_target_pairs={{8,0},{16,8},{24,16},{32,24},{40,32},{48,40},{56,48},{64,56},{72,6... | collective-permute-start | bytes 1572872 | tf_op jit(solution)/shard_map/ppermute | solution.py:302
  37.6 13.2 %collective-permute-start.2 = (bf16[4,256,256]{2,1,0:T(8,128)(2,1)S(1)}, bf16[4,256,256]{2,1,0:T(8,128)(2,1)S(1)}, u32[]{:S(2)}, u32[]{:S(2)}) collective-permute-start(bf16[4,256,256]{2,1,0:T(8,128)(2,1)S(1)} %get-tuple-element.34), channel_id=1, source_target_pairs={{8,0},{16,8},{24,16},{32,24},{40,32},{48,40},{56,48},{64,56},{72,6... | collective-permute-start | bytes 1572872 | tf_op jit(solution)/shard_map/ppermute | solution.py:302
  44.3 20.6 %collective-permute-start.5 = (bf16[4,256,256]{2,1,0:T(8,128)(2,1)S(1)}, bf16[4,256,256]{2,1,0:T(8,128)(2,1)S(1)}, u32[]{:S(2)}, u32[]{:S(2)}) collective-permute-start(bf16[4,256,256]{2,1,0:T(8,128)(2,1)S(1)} %get-tuple-element.48), channel_id=1, source_target_pairs={{8,0},{16,8},{24,16},{32,24},{40,32},{48,40},{56,48},{64,56},{72,6... | collective-permute-start | bytes 1572872 | tf_op jit(solution)/shard_map/ppermute | solution.py:302
  54.4 15.1 %collective-permute-start.4 = (bf16[4,256,256]{2,1,0:T(8,128)(2,1)S(1)}, bf16[4,256,256]{2,1,0:T(8,128)(2,1)S(1)}, u32[]{:S(2)}, u32[]{:S(2)}) collective-permute-start(bf16[4,256,256]{2,1,0:T(8,128)(2,1)S(1)} %get-tuple-element.38), channel_id=1, source_target_pairs={{8,0},{16,8},{24,16},{32,24},{40,32},{48,40},{56,48},{64,56},{72,6... | collective-permute-start | bytes 1572872 | tf_op jit(solution)/shard_map/ppermute | solution.py:302
  74.8 55.5 %reduce-scatter.5.cloned.1.call-start = ((), (), s32[]{:S(2)}) async-start(), calls=%async_computation.4 | async-start | bytes 1474560 | tf_op jit(solution)/shard_map/reduce_scatter | solution.py:401
  75.5 81.6 %reduce-scatter.11.cloned.1.call-start = ((), (), s32[]{:S(2)}) async-start(), calls=%async_computation.7 | async-start | bytes 442368 | tf_op jit(solution)/shard_map/reduce_scatter | solution.py:401
  101.3 79.1 %reduce-scatter.7.cloned.1.call-start = ((), (), s32[]{:S(2)}) async-start(), calls=%async_computation.5 | async-start | bytes 442368 | tf_op jit(solution)/shard_map/reduce_scatter | solution.py:401
Sparse Core Ops, SparseCore 0:
  74.9 26.3 reduce-scatter.8
  103.9 26.3 reduce-scatter.4
  132.8 24.2 reduce-scatter.10
  159.4 20.9 reduce-scatter.6
where the time goes:
time: 190 us; the launch traced here: 189 us
  waiting for transfers between devices  106 us (56%)
  Pallas kernels  39.3 us (21%)
  starting transfers between devices  27.8 us (15%)
  between operations  13.9 us (7%)
    reduce_scatter x4, waiting for transfers between devices, on_device(): share = lax.psum_scatter(share, axis, scatter_dimension=1, tiled=True)  105 us
    ppermute x6, starting transfers between devices, passed_down(): lax.ppermute(value, 'section', [(source, source - 1) for source in range(...  27.7 us
    pallas_call x6, Pallas kernels, on_device(): pl.pallas_call(functools.partial(early_tick, tick, half, width), out_shap...  22 us
    pallas_call x2, Pallas kernels, on_device(): pl.pallas_call(functools.partial(last_tick, half, width), out_shape=(stat...  9.82 us
    pallas_call x2, Pallas kernels, on_device(): pl.pallas_call(functools.partial(early_terms, width), out_shape=(pltpu.HB...  7.39 us
  transfers between devices with their start and end apart: 10, of which 6 were waited for; matrix products, arithmetic and copies ran while one was open for 0% of the time, Pallas kernels for 16%

commit v1 on v0

--- a/solution.py
+++ b/solution.py
@@ -13,6 +13,7 @@
 TICKS = 4
 CELLS = HW * HW
 ROWS = 9 * GW
+SHARE = ROWS // 8
 HALVES = 2
 VMEM_LIMIT = 24 * 1024 * 1024
 
@@ -125,8 +126,8 @@
     return loaded
 
 
-def take_top(is_top, tick, half, width, top, made, sem):
-    @pl.when(is_top[0] == 1)
+def take_top(places, tick, half, width, top, made, sem):
+    @pl.when(places[0] == 1)
     def _():
         copy = pltpu.make_async_copy(
             top.at[tick - 1, :, :, pl.ds(half * width, width)], made, sem
@@ -137,7 +138,7 @@
 
 def early_tick(tick, half, width, *refs):
     if tick:
-        is_top, received, top, kernels, earlier, made, kept, turn, held, sent, sems, sem, out_sems = refs
+        places, received, top, kernels, earlier, made, kept, turn, held, sent, sems, sem, out_sems = refs
     else:
         states, kernels, earlier, made, kept, turn, held, sent, sems, sem, out_sems = refs
     if not tick:
@@ -152,7 +153,7 @@
     loaded = kernel_loads(half, width, kernels, held, sems)
     turn[...] = jnp.zeros_like(turn)
     if tick:
-        take_top(is_top, tick, half, width, top, made, sem.at[0])
+        take_top(places, tick, half, width, top, made, sem.at[0])
     outgoing = []
     for group in range(width // GW):
         lanes = group_lanes(group)
@@ -226,13 +227,15 @@
         copy.wait()
 
 
-def last_tick(half, width, is_top, received, top, kernels, total, earlier, *rest):
-    made, final, share, turn, held, summed, sent, sems, sem, total_sem, final_sem, share_sems = rest[-12:]
+def last_tick(half, width, places, received, top, kernels, total, earlier, *rest):
+    made, final, mine, theirs, turn, held, summed, sent, sems, sem, total_sem, final_sem, share_sems = (
+        rest[-13:]
+    )
     loaded = kernel_loads(half, width, kernels, held, sems)
     total_copy = pltpu.make_async_copy(total, summed, total_sem)
     total_copy.start()
     turn[...] = jnp.zeros_like(turn)
-    take_top(is_top, TICKS - 1, half, width, top, made, sem)
+    take_top(places, TICKS - 1, half, width, top, made, sem)
     outgoing = []
     for group in range(width // GW):
         lanes = group_lanes(group)
@@ -250,11 +253,16 @@
                     sent[branch, rows, lanes] = (
                         summed[branch, rows, lanes] + term[:, a * GW : (a + 1) * GW]
                     ).astype(jnp.bfloat16)
-                copy = pltpu.make_async_copy(
-                    sent.at[branch, :, lanes], share.at[branch, :, lanes], share_sems.at[branch, group]
-                )
-                copy.start()
-                outgoing.append(copy)
+                for slot in range(4):
+                    for z_slot in range(2):
+                        block = pl.multiple_of(places[1 + slot] + places[5 + z_slot], 16)
+                        copy = pltpu.make_async_copy(
+                            sent.at[branch, pl.ds(block, SHARE), lanes],
+                            (mine, theirs)[slot // 2].at[slot % 2, z_slot, branch, :, lanes],
+                            share_sems.at[branch, group, slot, z_slot],
+                        )
+                        copy.start()
+                        outgoing.append(copy)
 
         section_back(
             made,
@@ -302,13 +310,96 @@
     return lax.ppermute(value, "section", [(source, source - 1) for source in range(1, count)])
 
 
+def partners(half, x):
+    return (x ^ 1, 3 - x) if half == 0 else (3 - x, x ^ 1)
+
+
+def share_places(half):
+    x, z = lax.axis_index("dp_0"), lax.axis_index("dp_1")
+    first, second = partners(half, x)
+    is_top = lax.axis_index("section") == lax.axis_size("section") - 1
+    blocks = [x, second, first, partners(half, first)[1]]
+    rows = [block * (2 * SHARE) for block in blocks] + [z * SHARE, (1 - z) * SHARE]
+    return jnp.stack([is_top.astype(jnp.int32)] + [row.astype(jnp.int32) for row in rows])
+
+
+def first_sum(mine, came, earlier, passed, turn):
+    turn[...] = jnp.zeros_like(turn)
+    passed[...] = (mine[1].astype(jnp.float32) + came[1].astype(jnp.float32)).astype(jnp.bfloat16)
+
+
+def second_sum(mine, came, came_next, earlier, across, kept, turn):
+    turn[...] = jnp.zeros_like(turn)
+    total = [
+        mine[0, z_slot].astype(jnp.float32)
+        + came[0, z_slot].astype(jnp.float32)
+        + came_next[z_slot].astype(jnp.float32)
+        for z_slot in range(2)
+    ]
+    kept[...] = total[0]
+    across[...] = total[1].astype(jnp.bfloat16)
+
+
+def last_sum(*refs):
+    kept, came, out = refs[:HALVES], refs[HALVES:-1], refs[-1]
+    for half in range(HALVES):
+        width = kept[half].shape[-1]
+        out[:, :, pl.ds(half * width, width)] = (
+            kept[half][...] + came[half][...].astype(jnp.float32)
+        ) * (1.0 / (HW * HW))
+
+
+def summed_shares(mine, theirs, turn):
+    width = mine[0].shape[-1]
+    turn_type = pltpu.VMEM((8, 128), jnp.float32)
+    halves = range(HALVES)
+    pairs = [
+        [[(x, partners(half, x)[step]) for x in range(4)] for step in range(2)] for half in halves
+    ]
+    came = [lax.ppermute(theirs[half], "dp_0", pairs[half][0]) for half in halves]
+    came_next, came_last, kept = [], [], []
+    for half in halves:
+        passed, turn = pl.pallas_call(
+            first_sum,
+            out_shape=(pltpu.VMEM((2, 2, SHARE, width), jnp.bfloat16), turn_type),
+            in_specs=[VMEM_REF, VMEM_REF, ANY_REF],
+            out_specs=(VMEM_REF, VMEM_REF),
+            compiler_params=params(),
+            name=f"first_sum_{half}",
+        )(mine[half], in_vmem(came[half]), turn)
+        came_next.append(lax.ppermute(passed, "dp_0", pairs[half][1]))
+    for half in halves:
+        across, own, turn = pl.pallas_call(
+            second_sum,
+            out_shape=(
+                pltpu.VMEM((2, SHARE, width), jnp.bfloat16),
+                pltpu.VMEM((2, SHARE, width), jnp.float32),
+                turn_type,
+            ),
+            in_specs=[VMEM_REF, VMEM_REF, VMEM_REF, ANY_REF],
+            out_specs=(VMEM_REF, VMEM_REF, VMEM_REF),
+            compiler_params=params(),
+            name=f"second_sum_{half}",
+        )(mine[half], in_vmem(came[half]), in_vmem(came_next[half]), turn)
+        came_last.append(lax.ppermute(across, "dp_1", [(0, 1), (1, 0)]))
+        kept.append(own)
+    return pl.pallas_call(
+        last_sum,
+        out_shape=jax.ShapeDtypeStruct((2, SHARE, width * HALVES), jnp.float32),
+        in_specs=[VMEM_REF] * (2 * HALVES),
+        out_specs=VMEM_REF,
+        compiler_params=params(),
+        name="last_sum",
+    )(*[in_vmem(own) for own in kept], *[in_vmem(part) for part in came_last])
+
+
 def on_device(section_states, conv_kernels, top_feed):
     chans = section_states.shape[-1]
     width = chans // HALVES
     states = in_hbm(section_states.reshape(4, CELLS, chans))
     kernels = in_hbm(conv_kernels[0])
     top = in_hbm(top_feed.reshape(TICKS - 1, 4, CELLS, chans))
-    is_top = (lax.axis_index("section") == lax.axis_size("section") - 1).astype(jnp.int32)[None]
+    places = [share_places(half) for half in range(HALVES)]
 
     groups = width // GW
     state_type = pltpu.VMEM((4, CELLS, width), jnp.bfloat16)
@@ -321,7 +412,7 @@
         for half in range(HALVES):
             operands, specs = [states, kernels, turn], [ANY_REF] * 3
             if tick:
-                operands = [is_top, in_vmem(made[half]), top, kernels, turn]
+                operands = [places[half], in_vmem(made[half]), top, kernels, turn]
                 specs = [SMEM_REF, VMEM_REF, ANY_REF, ANY_REF, ANY_REF]
             out, fields, turn = pl.pallas_call(
                 functools.partial(early_tick, tick, half, width),
@@ -363,25 +454,27 @@
         total.append(in_hbm(summed))
 
     final = None
-    shares = []
+    mine, theirs = [None] * HALVES, [None] * HALVES
+    share_type = pltpu.HBM((2, 2, 2, SHARE, width), jnp.bfloat16)
     for half in range(HALVES):
-        operands = [is_top, in_vmem(made[half]), top, kernels, total[half], turn]
+        operands = [places[half], in_vmem(made[half]), top, kernels, total[half], turn]
         specs = [SMEM_REF, VMEM_REF, ANY_REF, ANY_REF, ANY_REF, ANY_REF]
         aliases = {1: 0}
         if half:
             operands.append(in_hbm(final))
             specs.append(ANY_REF)
             aliases[6] = 1
-        _, final, share, turn = pl.pallas_call(
+        _, final, mine[half], theirs[half], turn = pl.pallas_call(
             functools.partial(last_tick, half, width),
             out_shape=(
                 state_type,
                 pltpu.HBM((4, CELLS, chans), jnp.bfloat16),
-                pltpu.HBM((2, ROWS, width), jnp.bfloat16),
+                share_type,
+                share_type,
                 turn_type,
             ),
             in_specs=specs,
-            out_specs=(VMEM_REF, ANY_REF, ANY_REF, VMEM_REF),
+            out_specs=(VMEM_REF, ANY_REF, ANY_REF, ANY_REF, VMEM_REF),
             scratch_shapes=[
                 held_scratch,
                 pltpu.VMEM((2, ROWS, width), jnp.float32),
@@ -390,17 +483,14 @@
                 pltpu.SemaphoreType.DMA(()),
                 pltpu.SemaphoreType.DMA(()),
                 pltpu.SemaphoreType.DMA(()),
-                pltpu.SemaphoreType.DMA((2, groups)),
+                pltpu.SemaphoreType.DMA((2, groups, 4, 2)),
             ],
             input_output_aliases=aliases,
             compiler_params=params(),
             cost_estimate=cost(6, width),
             name=f"last_tick_{half}",
         )(*operands)
-        for axis in ("dp_0", "dp_1"):
-            share = lax.psum_scatter(share, axis, scatter_dimension=1, tiled=True)
-        shares.append(share)
-    grads = jnp.concatenate(shares, axis=2).astype(jnp.float32) * (1.0 / (HW * HW))
+    grads = summed_shares(mine, theirs, turn)
     return (final.reshape(1, 4, 1, HW, HW, chans), grads[None])
 
 

time: 190 us -> 111 us (0.58)
  waiting for transfers between devices: 106 us -> 23.4 us
  between operations: 13.9 us -> 0.83 us
  starting transfers between devices: 27.8 us -> 40.6 us
  Pallas kernels: 39.3 us -> 44.1 us
    reduce_scatter x4 -> x0, waiting for transfers between devices: 105 us -> none  [on_device(): share = lax.psum_scatter(share, axis, scatter_dimension=1, tiled=True)]
    ppermute x0 -> x6, waiting for transfers between devices: none -> 23.2 us  [the longest x2 12.6 us: summed_shares(): lax.ppermute(theirs[half], 'dp_0', pairs[half][0])]
    ppermute x0 -> x6, starting transfers between devices: none -> 14 us  [the longest x2 7.27 us: summed_shares(): came_last.append(lax.ppermute(across, 'dp_1', [(0, 1), (1, 0)]))]
    pallas_call x6, Pallas kernels: 22 us -> 24.2 us  [on_device(): pl.pallas_call(functools.partial(early_tick, tick, half, width), out_shap...]
  transfers between devices with their start and end apart: 10 -> 12, of which waited for: 6 -> 7; matrix products, arithmetic and copies ran while one was open for 0% -> 0% of each run, Pallas kernels for 16% -> 36%
where the time goes in v1:
time: 111 us; the launch traced here: 110 us
  Pallas kernels  44.1 us (40%)
  starting transfers between devices  40.6 us (37%)
  waiting for transfers between devices  23.4 us (21%)
  local copies, waits for them, and re-layouts  1.25 us (1%)
    ppermute x6, starting transfers between devices, passed_down(): lax.ppermute(value, 'section', [(source, source - 1) for source in range(...  26.6 us
    pallas_call x6, Pallas kernels, on_device(): pl.pallas_call(functools.partial(early_tick, tick, half, width), out_shap...  24.2 us
    ppermute x2, waiting for transfers between devices, summed_shares(): lax.ppermute(theirs[half], 'dp_0', pairs[half][0])  12.6 us
    pallas_call x2, Pallas kernels, on_device(): pl.pallas_call(functools.partial(last_tick, half, width), out_shape=(stat...  10.8 us
    pallas_call x2, Pallas kernels, on_device(): pl.pallas_call(functools.partial(early_terms, width), out_shape=(pltpu.HB...  7.41 us
    ppermute x2, starting transfers between devices, summed_shares(): came_last.append(lax.ppermute(across, 'dp_1', [(0, 1), (1, 0)]))  7.27 us
    ppermute x2, waiting for transfers between devices, summed_shares(): came_last.append(lax.ppermute(across, 'dp_1', [(0, 1), (1, 0)]))  6.7 us
    ppermute x2, waiting for transfers between devices, summed_shares(): came_next.append(lax.ppermute(passed, 'dp_0', pairs[half][1]))  3.82 us
  transfers between devices with their start and end apart: 12, of which 7 were waited for; matrix products, arithmetic and copies ran while one was open for 0% of the time, Pallas kernels for 36%

profile of v1, /device:TPU:24, one launch (start us, length us, event | category | flops | bytes accessed | tf_op | source)
XLA Modules:
  0.0 110.2 jit_solution(14313248941247723347)
XLA Ops:
  0.6 3.9 %tick_0_0.1 = (bf16[4,256,256]{2,1,0:T(8,128)(2,1)S(1)}, bf16[4,256,256]{2,1,0:T(8,128)(2,1)}, f32[8,128]{1,0:T(8,128)S(1)}) custom-call(bf16[4,256,512]{2,1,0:T(8,128)(2,1)} %bitcast.29, bf16[2,1152,512]{2,1,0:T(8,128)(2,1)} %bitcast.15, f32[8,128]{1,0:T(8,128)S(1)} %broadcast_in_dim.6.refs_2_), custom_call_target="tpu_custom_call" | custom-call | flops 603979776 | bytes 1048576 | tf_op jit(solution)/shard_map/tick_0_0/pallas_call | solution.py:417
  4.5 6.1 %collective-permute-start.1 = (bf16[4,256,256]{2,1,0:T(8,128)(2,1)S(1)}, bf16[4,256,256]{2,1,0:T(8,128)(2,1)S(1)}, u32[]{:S(2)}, u32[]{:S(2)}) collective-permute-start(bf16[4,256,256]{2,1,0:T(8,128)(2,1)S(1)} %get-tuple-element.43), channel_id=1, source_target_pairs={{8,0},{16,8},{24,16},{32,24},{40,32},{48,40},{56,48},{64,56},{72,6... | collective-permute-start | bytes 1572872 | tf_op jit(solution)/shard_map/ppermute | solution.py:310
  10.7 3.9 %tick_0_1.1 = (bf16[4,256,256]{2,1,0:T(8,128)(2,1)S(1)}, bf16[4,256,256]{2,1,0:T(8,128)(2,1)}, f32[8,128]{1,0:T(8,128)S(1)}) custom-call(bf16[4,256,512]{2,1,0:T(8,128)(2,1)} %bitcast.30, bf16[2,1152,512]{2,1,0:T(8,128)(2,1)} %bitcast.16, f32[8,128]{1,0:T(8,128)S(1)} %get-tuple-element.41.refs_2_), custom_call_target="tpu_custom_call" | custom-call | flops 603979776 | bytes 1048576 | tf_op jit(solution)/shard_map/tick_0_1/pallas_call | solution.py:417
  14.5 2.6 %collective-permute-start = (bf16[4,256,256]{2,1,0:T(8,128)(2,1)S(1)}, bf16[4,256,256]{2,1,0:T(8,128)(2,1)S(1)}, u32[]{:S(2)}, u32[]{:S(2)}) collective-permute-start(bf16[4,256,256]{2,1,0:T(8,128)(2,1)S(1)} %get-tuple-element.42), channel_id=1, source_target_pairs={{8,0},{16,8},{24,16},{32,24},{40,32},{48,40},{56,48},{64,56},{72,6... | collective-permute-start | bytes 1572872 | tf_op jit(solution)/shard_map/ppermute | solution.py:310
  17.2 0.1 stack.49.refs_0_.places
  17.3 0.1 collective-permute-done.1.refs_1_
  17.4 4.1 %tick_1_0.1 = (bf16[4,256,256]{2,1,0:T(8,128)(2,1)S(1)}, bf16[4,256,256]{2,1,0:T(8,128)(2,1)}, f32[8,128]{1,0:T(8,128)S(1)}) custom-call(s32[7]{0:T(128)S(1)} %stack.49.refs_0_.places, bf16[4,256,256]{2,1,0:T(8,128)(2,1)S(1)} %collective-permute-done.1.refs_1_, bf16[3,4,256,512]{3,2,1,0:T(8,128)(2,1)} %bitcast.23, ...), custom_call_target="tpu_custom_call", output_to_operand_aliasing={{0}: (1, {})} | custom-call | flops 603979776 | bytes 1048576 | tf_op jit(solution)/shard_map/tick_1_0/pallas_call | solution.py:417
  21.5 6.5 %collective-permute-start.3 = (bf16[4,256,256]{2,1,0:T(8,128)(2,1)S(1)}, bf16[4,256,256]{2,1,0:T(8,128)(2,1)S(1)}, u32[]{:S(2)}, u32[]{:S(2)}) collective-permute-start(bf16[4,256,256]{2,1,0:T(8,128)(2,1)S(1)} %get-tuple-element.47), channel_id=1, source_target_pairs={{8,0},{16,8},{24,16},{32,24},{40,32},{48,40},{56,48},{64,56},{72,6... | collective-permute-start | bytes 1572872 | tf_op jit(solution)/shard_map/ppermute | solution.py:310
  28.0 0.1 stack.47.refs_0_.places
  28.1 0.0 collective-permute-done.refs_1_
  28.1 4.2 %tick_1_1.1 = (bf16[4,256,256]{2,1,0:T(8,128)(2,1)S(1)}, bf16[4,256,256]{2,1,0:T(8,128)(2,1)}, f32[8,128]{1,0:T(8,128)S(1)}) custom-call(s32[7]{0:T(128)S(1)} %stack.47.refs_0_.places, bf16[4,256,256]{2,1,0:T(8,128)(2,1)S(1)} %collective-permute-done.refs_1_, bf16[3,4,256,512]{3,2,1,0:T(8,128)(2,1)} %bitcast.24, ...), custom_call_target="tpu_custom_call", output_to_operand_aliasing={{0}: (1, {})} | custom-call | flops 603979776 | bytes 1048576 | tf_op jit(solution)/shard_map/tick_1_1/pallas_call | solution.py:417
  32.2 2.2 %collective-permute-start.2 = (bf16[4,256,256]{2,1,0:T(8,128)(2,1)S(1)}, bf16[4,256,256]{2,1,0:T(8,128)(2,1)S(1)}, u32[]{:S(2)}, u32[]{:S(2)}) collective-permute-start(bf16[4,256,256]{2,1,0:T(8,128)(2,1)S(1)} %get-tuple-element.46), channel_id=1, source_target_pairs={{8,0},{16,8},{24,16},{32,24},{40,32},{48,40},{56,48},{64,56},{72,6... | collective-permute-start | bytes 1572872 | tf_op jit(solution)/shard_map/ppermute | solution.py:310
  34.5 0.2 collective-permute-done.3.refs_1_
  34.7 4.1 %tick_2_0.1 = (bf16[4,256,256]{2,1,0:T(8,128)(2,1)S(1)}, bf16[4,256,256]{2,1,0:T(8,128)(2,1)}, f32[8,128]{1,0:T(8,128)S(1)}) custom-call(s32[7]{0:T(128)S(1)} %stack.49.refs_0_.places, bf16[4,256,256]{2,1,0:T(8,128)(2,1)S(1)} %collective-permute-done.3.refs_1_, bf16[3,4,256,512]{3,2,1,0:T(8,128)(2,1)} %bitcast.25, ...), custom_call_target="tpu_custom_call", output_to_operand_aliasing={{0}: (1, {})} | custom-call | flops 603979776 | bytes 1048576 | tf_op jit(solution)/shard_map/tick_2_0/pallas_call | solution.py:417
  38.8 6.5 %collective-permute-start.5 = (bf16[4,256,256]{2,1,0:T(8,128)(2,1)S(1)}, bf16[4,256,256]{2,1,0:T(8,128)(2,1)S(1)}, u32[]{:S(2)}, u32[]{:S(2)}) collective-permute-start(bf16[4,256,256]{2,1,0:T(8,128)(2,1)S(1)} %get-tuple-element.60), channel_id=1, source_target_pairs={{8,0},{16,8},{24,16},{32,24},{40,32},{48,40},{56,48},{64,56},{72,6... | collective-permute-start | bytes 1572872 | tf_op jit(solution)/shard_map/ppermute | solution.py:310
  45.3 0.0 collective-permute-done.2.refs_1_
  45.3 4.1 %tick_2_1.1 = (bf16[4,256,256]{2,1,0:T(8,128)(2,1)S(1)}, bf16[4,256,256]{2,1,0:T(8,128)(2,1)}, f32[8,128]{1,0:T(8,128)S(1)}) custom-call(s32[7]{0:T(128)S(1)} %stack.47.refs_0_.places, bf16[4,256,256]{2,1,0:T(8,128)(2,1)S(1)} %collective-permute-done.2.refs_1_, bf16[3,4,256,512]{3,2,1,0:T(8,128)(2,1)} %bitcast.26, ...), custom_call_target="tpu_custom_call", output_to_operand_aliasing={{0}: (1, {})} | custom-call | flops 603979776 | bytes 1048576 | tf_op jit(solution)/shard_map/tick_2_1/pallas_call | solution.py:417
  49.4 2.6 %collective-permute-start.4 = (bf16[4,256,256]{2,1,0:T(8,128)(2,1)S(1)}, bf16[4,256,256]{2,1,0:T(8,128)(2,1)S(1)}, u32[]{:S(2)}, u32[]{:S(2)}) collective-permute-start(bf16[4,256,256]{2,1,0:T(8,128)(2,1)S(1)} %get-tuple-element.50), channel_id=1, source_target_pairs={{8,0},{16,8},{24,16},{32,24},{40,32},{48,40},{56,48},{64,56},{72,6... | collective-permute-start | bytes 1572872 | tf_op jit(solution)/shard_map/ppermute | solution.py:310
  52.0 3.7 %early_terms_0.1 = (f32[2,1152,256]{2,1,0:T(8,128)}, f32[8,128]{1,0:T(8,128)S(1)}) custom-call(bf16[4,256,256]{2,1,0:T(8,128)(2,1)} %get-tuple-element.54.refs_0_, bf16[4,256,256]{2,1,0:T(8,128)(2,1)} %get-tuple-element.55.refs_1_, bf16[4,256,256]{2,1,0:T(8,128)(2,1)} %get-tuple-element.56.refs_2_, f32[8,128]{1,0:T(8,128)S(1)} %get-tuple-element.57.refs_3_), custom_call_target="tpu_custom_call" | custom-call | flops 905969664 | bytes 1048576 | tf_op jit(solution)/shard_map/early_terms_0/pallas_call | solution.py:439
  55.7 3.7 %early_terms_1.1 = (f32[2,1152,256]{2,1,0:T(8,128)}, f32[8,128]{1,0:T(8,128)S(1)}) custom-call(bf16[4,256,256]{2,1,0:T(8,128)(2,1)} %get-tuple-element.51.refs_0_, bf16[4,256,256]{2,1,0:T(8,128)(2,1)} %get-tuple-element.52.refs_1_, bf16[4,256,256]{2,1,0:T(8,128)(2,1)} %get-tuple-element.53.refs_2_, f32[8,128]{1,0:T(8,128)S(1)} %get-tuple-element.58.refs_3_), custom_call_target="tpu_custom_call" | custom-call | flops 905969664 | bytes 1048576 | tf_op jit(solution)/shard_map/early_terms_1/pallas_call | solution.py:439
  59.4 0.0 collective-permute-done.5.received
  59.4 5.4 %last_tick_0.1 = (bf16[4,256,256]{2,1,0:T(8,128)(2,1)S(1)}, bf16[4,256,512]{2,1,0:T(8,128)(2,1)}, bf16[2,2,2,144,256]{4,3,2,1,0:T(8,128)(2,1)}, bf16[2,2,2,144,256]{4,3,2,1,0:T(8,128)(2,1)}, f32[8,128]{1,0:T(8,128)S(1)}) custom-call(s32[7]{0:T(128)S(1)} %stack.49.refs_0_.places, ...), custom_call_target="tpu_custom_call", output_to_operand_aliasing={{0}: (1, {})} | custom-call | flops 905969664 | bytes 1048576 | tf_op jit(solution)/shard_map/last_tick_0/pallas_call | solution.py:467
  64.8 1.6 %collective-permute-start.6 = (bf16[2,2,2,144,256]{4,3,2,1,0:T(8,128)(2,1)}, bf16[2,2,2,144,256]{4,3,2,1,0:T(8,128)(2,1)S(1)}, u32[]{:S(2)}, u32[]{:S(2)}) collective-permute-start(bf16[2,2,2,144,256]{4,3,2,1,0:T(8,128)(2,1)} %get-tuple-element.67), channel_id=1, source_target_pairs={{0,2},{2,0},{4,6},{6,4},{1,3},{3,1},{5,7},{7,5},{8,10},{10,8},{12,... | collective-permute-start | bytes 1769480 | tf_op jit(solution)/shard_map/ppermute | solution.py:359
  66.4 0.0 collective-permute-done.4.received
  66.4 0.0 copy-start
  66.4 5.4 %last_tick_1.1 = (bf16[4,256,256]{2,1,0:T(8,128)(2,1)S(1)}, bf16[4,256,512]{2,1,0:T(8,128)(2,1)}, bf16[2,2,2,144,256]{4,3,2,1,0:T(8,128)(2,1)}, bf16[2,2,2,144,256]{4,3,2,1,0:T(8,128)(2,1)}, f32[8,128]{1,0:T(8,128)S(1)}) custom-call(s32[7]{0:T(128)S(1)} %stack.47.refs_0_.places, ...), custom_call_target="tpu_custom_call", output_to_operand_aliasing={{0}: (1, {}), {1}: (6, {})} | custom-call | flops 905969664 | bytes 1048576 | tf_op jit(solution)/shard_map/last_tick_1/pallas_call | solution.py:467
  71.8 2.2 %collective-permute-start.8 = (bf16[2,2,2,144,256]{4,3,2,1,0:T(8,128)(2,1)}, bf16[2,2,2,144,256]{4,3,2,1,0:T(8,128)(2,1)S(1)}, u32[]{:S(2)}, u32[]{:S(2)}) collective-permute-start(bf16[2,2,2,144,256]{4,3,2,1,0:T(8,128)(2,1)} %get-tuple-element.71), channel_id=1, source_target_pairs={{0,6},{2,4},{4,2},{6,0},{1,7},{3,5},{5,3},{7,1},{8,14},{10,12},{12... | collective-permute-start | bytes 1769480 | tf_op jit(solution)/shard_map/ppermute | solution.py:359
  74.0 6.4 %collective-permute-done.6.came = bf16[2,2,2,144,256]{4,3,2,1,0:T(8,128)(2,1)S(1)} collective-permute-done((bf16[2,2,2,144,256]{4,3,2,1,0:T(8,128)(2,1)}, bf16[2,2,2,144,256]{4,3,2,1,0:T(8,128)(2,1)S(1)}, u32[]{:S(2)}, u32[]{:S(2)}) %collective-permute-start.6) | collective-permute-done | bytes 589856 | tf_op jit(solution)/shard_map/ppermute | solution.py:359
  80.4 0.0 copy-done
  80.4 0.1 first_sum_0.1
  80.5 2.8 %collective-permute-start.7 = (bf16[2,2,144,256]{3,2,1,0:T(8,128)(2,1)S(1)}, bf16[2,2,144,256]{3,2,1,0:T(8,128)(2,1)S(1)}, u32[]{:S(2)}, u32[]{:S(2)}) collective-permute-start(bf16[2,2,144,256]{3,2,1,0:T(8,128)(2,1)S(1)} %get-tuple-element.69), channel_id=1, source_target_pairs={{0,6},{2,4},{4,2},{6,0},{1,7},{3,5},{5,3},{7,1},{8,14},{10,12},{12... | collective-permute-start | bytes 884744 | tf_op jit(solution)/shard_map/ppermute | solution.py:370
  83.3 6.3 %collective-permute-done.8.came = bf16[2,2,2,144,256]{4,3,2,1,0:T(8,128)(2,1)S(1)} collective-permute-done((bf16[2,2,2,144,256]{4,3,2,1,0:T(8,128)(2,1)}, bf16[2,2,2,144,256]{4,3,2,1,0:T(8,128)(2,1)S(1)}, u32[]{:S(2)}, u32[]{:S(2)}) %collective-permute-start.8) | collective-permute-done | bytes 589856 | tf_op jit(solution)/shard_map/ppermute | solution.py:359
  89.6 0.0 copy-start.1
  89.6 1.1 copy-done.1
  90.6 0.1 first_sum_1.1
  90.7 0.1 collective-permute-start.9
  90.8 3.8 %collective-permute-done.7.came_next = bf16[2,2,144,256]{3,2,1,0:T(8,128)(2,1)S(1)} collective-permute-done((bf16[2,2,144,256]{3,2,1,0:T(8,128)(2,1)S(1)}, bf16[2,2,144,256]{3,2,1,0:T(8,128)(2,1)S(1)}, u32[]{:S(2)}, u32[]{:S(2)}) %collective-permute-start.7) | collective-permute-done | bytes 294944 | tf_op jit(solution)/shard_map/ppermute | solution.py:370
  94.6 0.1 second_sum_0.1
  94.7 4.6 %collective-permute-start.10 = (bf16[2,144,256]{2,1,0:T(8,128)(2,1)S(1)}, bf16[2,144,256]{2,1,0:T(8,128)(2,1)S(1)}, u32[]{:S(2)}, u32[]{:S(2)}) collective-permute-start(bf16[2,144,256]{2,1,0:T(8,128)(2,1)S(1)} %get-tuple-element.78), channel_id=1, source_target_pairs={{0,1},{1,0},{2,3},{3,2},{4,5},{5,4},{6,7},{7,6},{8,9},{9,8},{10,11... | collective-permute-start | bytes 442376 | tf_op jit(solution)/shard_map/ppermute | solution.py:384
  99.3 0.0 collective-permute-done.9.came_next
  99.3 0.6 second_sum_1.1
  99.9 2.7 %collective-permute-start.11 = (bf16[2,144,256]{2,1,0:T(8,128)(2,1)S(1)}, bf16[2,144,256]{2,1,0:T(8,128)(2,1)S(1)}, u32[]{:S(2)}, u32[]{:S(2)}) collective-permute-start(bf16[2,144,256]{2,1,0:T(8,128)(2,1)S(1)} %get-tuple-element.79), channel_id=1, source_target_pairs={{0,1},{1,0},{2,3},{3,2},{4,5},{5,4},{6,7},{7,6},{8,9},{9,8},{10,11... | collective-permute-start | bytes 442376 | tf_op jit(solution)/shard_map/ppermute | solution.py:384
  102.6 4.4 %collective-permute-done.10.refs_2_ = bf16[2,144,256]{2,1,0:T(8,128)(2,1)S(1)} collective-permute-done((bf16[2,144,256]{2,1,0:T(8,128)(2,1)S(1)}, bf16[2,144,256]{2,1,0:T(8,128)(2,1)S(1)}, u32[]{:S(2)}, u32[]{:S(2)}) %collective-permute-start.10) | collective-permute-done | bytes 147488 | tf_op jit(solution)/shard_map/ppermute | solution.py:384
  107.1 2.3 %collective-permute-done.11.refs_3_ = bf16[2,144,256]{2,1,0:T(8,128)(2,1)S(1)} collective-permute-done((bf16[2,144,256]{2,1,0:T(8,128)(2,1)S(1)}, bf16[2,144,256]{2,1,0:T(8,128)(2,1)S(1)}, u32[]{:S(2)}, u32[]{:S(2)}) %collective-permute-start.11) | collective-permute-done | bytes 147488 | tf_op jit(solution)/shard_map/ppermute | solution.py:384
  109.3 0.9 last_sum.1
  (1 shorter events, 0.0 us)
Async XLA Ops:
  4.5 12.8 %collective-permute-start.1 = (bf16[4,256,256]{2,1,0:T(8,128)(2,1)S(1)}, bf16[4,256,256]{2,1,0:T(8,128)(2,1)S(1)}, u32[]{:S(2)}, u32[]{:S(2)}) collective-permute-start(bf16[4,256,256]{2,1,0:T(8,128)(2,1)S(1)} %get-tuple-element.43), channel_id=1, source_target_pairs={{8,0},{16,8},{24,16},{32,24},{40,32},{48,40},{56,48},{64,56},{72,6... | collective-permute-start | bytes 1572872 | tf_op jit(solution)/shard_map/ppermute | solution.py:310
  14.5 13.5 %collective-permute-start = (bf16[4,256,256]{2,1,0:T(8,128)(2,1)S(1)}, bf16[4,256,256]{2,1,0:T(8,128)(2,1)S(1)}, u32[]{:S(2)}, u32[]{:S(2)}) collective-permute-start(bf16[4,256,256]{2,1,0:T(8,128)(2,1)S(1)} %get-tuple-element.42), channel_id=1, source_target_pairs={{8,0},{16,8},{24,16},{32,24},{40,32},{48,40},{56,48},{64,56},{72,6... | collective-permute-start | bytes 1572872 | tf_op jit(solution)/shard_map/ppermute | solution.py:310
  21.5 13.2 %collective-permute-start.3 = (bf16[4,256,256]{2,1,0:T(8,128)(2,1)S(1)}, bf16[4,256,256]{2,1,0:T(8,128)(2,1)S(1)}, u32[]{:S(2)}, u32[]{:S(2)}) collective-permute-start(bf16[4,256,256]{2,1,0:T(8,128)(2,1)S(1)} %get-tuple-element.47), channel_id=1, source_target_pairs={{8,0},{16,8},{24,16},{32,24},{40,32},{48,40},{56,48},{64,56},{72,6... | collective-permute-start | bytes 1572872 | tf_op jit(solution)/shard_map/ppermute | solution.py:310
  32.2 13.0 %collective-permute-start.2 = (bf16[4,256,256]{2,1,0:T(8,128)(2,1)S(1)}, bf16[4,256,256]{2,1,0:T(8,128)(2,1)S(1)}, u32[]{:S(2)}, u32[]{:S(2)}) collective-permute-start(bf16[4,256,256]{2,1,0:T(8,128)(2,1)S(1)} %get-tuple-element.46), channel_id=1, source_target_pairs={{8,0},{16,8},{24,16},{32,24},{40,32},{48,40},{56,48},{64,56},{72,6... | collective-permute-start | bytes 1572872 | tf_op jit(solution)/shard_map/ppermute | solution.py:310
  38.8 20.7 %collective-permute-start.5 = (bf16[4,256,256]{2,1,0:T(8,128)(2,1)S(1)}, bf16[4,256,256]{2,1,0:T(8,128)(2,1)S(1)}, u32[]{:S(2)}, u32[]{:S(2)}) collective-permute-start(bf16[4,256,256]{2,1,0:T(8,128)(2,1)S(1)} %get-tuple-element.60), channel_id=1, source_target_pairs={{8,0},{16,8},{24,16},{32,24},{40,32},{48,40},{56,48},{64,56},{72,6... | collective-permute-start | bytes 1572872 | tf_op jit(solution)/shard_map/ppermute | solution.py:310
  49.4 17.0 %collective-permute-start.4 = (bf16[4,256,256]{2,1,0:T(8,128)(2,1)S(1)}, bf16[4,256,256]{2,1,0:T(8,128)(2,1)S(1)}, u32[]{:S(2)}, u32[]{:S(2)}) collective-permute-start(bf16[4,256,256]{2,1,0:T(8,128)(2,1)S(1)} %get-tuple-element.50), channel_id=1, source_target_pairs={{8,0},{16,8},{24,16},{32,24},{40,32},{48,40},{56,48},{64,56},{72,6... | collective-permute-start | bytes 1572872 | tf_op jit(solution)/shard_map/ppermute | solution.py:310
  64.8 15.5 %collective-permute-start.6 = (bf16[2,2,2,144,256]{4,3,2,1,0:T(8,128)(2,1)}, bf16[2,2,2,144,256]{4,3,2,1,0:T(8,128)(2,1)S(1)}, u32[]{:S(2)}, u32[]{:S(2)}) collective-permute-start(bf16[2,2,2,144,256]{4,3,2,1,0:T(8,128)(2,1)} %get-tuple-element.67), channel_id=1, source_target_pairs={{0,2},{2,0},{4,6},{6,4},{1,3},{3,1},{5,7},{7,5},{8,10},{10,8},{12,... | collective-permute-start | bytes 1769480 | tf_op jit(solution)/shard_map/ppermute | solution.py:359
  66.4 14.0 %copy-start = (bf16[2,2,2,144,256]{4,3,2,1,0:T(8,128)(2,1)S(1)}, bf16[2,2,2,144,256]{4,3,2,1,0:T(8,128)(2,1)}, u32[]{:S(2)}) copy-start(bf16[2,2,2,144,256]{4,3,2,1,0:T(8,128)(2,1)} %get-tuple-element.66.mine) | copy-start | bytes 1769476
  71.8 17.7 %collective-permute-start.8 = (bf16[2,2,2,144,256]{4,3,2,1,0:T(8,128)(2,1)}, bf16[2,2,2,144,256]{4,3,2,1,0:T(8,128)(2,1)S(1)}, u32[]{:S(2)}, u32[]{:S(2)}) collective-permute-start(bf16[2,2,2,144,256]{4,3,2,1,0:T(8,128)(2,1)} %get-tuple-element.71), channel_id=1, source_target_pairs={{0,6},{2,4},{4,2},{6,0},{1,7},{3,5},{5,3},{7,1},{8,14},{10,12},{12... | collective-permute-start | bytes 1769480 | tf_op jit(solution)/shard_map/ppermute | solution.py:359
  80.5 14.2 %collective-permute-start.7 = (bf16[2,2,144,256]{3,2,1,0:T(8,128)(2,1)S(1)}, bf16[2,2,144,256]{3,2,1,0:T(8,128)(2,1)S(1)}, u32[]{:S(2)}, u32[]{:S(2)}) collective-permute-start(bf16[2,2,144,256]{3,2,1,0:T(8,128)(2,1)S(1)} %get-tuple-element.69), channel_id=1, source_target_pairs={{0,6},{2,4},{4,2},{6,0},{1,7},{3,5},{5,3},{7,1},{8,14},{10,12},{12... | collective-permute-start | bytes 884744 | tf_op jit(solution)/shard_map/ppermute | solution.py:370
  89.6 1.1 copy-start.1
  90.7 8.6 %collective-permute-start.9 = (bf16[2,2,144,256]{3,2,1,0:T(8,128)(2,1)S(1)}, bf16[2,2,144,256]{3,2,1,0:T(8,128)(2,1)S(1)}, u32[]{:S(2)}, u32[]{:S(2)}) collective-permute-start(bf16[2,2,144,256]{3,2,1,0:T(8,128)(2,1)S(1)} %get-tuple-element.75), channel_id=1, source_target_pairs={{0,2},{2,0},{4,6},{6,4},{1,3},{3,1},{5,7},{7,5},{8,10},{10,8},{12,... | collective-permute-start | bytes 884744 | tf_op jit(solution)/shard_map/ppermute | solution.py:370
  94.7 12.3 %collective-permute-start.10 = (bf16[2,144,256]{2,1,0:T(8,128)(2,1)S(1)}, bf16[2,144,256]{2,1,0:T(8,128)(2,1)S(1)}, u32[]{:S(2)}, u32[]{:S(2)}) collective-permute-start(bf16[2,144,256]{2,1,0:T(8,128)(2,1)S(1)} %get-tuple-element.78), channel_id=1, source_target_pairs={{0,1},{1,0},{2,3},{3,2},{4,5},{5,4},{6,7},{7,6},{8,9},{9,8},{10,11... | collective-permute-start | bytes 442376 | tf_op jit(solution)/shard_map/ppermute | solution.py:384
  99.9 9.4 %collective-permute-start.11 = (bf16[2,144,256]{2,1,0:T(8,128)(2,1)S(1)}, bf16[2,144,256]{2,1,0:T(8,128)(2,1)S(1)}, u32[]{:S(2)}, u32[]{:S(2)}) collective-permute-start(bf16[2,144,256]{2,1,0:T(8,128)(2,1)S(1)} %get-tuple-element.79), channel_id=1, source_target_pairs={{0,1},{1,0},{2,3},{3,2},{4,5},{5,4},{6,7},{7,6},{8,9},{9,8},{10,11... | collective-permute-start | bytes 442376 | tf_op jit(solution)/shard_map/ppermute | solution.py:384

commit v2 on v1

v2 whole, which is shorter than its diff:
```python
import functools

import jax
import jax.numpy as jnp
from jax import lax
from jax.experimental import pallas as pl
from jax.experimental.pallas import tpu as pltpu
from jax.sharding import Mesh
from jax.sharding import PartitionSpec as P

GW = 128
HW = 16
TICKS = 4
CELLS = HW * HW
ROWS = 9 * GW
SHARE = ROWS // 8
HALVES = 2
FIRST = TICKS - 2
VMEM_LIMIT = 24 * 1024 * 1024


def column_shifts(field, at_left, at_right):
    before = jnp.where(at_left, 0.0, pltpu.roll(field, 1, 0))
    after = jnp.where(at_right, 0.0, pltpu.roll(field, CELLS - 1, 0))
    return jnp.concatenate(
        [before.astype(jnp.bfloat16), field.astype(jnp.bfloat16), after.astype(jnp.bfloat16)], axis=1
    )


def row_shifts(field):
    edge = jnp.zeros((HW, GW), field.dtype)
    up = jnp.concatenate([field[HW:], edge], axis=0)
    down = jnp.concatenate([edge, field[:-HW]], axis=0)
    return jnp.concatenate([up, field, down], axis=1)


def taps_by_row(kernel_ref, branch, lanes):
    return jnp.concatenate(
        [kernel_ref[branch, pl.ds(a * 3 * GW, 3 * GW), lanes] for a in range(3)], axis=1
    )


def conv(stack, kernel):
    parts = jnp.dot(stack, kernel, preferred_element_type=jnp.float32)
    edge = jnp.zeros((HW, GW), jnp.float32)
    above = jnp.concatenate([edge, parts[:-HW, :GW]], axis=0)
    below = jnp.concatenate([parts[HW:, 2 * GW :], edge], axis=0)
    return parts[:, GW : 2 * GW] + above + below


def conv_back(stack, kernel, at_left, at_right):
    parts = lax.dot_general(
        stack, kernel, (((1,), (1,)), ((), ())), preferred_element_type=jnp.float32
    )
    before = jnp.where(at_right, 0.0, pltpu.roll(parts[:, :GW], CELLS - 1, 0))
    after = jnp.where(at_left, 0.0, pltpu.roll(parts[:, 2 * GW :], 1, 0))
    return parts[:, GW : 2 * GW] + before + after


def correlate(columns, rows):
    return lax.dot_general(
        columns, rows, (((0,), (0,)), ((), ())), preferred_element_type=jnp.float32
    )


def masks():
    column = lax.rem(lax.broadcasted_iota(jnp.int32, (CELLS, GW), 0), HW)
    return column == 0, column == HW - 1


def masks():
    column = lax.rem(lax.broadcasted_iota(jnp.int32, (CELLS, GW), 0), HW)
    return column == 0, column == HW - 1


def group_lanes(group):
    return pl.ds(group * GW, GW)


def first_branch(state_ref, lanes, weights, keep):
    edges = masks()
    grad_two = state_ref[3, :, lanes]
    out_one = state_ref[0, :, lanes].astype(jnp.float32)
    sigma = jax.nn.sigmoid(out_one)
    slope = sigma * (1.0 + out_one * (1.0 - sigma))
    columns = column_shifts(out_one * sigma, *edges)
    rows = row_shifts(grad_two)
    keep(1, columns, rows)
    weights = weights()
    in_two = (state_ref[1, :, lanes].astype(jnp.float32) - conv(columns, weights)).astype(
        jnp.bfloat16
    )
    total_one = (
        state_ref[2, :, lanes].astype(jnp.float32) + conv_back(rows, weights, *edges) * slope
    ).astype(jnp.bfloat16)
    return in_two, total_one


def second_branch(state_ref, lanes, weights, in_two, total_one, keep):
    edges = masks()
    wide_two = in_two.astype(jnp.float32)
    sigma = jax.nn.sigmoid(wide_two)
    slope = sigma * (1.0 + wide_two * (1.0 - sigma))
    columns = column_shifts(wide_two * sigma, *edges)
    rows = row_shifts(total_one)
    keep(0, columns, rows)
    weights = weights()
    out_one = state_ref[0, :, lanes].astype(jnp.float32)
    grad_two = state_ref[3, :, lanes].astype(jnp.float32)
    state_ref[0, :, lanes] = (out_one - conv(columns, weights)).astype(jnp.bfloat16)
    state_ref[1, :, lanes] = in_two
    state_ref[2, :, lanes] = total_one
    state_ref[3, :, lanes] = (grad_two + conv_back(rows, weights, *edges) * slope).astype(
        jnp.bfloat16
    )


def section_back(state_ref, groups, weights, keep):
    halfway = [
        first_branch(
            state_ref,
            group_lanes(group),
            functools.partial(weights, group, 1),
            functools.partial(keep, group),
        )
        for group in range(groups)
    ]
    for group in range(groups):
        second_branch(
            state_ref,
            group_lanes(group),
            functools.partial(weights, group, 0),
            *halfway[group],
            functools.partial(keep, group),
        )


def take_state(places, tick, half, width, received, top, made, sem):
    @pl.when(places[0] == 1)
    def _():
        copy = pltpu.make_async_copy(
            top.at[tick - 1, :, :, pl.ds(half * width, width)], made, sem
        )
        copy.start()
        copy.wait()

    @pl.when(places[0] == 0)
    def _():
        made[...] = received[...]


def kernel_loads(half, width, kernels, held, sems):
    copies = {}
    for branch in (1, 0):
        for group in range(width // GW):
            wide = pl.ds(half * width + group * GW, GW)
            copies[group, branch] = pltpu.make_async_copy(
                kernels.at[branch, :, wide],
                held.at[branch, :, group_lanes(group)],
                sems.at[branch, group],
            )
            copies[group, branch].start()
    return copies


def early_tick(tick, half, width, *refs):
    groups = width // GW
    if (tick, half) == (0, 0):
        states, kernels, earlier, *refs = refs
    elif tick == 0:
        states, kernels, held, earlier, *refs = refs
    else:
        places, received, top, kernels, held, earlier, *refs = refs
    made, kept, turn, following, sent, next_sems, out_sems, *refs = refs
    loads = {}
    if tick == 0:
        state_sems, *refs = refs
        for group in range(groups):
            wide = pl.ds(half * width + group * GW, GW)
            loads[group] = pltpu.make_async_copy(
                states.at[:, :, wide], made.at[:, :, group_lanes(group)], state_sems.at[group]
            )
            loads[group].start()
    if (tick, half) == (0, 0):
        held, sems = refs
        loads.update(kernel_loads(half, width, kernels, held, sems))
    outgoing = list(
        kernel_loads((half + 1) % HALVES, width, kernels, following, next_sems).values()
    )
    turn[...] = jnp.zeros_like(turn)
    if tick:
        take_state(places, tick, half, width, received, top, made, refs[0])
    else:
        for group in range(groups):
            loads[group].wait()

    def weights(group, branch):
        if (group, branch) in loads:
            loads[group, branch].wait()
        return taps_by_row(held, branch, group_lanes(group))

    def keep(group, branch, columns, rows):
        lanes = group_lanes(group)
        sent[branch, 0, :, lanes] = columns[:, GW : 2 * GW]
        sent[branch, 1, :, lanes] = rows[:, GW : 2 * GW]
        if group == groups - 1:
            copy = pltpu.make_async_copy(sent.at[branch], kept.at[branch], out_sems.at[branch])
            copy.start()
            outgoing.append(copy)

    section_back(made, groups, weights, keep)
    for copy in outgoing:
        copy.wait()


def early_terms(width, *refs):
    kept = [refs[half * FIRST : (half + 1) * FIRST] for half in range(HALVES)]
    earlier, *refs = refs[HALVES * FIRST :]
    totals = refs[:HALVES]
    turn, fields, summed, sems, out_sems = refs[HALVES:]
    turn[...] = jnp.zeros_like(turn)
    edges = masks()
    copies = {}
    for half in range(HALVES):
        for tick in range(FIRST):
            copies[half, tick] = pltpu.make_async_copy(
                kept[half][tick], fields.at[half, tick], sems.at[half, tick]
            )
            copies[half, tick].start()
    outgoing = []
    for half in range(HALVES):
        for tick in range(FIRST):
            copies[half, tick].wait()
        for branch in range(2):
            for group in range(width // GW):
                lanes = group_lanes(group)
                planes = [
                    [fields[half, tick, branch, at, :, lanes] for tick in range(FIRST)]
                    for at in range(2)
                ]
                columns = [column_shifts(field.astype(jnp.float32), *edges) for field in planes[0]]
                rows = [row_shifts(field) for field in planes[1]]
                term = correlate(
                    jnp.concatenate(columns, axis=0), jnp.concatenate(rows, axis=0)
                ).astype(jnp.bfloat16)
                for a in range(3):
                    summed[half, branch, pl.ds(a * 3 * GW, 3 * GW), lanes] = term[
                        :, a * GW : (a + 1) * GW
                    ]
        copy = pltpu.make_async_copy(summed.at[half], totals[half], out_sems.at[half])
        copy.start()
        outgoing.append(copy)
    for copy in outgoing:
        copy.wait()


def last_tick(half, width, places, received, top, kernels, held, total, kept, earlier, *rest):
    if half:
        rest = rest[1:]
    made, final, mine, *rest = rest
    theirs, rest = rest[:2], rest[2:]
    groups = width // GW
    copies = []
    turn, *rest = rest
    if half + 1 < HALVES:
        following, summed, top_sem, final_sem, next_sems = rest
        copies.extend(kernel_loads(half + 1, width, kernels, following, next_sems).values())
    else:
        summed, top_sem, final_sem = rest
    turn[...] = jnp.zeros_like(turn)
    take_state(places, TICKS - 1, half, width, received, top, made, top_sem)
    stacks = {}

    def weights(group, branch):
        return taps_by_row(held, branch, group_lanes(group))

    def keep(group, branch, columns, rows):
        stacks[group, branch] = columns, rows

    section_back(made, groups, weights, keep)
    copy = pltpu.make_async_copy(made, final.at[:, :, pl.ds(half * width, width)], final_sem)
    copy.start()
    copies.append(copy)
    edges = masks()
    for branch in range(2):
        for group in range(groups):
            lanes = group_lanes(group)
            columns, rows = stacks[group, branch]
            early_columns = column_shifts(kept[branch, 0, :, lanes].astype(jnp.float32), *edges)
            term = correlate(
                jnp.concatenate([early_columns, columns], axis=0),
                jnp.concatenate([row_shifts(kept[branch, 1, :, lanes]), rows], axis=0),
            )
            for a in range(3):
                at = pl.ds(a * 3 * GW, 3 * GW)
                summed[branch, at, lanes] = (
                    total[branch, at, lanes].astype(jnp.float32) + term[:, a * GW : (a + 1) * GW]
                ).astype(jnp.bfloat16)
        for slot in range(4):
            for z_slot in range(2):
                block = pl.multiple_of(places[1 + 4 * branch + slot] + places[9 + z_slot], 16)
                share = summed[branch, pl.ds(block, SHARE), :]
                if slot < 2:
                    mine[branch, slot, z_slot] = share
                else:
                    theirs[branch][slot - 2, z_slot] = share
    for copy in copies:
        copy.wait()


ANY_REF = pl.BlockSpec(memory_space=pl.ANY)
VMEM_REF = pl.BlockSpec(memory_space=pltpu.VMEM)
SMEM_REF = pl.BlockSpec(memory_space=pltpu.SMEM)


def in_vmem(array):
    return pltpu.with_memory_space_constraint(array, pltpu.VMEM)


def in_hbm(array):
    return pltpu.with_memory_space_constraint(array, pltpu.HBM)


def params():
    return pltpu.CompilerParams(vmem_limit_bytes=VMEM_LIMIT)


def cost(products, width):
    groups = width // GW
    return pl.CostEstimate(
        flops=products * 2 * CELLS * ROWS * GW * groups,
        bytes_accessed=4 * 4 * CELLS * width,
        transcendentals=2 * CELLS * width,
    )


def passed_down(value):
    count = lax.axis_size("section")
    return lax.ppermute(value, "section", [(source, source - 1) for source in range(1, count)])


def partners(branch, x):
    return (x ^ 1, 3 - x) if branch == 0 else (3 - x, x ^ 1)


def share_places():
    x, z = lax.axis_index("dp_0"), lax.axis_index("dp_1")
    is_top = lax.axis_index("section") == lax.axis_size("section") - 1
    numbers = [is_top]
    for branch in range(2):
        first, second = partners(branch, x)
        numbers += [at * (2 * SHARE) for at in (x, second, first, partners(branch, first)[1])]
    numbers += [z * SHARE, (1 - z) * SHARE]
    return jnp.stack([number.astype(jnp.int32) for number in numbers])


def first_sum(mine, *refs):
    came, refs = refs[:2], refs[2:]
    earlier, passed, turn = refs[0], refs[1:3], refs[3]
    turn[...] = jnp.zeros_like(turn)
    for branch in range(2):
        passed[branch][...] = (
            mine[branch, 1].astype(jnp.float32) + came[branch][1].astype(jnp.float32)
        ).astype(jnp.bfloat16)


def second_sum(mine, *refs):
    came, came_next, refs = refs[:2], refs[2:4], refs[4:]
    earlier, across, kept, turn = refs
    turn[...] = jnp.zeros_like(turn)
    for branch in range(2):
        total = [
            mine[branch, 0, z_slot].astype(jnp.float32)
            + came[branch][0, z_slot].astype(jnp.float32)
            + came_next[branch][z_slot].astype(jnp.float32)
            for z_slot in range(2)
        ]
        kept[branch] = total[0]
        across[branch] = total[1].astype(jnp.bfloat16)


def last_sum(*refs):
    kept, came, out = refs[:HALVES], refs[HALVES:-1], refs[-1]
    for half in range(HALVES):
        width = kept[half].shape[-1]
        out[:, :, pl.ds(half * width, width)] = (
            kept[half][...] + came[half][...].astype(jnp.float32)
        ) * (1.0 / (HW * HW))


def summed_shares(mine, theirs, turn):
    width = mine[0].shape[-1]
    turn_type = pltpu.VMEM((8, 128), jnp.float32)
    halves = range(HALVES)
    pairs = [
        [[(x, partners(branch, x)[step]) for x in range(4)] for step in range(2)]
        for branch in range(2)
    ]
    passed_type = pltpu.VMEM((2, SHARE, width), jnp.bfloat16)
    came = [
        [in_vmem(lax.ppermute(theirs[half][b], "dp_0", pairs[b][0])) for b in range(2)]
        for half in halves
    ]
    came_next, came_last, kept = [], [], []
    for half in halves:
        *passed, turn = pl.pallas_call(
            first_sum,
            out_shape=(passed_type, passed_type, turn_type),
            in_specs=[VMEM_REF] * 3 + [ANY_REF],
            out_specs=(VMEM_REF,) * 3,
            compiler_params=params(),
            name=f"first_sum_{half}",
        )(mine[half], *came[half], turn)
        came_next.append(
            [in_vmem(lax.ppermute(passed[b], "dp_0", pairs[b][1])) for b in range(2)]
        )
    for half in halves:
        across, own, turn = pl.pallas_call(
            second_sum,
            out_shape=(passed_type, pltpu.VMEM((2, SHARE, width), jnp.float32), turn_type),
            in_specs=[VMEM_REF] * 5 + [ANY_REF],
            out_specs=(VMEM_REF, VMEM_REF, VMEM_REF),
            compiler_params=params(),
            name=f"second_sum_{half}",
        )(mine[half], *came[half], *came_next[half], turn)
        came_last.append(lax.ppermute(across, "dp_1", [(0, 1), (1, 0)]))
        kept.append(own)
    return pl.pallas_call(
        last_sum,
        out_shape=jax.ShapeDtypeStruct((2, SHARE, width * HALVES), jnp.float32),
        in_specs=[VMEM_REF] * (2 * HALVES),
        out_specs=VMEM_REF,
        compiler_params=params(),
        name="last_sum",
    )(*[in_vmem(own) for own in kept], *[in_vmem(part) for part in came_last])


def on_device(section_states, conv_kernels, top_feed):
    chans = section_states.shape[-1]
    width = chans // HALVES
    states = in_hbm(section_states.reshape(4, CELLS, chans))
    kernels = in_hbm(conv_kernels[0])
    top = in_hbm(top_feed.reshape(TICKS - 1, 4, CELLS, chans))
    places = share_places()

    groups = width // GW
    state_type = pltpu.VMEM((4, CELLS, width), jnp.bfloat16)
    kept_type = pltpu.HBM((2, 2, CELLS, width), jnp.bfloat16)
    held_type = pltpu.VMEM((2, ROWS, width), jnp.bfloat16)
    turn_type = pltpu.VMEM((8, 128), jnp.float32)
    dma = pltpu.SemaphoreType.DMA
    kept_scratch = pltpu.VMEM((2, 2, CELLS, width), jnp.bfloat16)
    turn = jnp.zeros((8, 128), jnp.float32)
    held = None
    made, kept = [None] * HALVES, [[] for _ in range(HALVES)]
    for tick in range(TICKS - 1):
        for half in range(HALVES):
            aliases = {}
            scratch = [kept_scratch, dma((2, groups)), dma((2,))]
            if tick:
                operands = [places, in_vmem(made[half]), top, kernels, held, turn]
                specs = [SMEM_REF, VMEM_REF, ANY_REF, ANY_REF, VMEM_REF, ANY_REF]
                aliases = {1: 0}
                scratch += [dma(())]
            elif half:
                operands, specs = [states, kernels, held, turn], [ANY_REF, ANY_REF, VMEM_REF, ANY_REF]
                scratch += [dma((groups,))]
            else:
                operands, specs = [states, kernels, turn], [ANY_REF] * 3
                scratch += [dma((groups,)), held_type, dma((2, groups))]
            out, fields, turn, following = pl.pallas_call(
                functools.partial(early_tick, tick, half, width),
                out_shape=(state_type, kept_type, turn_type, held_type),
                in_specs=specs,
                out_specs=(VMEM_REF, ANY_REF, VMEM_REF, VMEM_REF),
                scratch_shapes=scratch,
                input_output_aliases=aliases,
                compiler_params=params(),
                cost_estimate=cost(4, width),
                name=f"tick_{tick}_{half}",
            )(*operands)
            held = in_vmem(following)
            made[half] = passed_down(out)
            kept[half].append(fields)
            if (tick, half) == (FIRST, 0):
                *total, turn = pl.pallas_call(
                    functools.partial(early_terms, width),
                    out_shape=(
                        *[pltpu.HBM((2, ROWS, width), jnp.bfloat16) for _ in range(HALVES)],
                        turn_type,
                    ),
                    in_specs=[ANY_REF] * (HALVES * FIRST + 1),
                    out_specs=(*[ANY_REF] * HALVES, VMEM_REF),
                    scratch_shapes=[
                        pltpu.VMEM((HALVES, FIRST, 2, 2, CELLS, width), jnp.bfloat16),
                        pltpu.VMEM((HALVES, 2, ROWS, width), jnp.bfloat16),
                        dma((HALVES, FIRST)),
                        dma((HALVES,)),
                    ],
                    compiler_params=params(),
                    cost_estimate=cost(2 * FIRST * HALVES, width),
                    name="early_terms",
                )(*[in_hbm(plane) for side in kept for plane in side[:FIRST]], turn)

    final = None
    mine, theirs = [None] * HALVES, [None] * HALVES
    theirs_type = pltpu.VMEM((2, 2, SHARE, width), jnp.bfloat16)
    for half in range(HALVES):
        operands = [places, in_vmem(made[half]), top, kernels, held, total[half], kept[half][FIRST], turn]
        specs = [SMEM_REF, VMEM_REF, ANY_REF, ANY_REF, VMEM_REF, VMEM_REF, VMEM_REF, ANY_REF]
        aliases = {1: 0}
        if half:
            aliases[len(operands)] = 1
            operands.append(in_hbm(final))
            specs.append(ANY_REF)
        more = half + 1 < HALVES
        _, final, mine[half], *theirs[half], turn = pl.pallas_call(
            functools.partial(last_tick, half, width),
            out_shape=(
                state_type,
                pltpu.HBM((4, CELLS, chans), jnp.bfloat16),
                pltpu.VMEM((2, 2, 2, SHARE, width), jnp.bfloat16),
                theirs_type,
                theirs_type,
                turn_type,
                *[held_type] * more,
            ),
            in_specs=specs,
            out_specs=(VMEM_REF, ANY_REF, *[VMEM_REF] * (4 + more)),
            scratch_shapes=[
                pltpu.VMEM((2, ROWS, width), jnp.bfloat16),
                dma(()),
                dma(()),
                *[dma((2, groups))] * more,
            ],
            input_output_aliases=aliases,
            compiler_params=params(),
            cost_estimate=cost(6, width),
            name=f"last_tick_{half}",
        )(*operands)
        if more:
            held = in_vmem(turn)
            *theirs[half], turn = theirs[half]
    grads = summed_shares(mine, theirs, turn)
    return (final.reshape(1, 4, 1, HW, HW, chans), grads[None])


def solution(mesh):
    finer = Mesh(mesh.devices.reshape(mesh.shape["section"], 4, 2), ("section", "dp_0", "dp_1"))
    images = ("dp_0", "dp_1")
    in_specs = (
        P("section", None, images, None, None, None),
        P("section", None, None, None),
        P(None, None, images, None, None, None),
    )
    out_specs = (P("section", None, images, None, None, None), P("section", None, images, None))
    return jax.shard_map(
        on_device, mesh=finer, in_specs=in_specs, out_specs=out_specs, check_vma=False
    )
```

time: 111 us -> 92.4 us (0.83)
  Pallas kernels: 44.1 us -> 27.5 us
  waiting for transfers between devices: 23.4 us -> 15.7 us
  starting transfers between devices: 40.6 us -> 47.8 us
  local copies, waits for them, and re-layouts: 1.25 us -> 0.11 us
    ppermute x4 -> x8, waiting for transfers between devices: 16.5 us -> 7.23 us  [the longest x4 6.79 us: summed_shares(): lax.ppermute(theirs[half][b], 'dp_0', pairs[b][0])]
    pallas_call x6, Pallas kernels: 24.2 us -> 15.5 us  [on_device(): pl.pallas_call(functools.partial(early_tick, tick, half, width), out_shap...]
    ppermute x4 -> x8, starting transfers between devices: 6.7 us -> 11.6 us  [the longest x4 7.24 us: summed_shares(): lax.ppermute(theirs[half][b], 'dp_0', pairs[b][0])]
    pallas_call x2, Pallas kernels: 10.8 us -> 5.86 us  [on_device(): pl.pallas_call(functools.partial(last_tick, half, width), out_shape=(stat...]
    pallas_call x6 -> x5, Pallas kernels: 8.29 us -> 5.18 us  [the longest x1 4.3 us: on_device(): pl.pallas_call(functools.partial(early_terms, width), out_shape=(*[pltpu....]
    ppermute x6, waiting for transfers between devices: 0.27 us -> 2.15 us  [passed_down(): lax.ppermute(value, 'section', [(source, source - 1) for source in range(...]
    ppermute x2, starting transfers between devices: 7.27 us -> 9.07 us  [summed_shares(): came_last.append(lax.ppermute(across, 'dp_1', [(0, 1), (1, 0)]))]
  transfers between devices with their start and end apart: 12 -> 16, of which waited for: 7 -> 8; matrix products, arithmetic and copies ran while one was open for 0% -> 0% of each run, Pallas kernels for 36% -> 24%
where the time goes in v2:
time: 92.4 us; the launch traced here: 92 us
  starting transfers between devices  47.8 us (52%)
  Pallas kernels  27.5 us (30%)
  waiting for transfers between devices  15.7 us (17%)
    ppermute x6, starting transfers between devices, passed_down(): lax.ppermute(value, 'section', [(source, source - 1) for source in range(...  27.1 us
    pallas_call x6, Pallas kernels, on_device(): pl.pallas_call(functools.partial(early_tick, tick, half, width), out_shap...  15.5 us
    ppermute x2, starting transfers between devices, summed_shares(): came_last.append(lax.ppermute(across, 'dp_1', [(0, 1), (1, 0)]))  9.07 us
    ppermute x4, starting transfers between devices, summed_shares(): lax.ppermute(theirs[half][b], 'dp_0', pairs[b][0])  7.24 us
    ppermute x4, waiting for transfers between devices, summed_shares(): lax.ppermute(theirs[half][b], 'dp_0', pairs[b][0])  6.79 us
    ppermute x2, waiting for transfers between devices, summed_shares(): came_last.append(lax.ppermute(across, 'dp_1', [(0, 1), (1, 0)]))  6.32 us
    pallas_call x2, Pallas kernels, on_device(): pl.pallas_call(functools.partial(last_tick, half, width), out_shape=(stat...  5.86 us
    ppermute x4, starting transfers between devices, summed_shares(): lax.ppermute(passed[b], 'dp_0', pairs[b][1])  4.38 us
  transfers between devices with their start and end apart: 16, of which 8 were waited for; matrix products, arithmetic and copies ran while one was open for 0% of the time, Pallas kernels for 24%

profile of v2, /device:TPU:24, one launch (start us, length us, event | category | flops | bytes accessed | tf_op | source)
XLA Modules:
  0.0 92.0 jit_solution(9317480060688230962)
XLA Ops:
  0.6 4.1 %tick_0_0.1 = (bf16[4,256,256]{2,1,0:T(8,128)(2,1)S(1)}, bf16[2,2,256,256]{3,2,1,0:T(8,128)(2,1)}, f32[8,128]{1,0:T(8,128)S(1)}, bf16[2,1152,256]{2,1,0:T(8,128)(2,1)S(1)}) custom-call(bf16[4,256,512]{2,1,0:T(8,128)(2,1)} %bitcast.29, bf16[2,1152,512]{2,1,0:T(8,128)(2,1)} %bitcast.15, f32[8,128]{1,0:T(8,128)S(1)} %broadcast_in_dim.6.refs_2_), custom_call_target="tpu_custom_call" | custom-call | flops 603979776 | bytes 1048576 | tf_op jit(solution)/shard_map/tick_0_0/pallas_call | solution.py:471
  4.7 6.2 %collective-permute-start.1 = (bf16[4,256,256]{2,1,0:T(8,128)(2,1)S(1)}, bf16[4,256,256]{2,1,0:T(8,128)(2,1)S(1)}, u32[]{:S(2)}, u32[]{:S(2)}) collective-permute-start(bf16[4,256,256]{2,1,0:T(8,128)(2,1)S(1)} %get-tuple-element.54), channel_id=1, source_target_pairs={{8,0},{16,8},{24,16},{32,24},{40,32},{48,40},{56,48},{64,56},{72,6... | collective-permute-start | bytes 1572872 | tf_op jit(solution)/shard_map/ppermute | solution.py:339
  10.9 2.9 %tick_0_1.1 = (bf16[4,256,256]{2,1,0:T(8,128)(2,1)S(1)}, bf16[2,2,256,256]{3,2,1,0:T(8,128)(2,1)}, f32[8,128]{1,0:T(8,128)S(1)}, bf16[2,1152,256]{2,1,0:T(8,128)(2,1)S(1)}) custom-call(bf16[4,256,512]{2,1,0:T(8,128)(2,1)} %bitcast.30, bf16[2,1152,512]{2,1,0:T(8,128)(2,1)} %bitcast.16, bf16[2,1152,256]{2,1,0:T(8,128)(2,1)S(1)} %get-tuple-element.51.refs_2_, ...), custom_call_target="tpu_custom_call" | custom-call | flops 603979776 | bytes 1048576 | tf_op jit(solution)/shard_map/tick_0_1/pallas_call | solution.py:471
  13.7 2.6 %collective-permute-start = (bf16[4,256,256]{2,1,0:T(8,128)(2,1)S(1)}, bf16[4,256,256]{2,1,0:T(8,128)(2,1)S(1)}, u32[]{:S(2)}, u32[]{:S(2)}) collective-permute-start(bf16[4,256,256]{2,1,0:T(8,128)(2,1)S(1)} %get-tuple-element.53), channel_id=1, source_target_pairs={{8,0},{16,8},{24,16},{32,24},{40,32},{48,40},{56,48},{64,56},{72,6... | collective-permute-start | bytes 1572872 | tf_op jit(solution)/shard_map/ppermute | solution.py:339
  16.4 0.1 stack.42.refs_0_.places
  16.4 1.1 %collective-permute-done.1.refs_1_ = bf16[4,256,256]{2,1,0:T(8,128)(2,1)S(1)} collective-permute-done((bf16[4,256,256]{2,1,0:T(8,128)(2,1)S(1)}, bf16[4,256,256]{2,1,0:T(8,128)(2,1)S(1)}, u32[]{:S(2)}, u32[]{:S(2)}) %collective-permute-start.1) | collective-permute-done | bytes 524320 | tf_op jit(solution)/shard_map/ppermute | solution.py:339
  17.5 2.1 %tick_1_0.1 = (bf16[4,256,256]{2,1,0:T(8,128)(2,1)S(1)}, bf16[2,2,256,256]{3,2,1,0:T(8,128)(2,1)}, f32[8,128]{1,0:T(8,128)S(1)}, bf16[2,1152,256]{2,1,0:T(8,128)(2,1)S(1)}) custom-call(s32[11]{0:T(128)S(1)} %stack.42.refs_0_.places, bf16[4,256,256]{2,1,0:T(8,128)(2,1)S(1)} %collective-permute-done.1.refs_1_, ...), custom_call_target="tpu_custom_call", output_to_operand_aliasing={{0}: (1, {})} | custom-call | flops 603979776 | bytes 1048576 | tf_op jit(solution)/shard_map/tick_1_0/pallas_call | solution.py:471
  19.7 6.5 %collective-permute-start.3 = (bf16[4,256,256]{2,1,0:T(8,128)(2,1)S(1)}, bf16[4,256,256]{2,1,0:T(8,128)(2,1)S(1)}, u32[]{:S(2)}, u32[]{:S(2)}) collective-permute-start(bf16[4,256,256]{2,1,0:T(8,128)(2,1)S(1)} %get-tuple-element.60), channel_id=1, source_target_pairs={{8,0},{16,8},{24,16},{32,24},{40,32},{48,40},{56,48},{64,56},{72,6... | collective-permute-start | bytes 1572872 | tf_op jit(solution)/shard_map/ppermute | solution.py:339
  26.2 0.0 collective-permute-done.refs_1_
  26.2 2.1 %tick_1_1.1 = (bf16[4,256,256]{2,1,0:T(8,128)(2,1)S(1)}, bf16[2,2,256,256]{3,2,1,0:T(8,128)(2,1)}, f32[8,128]{1,0:T(8,128)S(1)}, bf16[2,1152,256]{2,1,0:T(8,128)(2,1)S(1)}) custom-call(s32[11]{0:T(128)S(1)} %stack.42.refs_0_.places, bf16[4,256,256]{2,1,0:T(8,128)(2,1)S(1)} %collective-permute-done.refs_1_, ...), custom_call_target="tpu_custom_call", output_to_operand_aliasing={{0}: (1, {})} | custom-call | flops 603979776 | bytes 1048576 | tf_op jit(solution)/shard_map/tick_1_1/pallas_call | solution.py:471
  28.3 3.5 %collective-permute-start.2 = (bf16[4,256,256]{2,1,0:T(8,128)(2,1)S(1)}, bf16[4,256,256]{2,1,0:T(8,128)(2,1)S(1)}, u32[]{:S(2)}, u32[]{:S(2)}) collective-permute-start(bf16[4,256,256]{2,1,0:T(8,128)(2,1)S(1)} %get-tuple-element.59), channel_id=1, source_target_pairs={{8,0},{16,8},{24,16},{32,24},{40,32},{48,40},{56,48},{64,56},{72,6... | collective-permute-start | bytes 1572872 | tf_op jit(solution)/shard_map/ppermute | solution.py:339
  31.8 1.0 %collective-permute-done.3.refs_1_ = bf16[4,256,256]{2,1,0:T(8,128)(2,1)S(1)} collective-permute-done((bf16[4,256,256]{2,1,0:T(8,128)(2,1)S(1)}, bf16[4,256,256]{2,1,0:T(8,128)(2,1)S(1)}, u32[]{:S(2)}, u32[]{:S(2)}) %collective-permute-start.3) | collective-permute-done | bytes 524320 | tf_op jit(solution)/shard_map/ppermute | solution.py:339
  32.9 2.2 %tick_2_0.1 = (bf16[4,256,256]{2,1,0:T(8,128)(2,1)S(1)}, bf16[2,2,256,256]{3,2,1,0:T(8,128)(2,1)}, f32[8,128]{1,0:T(8,128)S(1)}, bf16[2,1152,256]{2,1,0:T(8,128)(2,1)S(1)}) custom-call(s32[11]{0:T(128)S(1)} %stack.42.refs_0_.places, bf16[4,256,256]{2,1,0:T(8,128)(2,1)S(1)} %collective-permute-done.3.refs_1_, ...), custom_call_target="tpu_custom_call", output_to_operand_aliasing={{0}: (1, {})} | custom-call | flops 603979776 | bytes 1048576 | tf_op jit(solution)/shard_map/tick_2_0/pallas_call | solution.py:471
  35.1 6.5 %collective-permute-start.5 = (bf16[4,256,256]{2,1,0:T(8,128)(2,1)S(1)}, bf16[4,256,256]{2,1,0:T(8,128)(2,1)S(1)}, u32[]{:S(2)}, u32[]{:S(2)}) collective-permute-start(bf16[4,256,256]{2,1,0:T(8,128)(2,1)S(1)} %get-tuple-element.71), channel_id=1, source_target_pairs={{8,0},{16,8},{24,16},{32,24},{40,32},{48,40},{56,48},{64,56},{72,6... | collective-permute-start | bytes 1572872 | tf_op jit(solution)/shard_map/ppermute | solution.py:339
  41.6 4.3 %early_terms.1 = (bf16[2,1152,256]{2,1,0:T(8,128)(2,1)}, bf16[2,1152,256]{2,1,0:T(8,128)(2,1)}, f32[8,128]{1,0:T(8,128)S(1)}) custom-call(bf16[2,2,256,256]{3,2,1,0:T(8,128)(2,1)} %get-tuple-element.64.refs_0_, bf16[2,2,256,256]{3,2,1,0:T(8,128)(2,1)} %get-tuple-element.65.refs_1_, bf16[2,2,256,256]{3,2,1,0:T(8,128)(2,1)} %get-tuple-element.66.refs_2_, ...), custom_call_target="tpu_custom_call" | custom-call | flops 1207959552 | bytes 1048576 | tf_op jit(solution)/shard_map/early_terms/pallas_call | solution.py:486
  45.9 0.0 collective-permute-done.2.refs_1_
  45.9 0.0 copy-start.1
  45.9 0.0 copy-start.2
  45.9 2.1 %tick_2_1.1 = (bf16[4,256,256]{2,1,0:T(8,128)(2,1)S(1)}, bf16[2,2,256,256]{3,2,1,0:T(8,128)(2,1)}, f32[8,128]{1,0:T(8,128)S(1)}, bf16[2,1152,256]{2,1,0:T(8,128)(2,1)S(1)}) custom-call(s32[11]{0:T(128)S(1)} %stack.42.refs_0_.places, bf16[4,256,256]{2,1,0:T(8,128)(2,1)S(1)} %collective-permute-done.2.refs_1_, ...), custom_call_target="tpu_custom_call", output_to_operand_aliasing={{0}: (1, {})} | custom-call | flops 603979776 | bytes 1048576 | tf_op jit(solution)/shard_map/tick_2_1/pallas_call | solution.py:471
  48.1 1.9 %collective-permute-start.4 = (bf16[4,256,256]{2,1,0:T(8,128)(2,1)S(1)}, bf16[4,256,256]{2,1,0:T(8,128)(2,1)S(1)}, u32[]{:S(2)}, u32[]{:S(2)}) collective-permute-start(bf16[4,256,256]{2,1,0:T(8,128)(2,1)S(1)} %get-tuple-element.70), channel_id=1, source_target_pairs={{8,0},{16,8},{24,16},{32,24},{40,32},{48,40},{56,48},{64,56},{72,6... | collective-permute-start | bytes 1572872 | tf_op jit(solution)/shard_map/ppermute | solution.py:339
  50.0 0.0 collective-permute-done.5.received
  50.0 0.0 copy-done.1
  50.0 0.0 copy-done.2
  50.0 0.0 copy-start
  50.0 0.0 copy-start.3
  50.1 3.0 %last_tick_0.1 = (bf16[4,256,256]{2,1,0:T(8,128)(2,1)S(1)}, bf16[4,256,512]{2,1,0:T(8,128)(2,1)}, bf16[2,2,2,144,256]{4,3,2,1,0:T(8,128)(2,1)S(1)}, bf16[2,2,144...) custom-call(s32[11]{0:T(128)S(1)} %stack.42.refs_0_.places, ...), custom_call_target="tpu_custom_call", output_to_operand_aliasing={{0}: (1, {})} | custom-call | flops 905969664 | bytes 1048576 | tf_op jit(solution)/shard_map/last_tick_0/pallas_call | solution.py:517
  53.1 1.6 %collective-permute-start.6 = (bf16[2,2,144,256]{3,2,1,0:T(8,128)(2,1)S(1)}, bf16[2,2,144,256]{3,2,1,0:T(8,128)(2,1)S(1)}, u32[]{:S(2)}, u32[]{:S(2)}) collective-permute-start(bf16[2,2,144,256]{3,2,1,0:T(8,128)(2,1)S(1)} %get-tuple-element.83), channel_id=1, source_target_pairs={{0,2},{2,0},{4,6},{6,4},{1,3},{3,1},{5,7},{7,5},{8,10},{10,8},{12,... | collective-permute-start | bytes 884744 | tf_op jit(solution)/shard_map/ppermute | solution.py:401
  54.7 2.1 %collective-permute-start.7 = (bf16[2,2,144,256]{3,2,1,0:T(8,128)(2,1)S(1)}, bf16[2,2,144,256]{3,2,1,0:T(8,128)(2,1)S(1)}, u32[]{:S(2)}, u32[]{:S(2)}) collective-permute-start(bf16[2,2,144,256]{3,2,1,0:T(8,128)(2,1)S(1)} %get-tuple-element.84), channel_id=1, source_target_pairs={{0,6},{2,4},{4,2},{6,0},{1,7},{3,5},{5,3},{7,1},{8,14},{10,12},{12... | collective-permute-start | bytes 884744 | tf_op jit(solution)/shard_map/ppermute | solution.py:401
  56.8 0.0 collective-permute-done.4.received
  56.8 0.0 copy-done
  56.8 0.0 copy-done.3
  56.8 2.8 %last_tick_1.1 = (bf16[4,256,256]{2,1,0:T(8,128)(2,1)S(1)}, bf16[4,256,512]{2,1,0:T(8,128)(2,1)}, bf16[2,2,2,144,256]{4,3,2,1,0:T(8,128)(2,1)S(1)}, bf16[2,2,144...) custom-call(s32[11]{0:T(128)S(1)} %stack.42.refs_0_.places, ...), custom_call_target="tpu_custom_call", output_to_operand_aliasing={{0}: (1, {}), {1}: (8, {})} | custom-call | flops 905969664 | bytes 1048576 | tf_op jit(solution)/shard_map/last_tick_1/pallas_call | solution.py:517
  59.6 1.5 %collective-permute-start.10 = (bf16[2,2,144,256]{3,2,1,0:T(8,128)(2,1)S(1)}, bf16[2,2,144,256]{3,2,1,0:T(8,128)(2,1)S(1)}, u32[]{:S(2)}, u32[]{:S(2)}) collective-permute-start(bf16[2,2,144,256]{3,2,1,0:T(8,128)(2,1)S(1)} %get-tuple-element.89), channel_id=1, source_target_pairs={{0,2},{2,0},{4,6},{6,4},{1,3},{3,1},{5,7},{7,5},{8,10},{10,8},{12,... | collective-permute-start | bytes 884744 | tf_op jit(solution)/shard_map/ppermute | solution.py:401
  61.1 2.1 %collective-permute-start.11 = (bf16[2,2,144,256]{3,2,1,0:T(8,128)(2,1)S(1)}, bf16[2,2,144,256]{3,2,1,0:T(8,128)(2,1)S(1)}, u32[]{:S(2)}, u32[]{:S(2)}) collective-permute-start(bf16[2,2,144,256]{3,2,1,0:T(8,128)(2,1)S(1)} %get-tuple-element.90), channel_id=1, source_target_pairs={{0,6},{2,4},{4,2},{6,0},{1,7},{3,5},{5,3},{7,1},{8,14},{10,12},{12... | collective-permute-start | bytes 884744 | tf_op jit(solution)/shard_map/ppermute | solution.py:401
  63.2 0.0 collective-permute-done.6.refs_0_
  63.2 2.5 %collective-permute-done.7.refs_1_ = bf16[2,2,144,256]{3,2,1,0:T(8,128)(2,1)S(1)} collective-permute-done((bf16[2,2,144,256]{3,2,1,0:T(8,128)(2,1)S(1)}, bf16[2,2,144,256]{3,2,1,0:T(8,128)(2,1)S(1)}, u32[]{:S(2)}, u32[]{:S(2)}) %collective-permute-start.7) | collective-permute-done | bytes 294944 | tf_op jit(solution)/shard_map/ppermute | solution.py:401
  65.7 0.1 first_sum_0.1
  65.8 2.2 %collective-permute-start.8 = (bf16[2,144,256]{2,1,0:T(8,128)(2,1)S(1)}, bf16[2,144,256]{2,1,0:T(8,128)(2,1)S(1)}, u32[]{:S(2)}, u32[]{:S(2)}) collective-permute-start(bf16[2,144,256]{2,1,0:T(8,128)(2,1)S(1)} %get-tuple-element.86), channel_id=1, source_target_pairs={{0,6},{2,4},{4,2},{6,0},{1,7},{3,5},{5,3},{7,1},{8,14},{10,12},{12... | collective-permute-start | bytes 442376 | tf_op jit(solution)/shard_map/ppermute | solution.py:415
  68.0 0.0 collective-permute-start.9
  68.0 0.9 %collective-permute-done.10.refs_0_ = bf16[2,2,144,256]{3,2,1,0:T(8,128)(2,1)S(1)} collective-permute-done((bf16[2,2,144,256]{3,2,1,0:T(8,128)(2,1)S(1)}, bf16[2,2,144,256]{3,2,1,0:T(8,128)(2,1)S(1)}, u32[]{:S(2)}, u32[]{:S(2)}) %collective-permute-start.10) | collective-permute-done | bytes 294944 | tf_op jit(solution)/shard_map/ppermute | solution.py:401
  68.9 3.3 %collective-permute-done.11.refs_1_ = bf16[2,2,144,256]{3,2,1,0:T(8,128)(2,1)S(1)} collective-permute-done((bf16[2,2,144,256]{3,2,1,0:T(8,128)(2,1)S(1)}, bf16[2,2,144,256]{3,2,1,0:T(8,128)(2,1)S(1)}, u32[]{:S(2)}, u32[]{:S(2)}) %collective-permute-start.11) | collective-permute-done | bytes 294944 | tf_op jit(solution)/shard_map/ppermute | solution.py:401
  72.2 0.1 first_sum_1.1
  72.3 2.2 %collective-permute-start.12 = (bf16[2,144,256]{2,1,0:T(8,128)(2,1)S(1)}, bf16[2,144,256]{2,1,0:T(8,128)(2,1)S(1)}, u32[]{:S(2)}, u32[]{:S(2)}) collective-permute-start(bf16[2,144,256]{2,1,0:T(8,128)(2,1)S(1)} %get-tuple-element.94), channel_id=1, source_target_pairs={{0,6},{2,4},{4,2},{6,0},{1,7},{3,5},{5,3},{7,1},{8,14},{10,12},{12... | collective-permute-start | bytes 442376 | tf_op jit(solution)/shard_map/ppermute | solution.py:415
  74.5 0.0 collective-permute-start.13
  74.5 0.0 collective-permute-done.8.refs_2_
  74.5 0.0 collective-permute-done.9.refs_3_
  74.5 0.1 second_sum_0.1
  74.6 4.6 %collective-permute-start.14 = (bf16[2,144,256]{2,1,0:T(8,128)(2,1)S(1)}, bf16[2,144,256]{2,1,0:T(8,128)(2,1)S(1)}, u32[]{:S(2)}, u32[]{:S(2)}) collective-permute-start(bf16[2,144,256]{2,1,0:T(8,128)(2,1)S(1)} %get-tuple-element.98), channel_id=1, source_target_pairs={{0,1},{1,0},{2,3},{3,2},{4,5},{5,4},{6,7},{7,6},{8,9},{9,8},{10,11... | collective-permute-start | bytes 442376 | tf_op jit(solution)/shard_map/ppermute | solution.py:426
  79.2 0.0 collective-permute-done.12.refs_2_
  79.2 0.4 collective-permute-done.13.refs_3_
  79.7 0.6 second_sum_1.1
  80.3 4.5 %collective-permute-start.15 = (bf16[2,144,256]{2,1,0:T(8,128)(2,1)S(1)}, bf16[2,144,256]{2,1,0:T(8,128)(2,1)S(1)}, u32[]{:S(2)}, u32[]{:S(2)}) collective-permute-start(bf16[2,144,256]{2,1,0:T(8,128)(2,1)S(1)} %get-tuple-element.99), channel_id=1, source_target_pairs={{0,1},{1,0},{2,3},{3,2},{4,5},{5,4},{6,7},{7,6},{8,9},{9,8},{10,11... | collective-permute-start | bytes 442376 | tf_op jit(solution)/shard_map/ppermute | solution.py:426
  84.8 3.4 %collective-permute-done.14.refs_2_ = bf16[2,144,256]{2,1,0:T(8,128)(2,1)S(1)} collective-permute-done((bf16[2,144,256]{2,1,0:T(8,128)(2,1)S(1)}, bf16[2,144,256]{2,1,0:T(8,128)(2,1)S(1)}, u32[]{:S(2)}, u32[]{:S(2)}) %collective-permute-start.14) | collective-permute-done | bytes 147488 | tf_op jit(solution)/shard_map/ppermute | solution.py:426
  88.2 2.9 %collective-permute-done.15.refs_3_ = bf16[2,144,256]{2,1,0:T(8,128)(2,1)S(1)} collective-permute-done((bf16[2,144,256]{2,1,0:T(8,128)(2,1)S(1)}, bf16[2,144,256]{2,1,0:T(8,128)(2,1)S(1)}, u32[]{:S(2)}, u32[]{:S(2)}) %collective-permute-start.15) | collective-permute-done | bytes 147488 | tf_op jit(solution)/shard_map/ppermute | solution.py:426
  91.1 0.9 last_sum.1
  (1 shorter events, 0.0 us)
Async XLA Ops:
  4.7 12.8 %collective-permute-start.1 = (bf16[4,256,256]{2,1,0:T(8,128)(2,1)S(1)}, bf16[4,256,256]{2,1,0:T(8,128)(2,1)S(1)}, u32[]{:S(2)}, u32[]{:S(2)}) collective-permute-start(bf16[4,256,256]{2,1,0:T(8,128)(2,1)S(1)} %get-tuple-element.54), channel_id=1, source_target_pairs={{8,0},{16,8},{24,16},{32,24},{40,32},{48,40},{56,48},{64,56},{72,6... | collective-permute-start | bytes 1572872 | tf_op jit(solution)/shard_map/ppermute | solution.py:339
  13.7 12.4 %collective-permute-start = (bf16[4,256,256]{2,1,0:T(8,128)(2,1)S(1)}, bf16[4,256,256]{2,1,0:T(8,128)(2,1)S(1)}, u32[]{:S(2)}, u32[]{:S(2)}) collective-permute-start(bf16[4,256,256]{2,1,0:T(8,128)(2,1)S(1)} %get-tuple-element.53), channel_id=1, source_target_pairs={{8,0},{16,8},{24,16},{32,24},{40,32},{48,40},{56,48},{64,56},{72,6... | collective-permute-start | bytes 1572872 | tf_op jit(solution)/shard_map/ppermute | solution.py:339
  19.7 13.2 %collective-permute-start.3 = (bf16[4,256,256]{2,1,0:T(8,128)(2,1)S(1)}, bf16[4,256,256]{2,1,0:T(8,128)(2,1)S(1)}, u32[]{:S(2)}, u32[]{:S(2)}) collective-permute-start(bf16[4,256,256]{2,1,0:T(8,128)(2,1)S(1)} %get-tuple-element.60), channel_id=1, source_target_pairs={{8,0},{16,8},{24,16},{32,24},{40,32},{48,40},{56,48},{64,56},{72,6... | collective-permute-start | bytes 1572872 | tf_op jit(solution)/shard_map/ppermute | solution.py:339
  28.3 17.6 %collective-permute-start.2 = (bf16[4,256,256]{2,1,0:T(8,128)(2,1)S(1)}, bf16[4,256,256]{2,1,0:T(8,128)(2,1)S(1)}, u32[]{:S(2)}, u32[]{:S(2)}) collective-permute-start(bf16[4,256,256]{2,1,0:T(8,128)(2,1)S(1)} %get-tuple-element.59), channel_id=1, source_target_pairs={{8,0},{16,8},{24,16},{32,24},{40,32},{48,40},{56,48},{64,56},{72,6... | collective-permute-start | bytes 1572872 | tf_op jit(solution)/shard_map/ppermute | solution.py:339
  35.1 14.9 %collective-permute-start.5 = (bf16[4,256,256]{2,1,0:T(8,128)(2,1)S(1)}, bf16[4,256,256]{2,1,0:T(8,128)(2,1)S(1)}, u32[]{:S(2)}, u32[]{:S(2)}) collective-permute-start(bf16[4,256,256]{2,1,0:T(8,128)(2,1)S(1)} %get-tuple-element.71), channel_id=1, source_target_pairs={{8,0},{16,8},{24,16},{32,24},{40,32},{48,40},{56,48},{64,56},{72,6... | collective-permute-start | bytes 1572872 | tf_op jit(solution)/shard_map/ppermute | solution.py:339
  45.9 4.1 %copy-start.1 = (bf16[2,1152,256]{2,1,0:T(8,128)(2,1)S(1)}, bf16[2,1152,256]{2,1,0:T(8,128)(2,1)}, u32[]{:S(2)}) copy-start(bf16[2,1152,256]{2,1,0:T(8,128)(2,1)} %get-tuple-element.73.total) | copy-start | bytes 3538948
  45.9 4.1 %copy-start.2 = (bf16[2,2,256,256]{3,2,1,0:T(8,128)(2,1)S(1)}, bf16[2,2,256,256]{3,2,1,0:T(8,128)(2,1)}, u32[]{:S(2)}) copy-start(bf16[2,2,256,256]{3,2,1,0:T(8,128)(2,1)} %get-tuple-element.74.kept) | copy-start | bytes 1572868
  48.1 8.7 %collective-permute-start.4 = (bf16[4,256,256]{2,1,0:T(8,128)(2,1)S(1)}, bf16[4,256,256]{2,1,0:T(8,128)(2,1)S(1)}, u32[]{:S(2)}, u32[]{:S(2)}) collective-permute-start(bf16[4,256,256]{2,1,0:T(8,128)(2,1)S(1)} %get-tuple-element.70), channel_id=1, source_target_pairs={{8,0},{16,8},{24,16},{32,24},{40,32},{48,40},{56,48},{64,56},{72,6... | collective-permute-start | bytes 1572872 | tf_op jit(solution)/shard_map/ppermute | solution.py:339
  50.0 6.8 %copy-start = (bf16[2,1152,256]{2,1,0:T(8,128)(2,1)S(1)}, bf16[2,1152,256]{2,1,0:T(8,128)(2,1)}, u32[]{:S(2)}) copy-start(bf16[2,1152,256]{2,1,0:T(8,128)(2,1)} %get-tuple-element.77.total) | copy-start | bytes 3538948
  50.0 6.8 %copy-start.3 = (bf16[2,2,256,256]{3,2,1,0:T(8,128)(2,1)S(1)}, bf16[2,2,256,256]{3,2,1,0:T(8,128)(2,1)}, u32[]{:S(2)}) copy-start(bf16[2,2,256,256]{3,2,1,0:T(8,128)(2,1)} %get-tuple-element.78.kept) | copy-start | bytes 1572868
  53.1 10.1 %collective-permute-start.6 = (bf16[2,2,144,256]{3,2,1,0:T(8,128)(2,1)S(1)}, bf16[2,2,144,256]{3,2,1,0:T(8,128)(2,1)S(1)}, u32[]{:S(2)}, u32[]{:S(2)}) collective-permute-start(bf16[2,2,144,256]{3,2,1,0:T(8,128)(2,1)S(1)} %get-tuple-element.83), channel_id=1, source_target_pairs={{0,2},{2,0},{4,6},{6,4},{1,3},{3,1},{5,7},{7,5},{8,10},{10,8},{12,... | collective-permute-start | bytes 884744 | tf_op jit(solution)/shard_map/ppermute | solution.py:401
  54.7 11.1 %collective-permute-start.7 = (bf16[2,2,144,256]{3,2,1,0:T(8,128)(2,1)S(1)}, bf16[2,2,144,256]{3,2,1,0:T(8,128)(2,1)S(1)}, u32[]{:S(2)}, u32[]{:S(2)}) collective-permute-start(bf16[2,2,144,256]{3,2,1,0:T(8,128)(2,1)S(1)} %get-tuple-element.84), channel_id=1, source_target_pairs={{0,6},{2,4},{4,2},{6,0},{1,7},{3,5},{5,3},{7,1},{8,14},{10,12},{12... | collective-permute-start | bytes 884744 | tf_op jit(solution)/shard_map/ppermute | solution.py:401
  59.6 9.3 %collective-permute-start.10 = (bf16[2,2,144,256]{3,2,1,0:T(8,128)(2,1)S(1)}, bf16[2,2,144,256]{3,2,1,0:T(8,128)(2,1)S(1)}, u32[]{:S(2)}, u32[]{:S(2)}) collective-permute-start(bf16[2,2,144,256]{3,2,1,0:T(8,128)(2,1)S(1)} %get-tuple-element.89), channel_id=1, source_target_pairs={{0,2},{2,0},{4,6},{6,4},{1,3},{3,1},{5,7},{7,5},{8,10},{10,8},{12,... | collective-permute-start | bytes 884744 | tf_op jit(solution)/shard_map/ppermute | solution.py:401
  61.1 11.2 %collective-permute-start.11 = (bf16[2,2,144,256]{3,2,1,0:T(8,128)(2,1)S(1)}, bf16[2,2,144,256]{3,2,1,0:T(8,128)(2,1)S(1)}, u32[]{:S(2)}, u32[]{:S(2)}) collective-permute-start(bf16[2,2,144,256]{3,2,1,0:T(8,128)(2,1)S(1)} %get-tuple-element.90), channel_id=1, source_target_pairs={{0,6},{2,4},{4,2},{6,0},{1,7},{3,5},{5,3},{7,1},{8,14},{10,12},{12... | collective-permute-start | bytes 884744 | tf_op jit(solution)/shard_map/ppermute | solution.py:401
  65.8 8.7 %collective-permute-start.8 = (bf16[2,144,256]{2,1,0:T(8,128)(2,1)S(1)}, bf16[2,144,256]{2,1,0:T(8,128)(2,1)S(1)}, u32[]{:S(2)}, u32[]{:S(2)}) collective-permute-start(bf16[2,144,256]{2,1,0:T(8,128)(2,1)S(1)} %get-tuple-element.86), channel_id=1, source_target_pairs={{0,6},{2,4},{4,2},{6,0},{1,7},{3,5},{5,3},{7,1},{8,14},{10,12},{12... | collective-permute-start | bytes 442376 | tf_op jit(solution)/shard_map/ppermute | solution.py:415
  68.0 6.5 %collective-permute-start.9 = (bf16[2,144,256]{2,1,0:T(8,128)(2,1)S(1)}, bf16[2,144,256]{2,1,0:T(8,128)(2,1)S(1)}, u32[]{:S(2)}, u32[]{:S(2)}) collective-permute-start(bf16[2,144,256]{2,1,0:T(8,128)(2,1)S(1)} %get-tuple-element.87), channel_id=1, source_target_pairs={{0,2},{2,0},{4,6},{6,4},{1,3},{3,1},{5,7},{7,5},{8,10},{10,8},{12,... | collective-permute-start | bytes 442376 | tf_op jit(solution)/shard_map/ppermute | solution.py:415
  72.3 6.9 %collective-permute-start.12 = (bf16[2,144,256]{2,1,0:T(8,128)(2,1)S(1)}, bf16[2,144,256]{2,1,0:T(8,128)(2,1)S(1)}, u32[]{:S(2)}, u32[]{:S(2)}) collective-permute-start(bf16[2,144,256]{2,1,0:T(8,128)(2,1)S(1)} %get-tuple-element.94), channel_id=1, source_target_pairs={{0,6},{2,4},{4,2},{6,0},{1,7},{3,5},{5,3},{7,1},{8,14},{10,12},{12... | collective-permute-start | bytes 442376 | tf_op jit(solution)/shard_map/ppermute | solution.py:415
  74.5 5.1 %collective-permute-start.13 = (bf16[2,144,256]{2,1,0:T(8,128)(2,1)S(1)}, bf16[2,144,256]{2,1,0:T(8,128)(2,1)S(1)}, u32[]{:S(2)}, u32[]{:S(2)}) collective-permute-start(bf16[2,144,256]{2,1,0:T(8,128)(2,1)S(1)} %get-tuple-element.95), channel_id=1, source_target_pairs={{0,2},{2,0},{4,6},{6,4},{1,3},{3,1},{5,7},{7,5},{8,10},{10,8},{12,... | collective-permute-start | bytes 442376 | tf_op jit(solution)/shard_map/ppermute | solution.py:415
  74.6 13.5 %collective-permute-start.14 = (bf16[2,144,256]{2,1,0:T(8,128)(2,1)S(1)}, bf16[2,144,256]{2,1,0:T(8,128)(2,1)S(1)}, u32[]{:S(2)}, u32[]{:S(2)}) collective-permute-start(bf16[2,144,256]{2,1,0:T(8,128)(2,1)S(1)} %get-tuple-element.98), channel_id=1, source_target_pairs={{0,1},{1,0},{2,3},{3,2},{4,5},{5,4},{6,7},{7,6},{8,9},{9,8},{10,11... | collective-permute-start | bytes 442376 | tf_op jit(solution)/shard_map/ppermute | solution.py:426
  80.3 10.8 %collective-permute-start.15 = (bf16[2,144,256]{2,1,0:T(8,128)(2,1)S(1)}, bf16[2,144,256]{2,1,0:T(8,128)(2,1)S(1)}, u32[]{:S(2)}, u32[]{:S(2)}) collective-permute-start(bf16[2,144,256]{2,1,0:T(8,128)(2,1)S(1)} %get-tuple-element.99), channel_id=1, source_target_pairs={{0,1},{1,0},{2,3},{3,2},{4,5},{5,4},{6,7},{7,6},{8,9},{9,8},{10,11... | collective-permute-start | bytes 442376 | tf_op jit(solution)/shard_map/ppermute | solution.py:426

commit v3 on v2

--- a/solution.py
+++ b/solution.py
@@ -135,8 +135,10 @@
         )
 
 
-def take_state(places, tick, half, width, received, top, made, sem):
-    @pl.when(places[0] == 1)
+def take_state(tick, half, width, received, top, made, sem):
+    is_top = lax.axis_index("section") == lax.axis_size("section") - 1
+
+    @pl.when(is_top)
     def _():
         copy = pltpu.make_async_copy(
             top.at[tick - 1, :, :, pl.ds(half * width, width)], made, sem
@@ -144,59 +146,67 @@
         copy.start()
         copy.wait()
 
-    @pl.when(places[0] == 0)
+    @pl.when(jnp.logical_not(is_top))
     def _():
         made[...] = received[...]
 
 
-def kernel_loads(half, width, kernels, held, sems):
-    copies = {}
-    for branch in (1, 0):
-        for group in range(width // GW):
-            wide = pl.ds(half * width + group * GW, GW)
-            copies[group, branch] = pltpu.make_async_copy(
-                kernels.at[branch, :, wide],
-                held.at[branch, :, group_lanes(group)],
-                sems.at[branch, group],
-            )
-            copies[group, branch].start()
-    return copies
+def started(*copies):
+    for copy in copies:
+        copy.start()
+    return list(copies)
 
 
 def early_tick(tick, half, width, *refs):
     groups = width // GW
-    if (tick, half) == (0, 0):
-        states, kernels, earlier, *refs = refs
-    elif tick == 0:
-        states, kernels, held, earlier, *refs = refs
+    made, kept, turn, following = None, None, None, None
+    loads, outgoing = {}, []
+    if tick == 0:
+        if half == 0:
+            states, kernels, earlier, made, kept, turn, following, stored, *refs = refs
+            sent, next_sems, out_sems, state_sem, stored_sems, held, sems = refs
+        else:
+            states, kernels, held, store_next, earlier, made, kept, turn, following, stored, *refs = refs
+            sent, next_sems, out_sems, state_sem, stored_sems = refs
+        wide = pl.ds(half * width, width)
+        (state_load,) = started(pltpu.make_async_copy(states.at[:, :, wide], made, state_sem))
+        if half == 0:
+            for branch in (1, 0):
+                (loads[branch],) = started(
+                    pltpu.make_async_copy(
+                        kernels.at[branch, :, wide], held.at[branch], sems.at[branch]
+                    )
+                )
+            later = pl.ds(width, width)
+            sources = [kernels.at[branch, :, later] for branch in range(2)]
+        else:
+            sources = [store_next.at[branch] for branch in range(2)]
+            for branch in (1, 0):
+                outgoing += started(
+                    pltpu.make_async_copy(held.at[branch], stored.at[branch], stored_sems.at[branch])
+                )
     else:
-        places, received, top, kernels, held, earlier, *refs = refs
-    made, kept, turn, following, sent, next_sems, out_sems, *refs = refs
-    loads = {}
-    if tick == 0:
-        state_sems, *refs = refs
-        for group in range(groups):
-            wide = pl.ds(half * width + group * GW, GW)
-            loads[group] = pltpu.make_async_copy(
-                states.at[:, :, wide], made.at[:, :, group_lanes(group)], state_sems.at[group]
-            )
-            loads[group].start()
-    if (tick, half) == (0, 0):
-        held, sems = refs
-        loads.update(kernel_loads(half, width, kernels, held, sems))
-    outgoing = list(
-        kernel_loads((half + 1) % HALVES, width, kernels, following, next_sems).values()
-    )
+        received, top, store_next, held, earlier, made, kept, turn, following, *refs = refs
+        sent, next_sems, out_sems, top_sem = refs
+        sources = [store_next.at[branch] for branch in range(2)]
+    for branch in (1, 0):
+        outgoing += started(
+            pltpu.make_async_copy(sources[branch], following.at[branch], next_sems.at[branch])
+        )
     turn[...] = jnp.zeros_like(turn)
     if tick:
-        take_state(places, tick, half, width, received, top, made, refs[0])
+        take_state(tick, half, width, received, top, made, top_sem)
     else:
-        for group in range(groups):
-            loads[group].wait()
+        state_load.wait()
 
     def weights(group, branch):
-        if (group, branch) in loads:
-            loads[group, branch].wait()
+        if group == 0 and branch in loads:
+            loads[branch].wait()
+            outgoing.extend(
+                started(
+                    pltpu.make_async_copy(held.at[branch], stored.at[branch], stored_sems.at[branch])
+                )
+            )
         return taps_by_row(held, branch, group_lanes(group))
 
     def keep(group, branch, columns, rows):
@@ -204,9 +214,9 @@
         sent[branch, 0, :, lanes] = columns[:, GW : 2 * GW]
         sent[branch, 1, :, lanes] = rows[:, GW : 2 * GW]
         if group == groups - 1:
-            copy = pltpu.make_async_copy(sent.at[branch], kept.at[branch], out_sems.at[branch])
-            copy.start()
-            outgoing.append(copy)
+            outgoing.extend(
+                started(pltpu.make_async_copy(sent.at[branch], kept.at[branch], out_sems.at[branch]))
+            )
 
     section_back(made, groups, weights, keep)
     for copy in outgoing:
@@ -254,7 +264,7 @@
         copy.wait()
 
 
-def last_tick(half, width, places, received, top, kernels, held, total, kept, earlier, *rest):
+def last_tick(half, width, received, top, store_next, held, total, kept, earlier, *rest):
     if half:
         rest = rest[1:]
     made, final, mine, *rest = rest
@@ -264,11 +274,16 @@
     turn, *rest = rest
     if half + 1 < HALVES:
         following, summed, top_sem, final_sem, next_sems = rest
-        copies.extend(kernel_loads(half + 1, width, kernels, following, next_sems).values())
+        for branch in (1, 0):
+            copies += started(
+                pltpu.make_async_copy(
+                    store_next.at[branch], following.at[branch], next_sems.at[branch]
+                )
+            )
     else:
         summed, top_sem, final_sem = rest
     turn[...] = jnp.zeros_like(turn)
-    take_state(places, TICKS - 1, half, width, received, top, made, top_sem)
+    take_state(TICKS - 1, half, width, received, top, made, top_sem)
     stacks = {}
 
     def weights(group, branch):
@@ -282,6 +297,7 @@
     copy.start()
     copies.append(copy)
     edges = masks()
+    z = lax.axis_index("dp_1")
     for branch in range(2):
         for group in range(groups):
             lanes = group_lanes(group)
@@ -296,10 +312,10 @@
                 summed[branch, at, lanes] = (
                     total[branch, at, lanes].astype(jnp.float32) + term[:, a * GW : (a + 1) * GW]
                 ).astype(jnp.bfloat16)
-        for slot in range(4):
+        for slot, block in enumerate(share_blocks(branch)):
             for z_slot in range(2):
-                block = pl.multiple_of(places[1 + 4 * branch + slot] + places[9 + z_slot], 16)
-                share = summed[branch, pl.ds(block, SHARE), :]
+                first = pl.multiple_of((2 * block + (z ^ z_slot)) * SHARE, 16)
+                share = summed[branch, pl.ds(first, SHARE), :]
                 if slot < 2:
                     mine[branch, slot, z_slot] = share
                 else:
@@ -310,7 +326,6 @@
 
 ANY_REF = pl.BlockSpec(memory_space=pl.ANY)
 VMEM_REF = pl.BlockSpec(memory_space=pltpu.VMEM)
-SMEM_REF = pl.BlockSpec(memory_space=pltpu.SMEM)
 
 
 def in_vmem(array):
@@ -343,15 +358,10 @@
     return (x ^ 1, 3 - x) if branch == 0 else (3 - x, x ^ 1)
 
 
-def share_places():
-    x, z = lax.axis_index("dp_0"), lax.axis_index("dp_1")
-    is_top = lax.axis_index("section") == lax.axis_size("section") - 1
-    numbers = [is_top]
-    for branch in range(2):
-        first, second = partners(branch, x)
-        numbers += [at * (2 * SHARE) for at in (x, second, first, partners(branch, first)[1])]
-    numbers += [z * SHARE, (1 - z) * SHARE]
-    return jnp.stack([number.astype(jnp.int32) for number in numbers])
+def share_blocks(branch):
+    x = lax.axis_index("dp_0")
+    first, second = partners(branch, x)
+    return x, second, first, partners(branch, first)[1]
 
 
 def first_sum(mine, *refs):
@@ -441,7 +451,6 @@
     states = in_hbm(section_states.reshape(4, CELLS, chans))
     kernels = in_hbm(conv_kernels[0])
     top = in_hbm(top_feed.reshape(TICKS - 1, 4, CELLS, chans))
-    places = share_places()
 
     groups = width // GW
     state_type = pltpu.VMEM((4, CELLS, width), jnp.bfloat16)
@@ -451,37 +460,11 @@
     dma = pltpu.SemaphoreType.DMA
     kept_scratch = pltpu.VMEM((2, 2, CELLS, width), jnp.bfloat16)
     turn = jnp.zeros((8, 128), jnp.float32)
-    held = None
+    held, stored = None, []
+    stored_type = pltpu.HBM((2, ROWS, width), jnp.bfloat16)
     made, kept = [None] * HALVES, [[] for _ in range(HALVES)]
     for tick in range(TICKS - 1):
         for half in range(HALVES):
-            aliases = {}
-            scratch = [kept_scratch, dma((2, groups)), dma((2,))]
-            if tick:
-                operands = [places, in_vmem(made[half]), top, kernels, held, turn]
-                specs = [SMEM_REF, VMEM_REF, ANY_REF, ANY_REF, VMEM_REF, ANY_REF]
-                aliases = {1: 0}
-                scratch += [dma(())]
-            elif half:
-                operands, specs = [states, kernels, held, turn], [ANY_REF, ANY_REF, VMEM_REF, ANY_REF]
-                scratch += [dma((groups,))]
-            else:
-                operands, specs = [states, kernels, turn], [ANY_REF] * 3
-                scratch += [dma((groups,)), held_type, dma((2, groups))]
-            out, fields, turn, following = pl.pallas_call(
-                functools.partial(early_tick, tick, half, width),
-                out_shape=(state_type, kept_type, turn_type, held_type),
-                in_specs=specs,
-                out_specs=(VMEM_REF, ANY_REF, VMEM_REF, VMEM_REF),
-                scratch_shapes=scratch,
-                input_output_aliases=aliases,
-                compiler_params=params(),
-                cost_estimate=cost(4, width),
-                name=f"tick_{tick}_{half}",
-            )(*operands)
-            held = in_vmem(following)
-            made[half] = passed_down(out)
-            kept[half].append(fields)
             if (tick, half) == (FIRST, 0):
                 *total, turn = pl.pallas_call(
                     functools.partial(early_terms, width),
@@ -500,15 +483,48 @@
                     compiler_params=params(),
                     cost_estimate=cost(2 * FIRST * HALVES, width),
                     name="early_terms",
-                )(*[in_hbm(plane) for side in kept for plane in side[:FIRST]], turn)
+                )(*[in_hbm(plane) for side in kept for plane in side], turn)
+            aliases = {}
+            outs = [state_type, kept_type, turn_type, held_type]
+            out_specs = [VMEM_REF, ANY_REF, VMEM_REF, VMEM_REF]
+            scratch = [kept_scratch, dma((2,)), dma((2,)), dma(())]
+            if tick:
+                operands = [in_vmem(made[half]), top, stored[1 - half], held, turn]
+                specs = [VMEM_REF, ANY_REF, ANY_REF, VMEM_REF, ANY_REF]
+                aliases = {0: 0}
+            else:
+                outs.append(stored_type)
+                out_specs.append(ANY_REF)
+                scratch.append(dma((2,)))
+                if half:
+                    operands = [states, kernels, held, stored[0], turn]
+                    specs = [ANY_REF, ANY_REF, VMEM_REF, ANY_REF, ANY_REF]
+                else:
+                    operands, specs = [states, kernels, turn], [ANY_REF] * 3
+                    scratch += [held_type, dma((2,))]
+            out, fields, turn, following, *rest = pl.pallas_call(
+                functools.partial(early_tick, tick, half, width),
+                out_shape=tuple(outs),
+                in_specs=specs,
+                out_specs=tuple(out_specs),
+                scratch_shapes=scratch,
+                input_output_aliases=aliases,
+                compiler_params=params(),
+                cost_estimate=cost(4, width),
+                name=f"tick_{tick}_{half}",
+            )(*operands)
+            stored += [in_hbm(copy) for copy in rest]
+            held = in_vmem(following)
+            made[half] = passed_down(out)
+            kept[half].append(fields)
 
     final = None
     mine, theirs = [None] * HALVES, [None] * HALVES
     theirs_type = pltpu.VMEM((2, 2, SHARE, width), jnp.bfloat16)
     for half in range(HALVES):
-        operands = [places, in_vmem(made[half]), top, kernels, held, total[half], kept[half][FIRST], turn]
-        specs = [SMEM_REF, VMEM_REF, ANY_REF, ANY_REF, VMEM_REF, VMEM_REF, VMEM_REF, ANY_REF]
-        aliases = {1: 0}
+        operands = [in_vmem(made[half]), top, stored[1], held, total[half], kept[half][FIRST], turn]
+        specs = [VMEM_REF, ANY_REF, ANY_REF, VMEM_REF, VMEM_REF, VMEM_REF, ANY_REF]
+        aliases = {0: 0}
         if half:
             aliases[len(operands)] = 1
             operands.append(in_hbm(final))
@@ -531,7 +547,7 @@
                 pltpu.VMEM((2, ROWS, width), jnp.bfloat16),
                 dma(()),
                 dma(()),
-                *[dma((2, groups))] * more,
+                *[dma((2,))] * more,
             ],
             input_output_aliases=aliases,
             compiler_params=params(),

time: 92.4 us -> 88.7 us (0.960)
  Pallas kernels: 27.5 us -> 24.1 us
    pallas_call x6, Pallas kernels: 15.5 us -> 13.3 us  [on_device(): pl.pallas_call(functools.partial(early_tick, tick, half, width), out_shap...]
    pallas_call x2, Pallas kernels: 5.86 us -> 4.81 us  [on_device(): pl.pallas_call(functools.partial(last_tick, half, width), out_shape=(stat...]
    ppermute x2, waiting for transfers between devices: 6.32 us -> 7.32 us  [summed_shares(): came_last.append(lax.ppermute(across, 'dp_1', [(0, 1), (1, 0)]))]
  transfers between devices with their start and end apart: 16 -> 16, of which waited for: 8 -> 8; matrix products, arithmetic and copies ran while one was open for 0% -> 0% of each run, Pallas kernels for 24% -> 22%
where the time goes in v3:
time: 88.7 us; the launch traced here: 88.3 us
  starting transfers between devices  46.9 us (53%)
  Pallas kernels  24.1 us (27%)
  waiting for transfers between devices  16.3 us (18%)
    ppermute x6, starting transfers between devices, passed_down(): lax.ppermute(value, 'section', [(source, source - 1) for source in range(...  26.6 us
    pallas_call x6, Pallas kernels, on_device(): pl.pallas_call(functools.partial(early_tick, tick, half, width), out_shap...  13.3 us
    ppermute x2, starting transfers between devices, summed_shares(): came_last.append(lax.ppermute(across, 'dp_1', [(0, 1), (1, 0)]))  9.06 us
    ppermute x2, waiting for transfers between devices, summed_shares(): came_last.append(lax.ppermute(across, 'dp_1', [(0, 1), (1, 0)]))  7.32 us
    ppermute x4, starting transfers between devices, summed_shares(): lax.ppermute(theirs[half][b], 'dp_0', pairs[b][0])  6.92 us
    ppermute x4, waiting for transfers between devices, summed_shares(): lax.ppermute(theirs[half][b], 'dp_0', pairs[b][0])  6.8 us
    pallas_call x2, Pallas kernels, on_device(): pl.pallas_call(functools.partial(last_tick, half, width), out_shape=(stat...  4.81 us
    ppermute x4, starting transfers between devices, summed_shares(): lax.ppermute(passed[b], 'dp_0', pairs[b][1])  4.37 us
  transfers between devices with their start and end apart: 16, of which 8 were waited for; matrix products, arithmetic and copies ran while one was open for 0% of the time, Pallas kernels for 22%

profile of v3, /device:TPU:24, one launch (start us, length us, event | category | flops | bytes accessed | tf_op | source)
XLA Modules:
  0.0 88.3 jit_solution(11804020357185527249)
XLA Ops:
  0.6 3.6 %tick_0_0.1 = (bf16[4,256,256]{2,1,0:T(8,128)(2,1)S(1)}, bf16[2,2,256,256]{3,2,1,0:T(8,128)(2,1)}, f32[8,128]{1,0:T(8,128)S(1)}, bf16[2,1152,256]{2,1,0:T(8,128)(2,1)S(1)}, bf16[2,1152,256]{2,1,0:T(8,128)(2,1)}) custom-call(bf16[4,256,512]{2,1,0:T(8,128)(2,1)} %bitcast.15, bf16[2,1152,512]{2,1,0:T(8,128)(2,1)} %bitcast.13, f32[8,128]{1,0:T(8,128)S(1)} %broadcast_in_dim.6.refs_2_), custom_call_target="tpu_custom_call" | custom-call | flops 603979776 | bytes 1048576 | tf_op jit(solution)/shard_map/tick_0_0/pallas_call | solution.py:505
  4.3 6.2 %collective-permute-start.1 = (bf16[4,256,256]{2,1,0:T(8,128)(2,1)S(1)}, bf16[4,256,256]{2,1,0:T(8,128)(2,1)S(1)}, u32[]{:S(2)}, u32[]{:S(2)}) collective-permute-start(bf16[4,256,256]{2,1,0:T(8,128)(2,1)S(1)} %get-tuple-element.57), channel_id=1, source_target_pairs={{8,0},{16,8},{24,16},{32,24},{40,32},{48,40},{56,48},{64,56},{72,6... | collective-permute-start | bytes 1572872 | tf_op jit(solution)/shard_map/ppermute | solution.py:354
  10.4 3.2 %tick_0_1.1 = (bf16[4,256,256]{2,1,0:T(8,128)(2,1)S(1)}, bf16[2,2,256,256]{3,2,1,0:T(8,128)(2,1)}, f32[8,128]{1,0:T(8,128)S(1)}, bf16[2,1152,256]{2,1,0:T(8,128)(2,1)S(1)}, bf16[2,1152,256]{2,1,0:T(8,128)(2,1)}) custom-call(bf16[4,256,512]{2,1,0:T(8,128)(2,1)} %bitcast.16, bf16[2,1152,512]{2,1,0:T(8,128)(2,1)} %bitcast.14, ...), custom_call_target="tpu_custom_call" | custom-call | flops 603979776 | bytes 1048576 | tf_op jit(solution)/shard_map/tick_0_1/pallas_call | solution.py:505
  13.6 2.6 %collective-permute-start = (bf16[4,256,256]{2,1,0:T(8,128)(2,1)S(1)}, bf16[4,256,256]{2,1,0:T(8,128)(2,1)S(1)}, u32[]{:S(2)}, u32[]{:S(2)}) collective-permute-start(bf16[4,256,256]{2,1,0:T(8,128)(2,1)S(1)} %get-tuple-element.56), channel_id=1, source_target_pairs={{8,0},{16,8},{24,16},{32,24},{40,32},{48,40},{56,48},{64,56},{72,6... | collective-permute-start | bytes 1572872 | tf_op jit(solution)/shard_map/ppermute | solution.py:354
  16.2 0.9 collective-permute-done.1.refs_0_
  17.1 1.6 %tick_1_0.1 = (bf16[4,256,256]{2,1,0:T(8,128)(2,1)S(1)}, bf16[2,2,256,256]{3,2,1,0:T(8,128)(2,1)}, f32[8,128]{1,0:T(8,128)S(1)}, bf16[2,1152,256]{2,1,0:T(8,128)(2,1)S(1)}) custom-call(bf16[4,256,256]{2,1,0:T(8,128)(2,1)S(1)} %collective-permute-done.1.refs_0_, bf16[3,4,256,512]{3,2,1,0:T(8,128)(2,1)} %bitcast.7, ...), custom_call_target="tpu_custom_call", output_to_operand_aliasing={{0}: (0, {})} | custom-call | flops 603979776 | bytes 1048576 | tf_op jit(solution)/shard_map/tick_1_0/pallas_call | solution.py:505
  18.7 6.5 %collective-permute-start.3 = (bf16[4,256,256]{2,1,0:T(8,128)(2,1)S(1)}, bf16[4,256,256]{2,1,0:T(8,128)(2,1)S(1)}, u32[]{:S(2)}, u32[]{:S(2)}) collective-permute-start(bf16[4,256,256]{2,1,0:T(8,128)(2,1)S(1)} %get-tuple-element.64), channel_id=1, source_target_pairs={{8,0},{16,8},{24,16},{32,24},{40,32},{48,40},{56,48},{64,56},{72,6... | collective-permute-start | bytes 1572872 | tf_op jit(solution)/shard_map/ppermute | solution.py:354
  25.2 0.0 collective-permute-done.refs_0_
  25.2 1.6 %tick_1_1.1 = (bf16[4,256,256]{2,1,0:T(8,128)(2,1)S(1)}, bf16[2,2,256,256]{3,2,1,0:T(8,128)(2,1)}, f32[8,128]{1,0:T(8,128)S(1)}, bf16[2,1152,256]{2,1,0:T(8,128)(2,1)S(1)}) custom-call(bf16[4,256,256]{2,1,0:T(8,128)(2,1)S(1)} %collective-permute-done.refs_0_, bf16[3,4,256,512]{3,2,1,0:T(8,128)(2,1)} %bitcast.8, ...), custom_call_target="tpu_custom_call", output_to_operand_aliasing={{0}: (0, {})} | custom-call | flops 603979776 | bytes 1048576 | tf_op jit(solution)/shard_map/tick_1_1/pallas_call | solution.py:505
  26.9 4.1 %collective-permute-start.2 = (bf16[4,256,256]{2,1,0:T(8,128)(2,1)S(1)}, bf16[4,256,256]{2,1,0:T(8,128)(2,1)S(1)}, u32[]{:S(2)}, u32[]{:S(2)}) collective-permute-start(bf16[4,256,256]{2,1,0:T(8,128)(2,1)S(1)} %get-tuple-element.63), channel_id=1, source_target_pairs={{8,0},{16,8},{24,16},{32,24},{40,32},{48,40},{56,48},{64,56},{72,6... | collective-permute-start | bytes 1572872 | tf_op jit(solution)/shard_map/ppermute | solution.py:354
  31.0 4.3 %early_terms.1 = (bf16[2,1152,256]{2,1,0:T(8,128)(2,1)}, bf16[2,1152,256]{2,1,0:T(8,128)(2,1)}, f32[8,128]{1,0:T(8,128)S(1)}) custom-call(bf16[2,2,256,256]{3,2,1,0:T(8,128)(2,1)} %get-tuple-element.66.refs_0_, bf16[2,2,256,256]{3,2,1,0:T(8,128)(2,1)} %get-tuple-element.67.refs_1_, bf16[2,2,256,256]{3,2,1,0:T(8,128)(2,1)} %get-tuple-element.68.refs_2_, ...), custom_call_target="tpu_custom_call" | custom-call | flops 1207959552 | bytes 1048576 | tf_op jit(solution)/shard_map/early_terms/pallas_call | solution.py:469
  35.3 0.0 collective-permute-done.3.refs_0_
  35.3 1.6 %tick_2_0.1 = (bf16[4,256,256]{2,1,0:T(8,128)(2,1)S(1)}, bf16[2,2,256,256]{3,2,1,0:T(8,128)(2,1)}, f32[8,128]{1,0:T(8,128)S(1)}, bf16[2,1152,256]{2,1,0:T(8,128)(2,1)S(1)}) custom-call(bf16[4,256,256]{2,1,0:T(8,128)(2,1)S(1)} %collective-permute-done.3.refs_0_, bf16[3,4,256,512]{3,2,1,0:T(8,128)(2,1)} %bitcast.9, ...), custom_call_target="tpu_custom_call", output_to_operand_aliasing={{0}: (0, {})} | custom-call | flops 603979776 | bytes 1048576 | tf_op jit(solution)/shard_map/tick_2_0/pallas_call | solution.py:505
  36.9 3.1 %collective-permute-start.5 = (bf16[4,256,256]{2,1,0:T(8,128)(2,1)S(1)}, bf16[4,256,256]{2,1,0:T(8,128)(2,1)S(1)}, u32[]{:S(2)}, u32[]{:S(2)}) collective-permute-start(bf16[4,256,256]{2,1,0:T(8,128)(2,1)S(1)} %get-tuple-element.75), channel_id=1, source_target_pairs={{8,0},{16,8},{24,16},{32,24},{40,32},{48,40},{56,48},{64,56},{72,6... | collective-permute-start | bytes 1572872 | tf_op jit(solution)/shard_map/ppermute | solution.py:354
  40.0 0.0 collective-permute-done.2.refs_0_
  40.0 0.0 copy-start
  40.1 0.0 copy-start.2
  40.1 1.6 %tick_2_1.1 = (bf16[4,256,256]{2,1,0:T(8,128)(2,1)S(1)}, bf16[2,2,256,256]{3,2,1,0:T(8,128)(2,1)}, f32[8,128]{1,0:T(8,128)S(1)}, bf16[2,1152,256]{2,1,0:T(8,128)(2,1)S(1)}) custom-call(bf16[4,256,256]{2,1,0:T(8,128)(2,1)S(1)} %collective-permute-done.2.refs_0_, bf16[3,4,256,512]{3,2,1,0:T(8,128)(2,1)} %bitcast.10, ...), custom_call_target="tpu_custom_call", output_to_operand_aliasing={{0}: (0, {})} | custom-call | flops 603979776 | bytes 1048576 | tf_op jit(solution)/shard_map/tick_2_1/pallas_call | solution.py:505
  41.7 4.1 %collective-permute-start.4 = (bf16[4,256,256]{2,1,0:T(8,128)(2,1)S(1)}, bf16[4,256,256]{2,1,0:T(8,128)(2,1)S(1)}, u32[]{:S(2)}, u32[]{:S(2)}) collective-permute-start(bf16[4,256,256]{2,1,0:T(8,128)(2,1)S(1)} %get-tuple-element.74), channel_id=1, source_target_pairs={{8,0},{16,8},{24,16},{32,24},{40,32},{48,40},{56,48},{64,56},{72,6... | collective-permute-start | bytes 1572872 | tf_op jit(solution)/shard_map/ppermute | solution.py:354
  45.8 0.9 collective-permute-done.5.received
  46.7 0.0 copy-done
  46.7 0.0 copy-done.2
  46.7 0.0 copy-start.1
  46.7 0.0 copy-start.3
  46.7 2.5 %last_tick_0.1 = (bf16[4,256,256]{2,1,0:T(8,128)(2,1)S(1)}, bf16[4,256,512]{2,1,0:T(8,128)(2,1)}, bf16[2,2,2,144,256]{4,3,2,1,0:T(8,128)(2,1)S(1)}, bf16[2,2,144...) custom-call(bf16[4,256,256]{2,1,0:T(8,128)(2,1)S(1)} %collective-per, ...), custom_call_target="tpu_custom_call", output_to_operand_aliasing={{0}: (0, {})} | custom-call | flops 905969664 | bytes 1048576 | tf_op jit(solution)/shard_map/last_tick_0/pallas_call | solution.py:533
  49.3 1.6 %collective-permute-start.6 = (bf16[2,2,144,256]{3,2,1,0:T(8,128)(2,1)S(1)}, bf16[2,2,144,256]{3,2,1,0:T(8,128)(2,1)S(1)}, u32[]{:S(2)}, u32[]{:S(2)}) collective-permute-start(bf16[2,2,144,256]{3,2,1,0:T(8,128)(2,1)S(1)} %get-tuple-element.87), channel_id=1, source_target_pairs={{0,2},{2,0},{4,6},{6,4},{1,3},{3,1},{5,7},{7,5},{8,10},{10,8},{12,... | collective-permute-start | bytes 884744 | tf_op jit(solution)/shard_map/ppermute | solution.py:411
  50.8 2.1 %collective-permute-start.7 = (bf16[2,2,144,256]{3,2,1,0:T(8,128)(2,1)S(1)}, bf16[2,2,144,256]{3,2,1,0:T(8,128)(2,1)S(1)}, u32[]{:S(2)}, u32[]{:S(2)}) collective-permute-start(bf16[2,2,144,256]{3,2,1,0:T(8,128)(2,1)S(1)} %get-tuple-element.88), channel_id=1, source_target_pairs={{0,6},{2,4},{4,2},{6,0},{1,7},{3,5},{5,3},{7,1},{8,14},{10,12},{12... | collective-permute-start | bytes 884744 | tf_op jit(solution)/shard_map/ppermute | solution.py:411
  52.9 0.0 collective-permute-done.4.received
  52.9 0.0 copy-done.1
  52.9 0.0 copy-done.3
  52.9 2.3 %last_tick_1.1 = (bf16[4,256,256]{2,1,0:T(8,128)(2,1)S(1)}, bf16[4,256,512]{2,1,0:T(8,128)(2,1)}, bf16[2,2,2,144,256]{4,3,2,1,0:T(8,128)(2,1)S(1)}, bf16[2,2,144...) custom-call(bf16[4,256,256]{2,1,0:T(8,128)(2,1)S(1)} %collective-per, ...), custom_call_target="tpu_custom_call", output_to_operand_aliasing={{0}: (0, {}), {1}: (7, {})} | custom-call | flops 905969664 | bytes 1048576 | tf_op jit(solution)/shard_map/last_tick_1/pallas_call | solution.py:533
  55.2 1.1 %collective-permute-start.10 = (bf16[2,2,144,256]{3,2,1,0:T(8,128)(2,1)S(1)}, bf16[2,2,144,256]{3,2,1,0:T(8,128)(2,1)S(1)}, u32[]{:S(2)}, u32[]{:S(2)}) collective-permute-start(bf16[2,2,144,256]{3,2,1,0:T(8,128)(2,1)S(1)} %get-tuple-element.93), channel_id=1, source_target_pairs={{0,2},{2,0},{4,6},{6,4},{1,3},{3,1},{5,7},{7,5},{8,10},{10,8},{12,... | collective-permute-start | bytes 884744 | tf_op jit(solution)/shard_map/ppermute | solution.py:411
  56.4 2.1 %collective-permute-start.11 = (bf16[2,2,144,256]{3,2,1,0:T(8,128)(2,1)S(1)}, bf16[2,2,144,256]{3,2,1,0:T(8,128)(2,1)S(1)}, u32[]{:S(2)}, u32[]{:S(2)}) collective-permute-start(bf16[2,2,144,256]{3,2,1,0:T(8,128)(2,1)S(1)} %get-tuple-element.94), channel_id=1, source_target_pairs={{0,6},{2,4},{4,2},{6,0},{1,7},{3,5},{5,3},{7,1},{8,14},{10,12},{12... | collective-permute-start | bytes 884744 | tf_op jit(solution)/shard_map/ppermute | solution.py:411
  58.5 0.0 collective-permute-done.6.refs_0_
  58.5 1.9 %collective-permute-done.7.refs_1_ = bf16[2,2,144,256]{3,2,1,0:T(8,128)(2,1)S(1)} collective-permute-done((bf16[2,2,144,256]{3,2,1,0:T(8,128)(2,1)S(1)}, bf16[2,2,144,256]{3,2,1,0:T(8,128)(2,1)S(1)}, u32[]{:S(2)}, u32[]{:S(2)}) %collective-permute-start.7) | collective-permute-done | bytes 294944 | tf_op jit(solution)/shard_map/ppermute | solution.py:411
  60.4 0.1 first_sum_0.1
  60.5 2.2 %collective-permute-start.8 = (bf16[2,144,256]{2,1,0:T(8,128)(2,1)S(1)}, bf16[2,144,256]{2,1,0:T(8,128)(2,1)S(1)}, u32[]{:S(2)}, u32[]{:S(2)}) collective-permute-start(bf16[2,144,256]{2,1,0:T(8,128)(2,1)S(1)} %get-tuple-element.90), channel_id=1, source_target_pairs={{0,6},{2,4},{4,2},{6,0},{1,7},{3,5},{5,3},{7,1},{8,14},{10,12},{12... | collective-permute-start | bytes 442376 | tf_op jit(solution)/shard_map/ppermute | solution.py:425
  62.6 0.0 collective-permute-start.9
  62.6 2.4 %collective-permute-done.10.refs_0_ = bf16[2,2,144,256]{3,2,1,0:T(8,128)(2,1)S(1)} collective-permute-done((bf16[2,2,144,256]{3,2,1,0:T(8,128)(2,1)S(1)}, bf16[2,2,144,256]{3,2,1,0:T(8,128)(2,1)S(1)}, u32[]{:S(2)}, u32[]{:S(2)}) %collective-permute-start.10) | collective-permute-done | bytes 294944 | tf_op jit(solution)/shard_map/ppermute | solution.py:411
  65.0 2.5 %collective-permute-done.11.refs_1_ = bf16[2,2,144,256]{3,2,1,0:T(8,128)(2,1)S(1)} collective-permute-done((bf16[2,2,144,256]{3,2,1,0:T(8,128)(2,1)S(1)}, bf16[2,2,144,256]{3,2,1,0:T(8,128)(2,1)S(1)}, u32[]{:S(2)}, u32[]{:S(2)}) %collective-permute-start.11) | collective-permute-done | bytes 294944 | tf_op jit(solution)/shard_map/ppermute | solution.py:411
  67.5 0.1 first_sum_1.1
  67.6 2.2 %collective-permute-start.12 = (bf16[2,144,256]{2,1,0:T(8,128)(2,1)S(1)}, bf16[2,144,256]{2,1,0:T(8,128)(2,1)S(1)}, u32[]{:S(2)}, u32[]{:S(2)}) collective-permute-start(bf16[2,144,256]{2,1,0:T(8,128)(2,1)S(1)} %get-tuple-element.98), channel_id=1, source_target_pairs={{0,6},{2,4},{4,2},{6,0},{1,7},{3,5},{5,3},{7,1},{8,14},{10,12},{12... | collective-permute-start | bytes 442376 | tf_op jit(solution)/shard_map/ppermute | solution.py:425
  69.8 0.0 collective-permute-start.13
  69.8 0.0 collective-permute-done.8.refs_2_
  69.8 0.0 collective-permute-done.9.refs_3_
  69.8 0.1 second_sum_0.1
  69.9 4.6 %collective-permute-start.14 = (bf16[2,144,256]{2,1,0:T(8,128)(2,1)S(1)}, bf16[2,144,256]{2,1,0:T(8,128)(2,1)S(1)}, u32[]{:S(2)}, u32[]{:S(2)}) collective-permute-start(bf16[2,144,256]{2,1,0:T(8,128)(2,1)S(1)} %get-tuple-element.102), channel_id=1, source_target_pairs={{0,1},{1,0},{2,3},{3,2},{4,5},{5,4},{6,7},{7,6},{8,9},{9,8},{10,11... | collective-permute-start | bytes 442376 | tf_op jit(solution)/shard_map/ppermute | solution.py:436
  74.5 0.0 collective-permute-done.12.refs_2_
  74.5 0.4 collective-permute-done.13.refs_3_
  74.9 0.6 second_sum_1.1
  75.6 4.5 %collective-permute-start.15 = (bf16[2,144,256]{2,1,0:T(8,128)(2,1)S(1)}, bf16[2,144,256]{2,1,0:T(8,128)(2,1)S(1)}, u32[]{:S(2)}, u32[]{:S(2)}) collective-permute-start(bf16[2,144,256]{2,1,0:T(8,128)(2,1)S(1)} %get-tuple-element.103), channel_id=1, source_target_pairs={{0,1},{1,0},{2,3},{3,2},{4,5},{5,4},{6,7},{7,6},{8,9},{9,8},{10,11... | collective-permute-start | bytes 442376 | tf_op jit(solution)/shard_map/ppermute | solution.py:436
  80.1 5.0 %collective-permute-done.14.refs_2_ = bf16[2,144,256]{2,1,0:T(8,128)(2,1)S(1)} collective-permute-done((bf16[2,144,256]{2,1,0:T(8,128)(2,1)S(1)}, bf16[2,144,256]{2,1,0:T(8,128)(2,1)S(1)}, u32[]{:S(2)}, u32[]{:S(2)}) %collective-permute-start.14) | collective-permute-done | bytes 147488 | tf_op jit(solution)/shard_map/ppermute | solution.py:436
  85.1 2.3 %collective-permute-done.15.refs_3_ = bf16[2,144,256]{2,1,0:T(8,128)(2,1)S(1)} collective-permute-done((bf16[2,144,256]{2,1,0:T(8,128)(2,1)S(1)}, bf16[2,144,256]{2,1,0:T(8,128)(2,1)S(1)}, u32[]{:S(2)}, u32[]{:S(2)}) %collective-permute-start.15) | collective-permute-done | bytes 147488 | tf_op jit(solution)/shard_map/ppermute | solution.py:436
  87.4 0.9 last_sum.1
  (1 shorter events, 0.0 us)
Async XLA Ops:
  4.3 12.8 %collective-permute-start.1 = (bf16[4,256,256]{2,1,0:T(8,128)(2,1)S(1)}, bf16[4,256,256]{2,1,0:T(8,128)(2,1)S(1)}, u32[]{:S(2)}, u32[]{:S(2)}) collective-permute-start(bf16[4,256,256]{2,1,0:T(8,128)(2,1)S(1)} %get-tuple-element.57), channel_id=1, source_target_pairs={{8,0},{16,8},{24,16},{32,24},{40,32},{48,40},{56,48},{64,56},{72,6... | collective-permute-start | bytes 1572872 | tf_op jit(solution)/shard_map/ppermute | solution.py:354
  13.6 11.6 %collective-permute-start = (bf16[4,256,256]{2,1,0:T(8,128)(2,1)S(1)}, bf16[4,256,256]{2,1,0:T(8,128)(2,1)S(1)}, u32[]{:S(2)}, u32[]{:S(2)}) collective-permute-start(bf16[4,256,256]{2,1,0:T(8,128)(2,1)S(1)} %get-tuple-element.56), channel_id=1, source_target_pairs={{8,0},{16,8},{24,16},{32,24},{40,32},{48,40},{56,48},{64,56},{72,6... | collective-permute-start | bytes 1572872 | tf_op jit(solution)/shard_map/ppermute | solution.py:354
  18.7 16.6 %collective-permute-start.3 = (bf16[4,256,256]{2,1,0:T(8,128)(2,1)S(1)}, bf16[4,256,256]{2,1,0:T(8,128)(2,1)S(1)}, u32[]{:S(2)}, u32[]{:S(2)}) collective-permute-start(bf16[4,256,256]{2,1,0:T(8,128)(2,1)S(1)} %get-tuple-element.64), channel_id=1, source_target_pairs={{8,0},{16,8},{24,16},{32,24},{40,32},{48,40},{56,48},{64,56},{72,6... | collective-permute-start | bytes 1572872 | tf_op jit(solution)/shard_map/ppermute | solution.py:354
  26.9 13.2 %collective-permute-start.2 = (bf16[4,256,256]{2,1,0:T(8,128)(2,1)S(1)}, bf16[4,256,256]{2,1,0:T(8,128)(2,1)S(1)}, u32[]{:S(2)}, u32[]{:S(2)}) collective-permute-start(bf16[4,256,256]{2,1,0:T(8,128)(2,1)S(1)} %get-tuple-element.63), channel_id=1, source_target_pairs={{8,0},{16,8},{24,16},{32,24},{40,32},{48,40},{56,48},{64,56},{72,6... | collective-permute-start | bytes 1572872 | tf_op jit(solution)/shard_map/ppermute | solution.py:354
  36.9 9.8 %collective-permute-start.5 = (bf16[4,256,256]{2,1,0:T(8,128)(2,1)S(1)}, bf16[4,256,256]{2,1,0:T(8,128)(2,1)S(1)}, u32[]{:S(2)}, u32[]{:S(2)}) collective-permute-start(bf16[4,256,256]{2,1,0:T(8,128)(2,1)S(1)} %get-tuple-element.75), channel_id=1, source_target_pairs={{8,0},{16,8},{24,16},{32,24},{40,32},{48,40},{56,48},{64,56},{72,6... | collective-permute-start | bytes 1572872 | tf_op jit(solution)/shard_map/ppermute | solution.py:354
  40.0 6.7 %copy-start = (bf16[2,1152,256]{2,1,0:T(8,128)(2,1)S(1)}, bf16[2,1152,256]{2,1,0:T(8,128)(2,1)}, u32[]{:S(2)}) copy-start(bf16[2,1152,256]{2,1,0:T(8,128)(2,1)} %get-tuple-element.77.total) | copy-start | bytes 3538948
  40.1 6.7 %copy-start.2 = (bf16[2,2,256,256]{3,2,1,0:T(8,128)(2,1)S(1)}, bf16[2,2,256,256]{3,2,1,0:T(8,128)(2,1)}, u32[]{:S(2)}) copy-start(bf16[2,2,256,256]{3,2,1,0:T(8,128)(2,1)} %get-tuple-element.78.kept) | copy-start | bytes 1572868
  41.7 11.2 %collective-permute-start.4 = (bf16[4,256,256]{2,1,0:T(8,128)(2,1)S(1)}, bf16[4,256,256]{2,1,0:T(8,128)(2,1)S(1)}, u32[]{:S(2)}, u32[]{:S(2)}) collective-permute-start(bf16[4,256,256]{2,1,0:T(8,128)(2,1)S(1)} %get-tuple-element.74), channel_id=1, source_target_pairs={{8,0},{16,8},{24,16},{32,24},{40,32},{48,40},{56,48},{64,56},{72,6... | collective-permute-start | bytes 1572872 | tf_op jit(solution)/shard_map/ppermute | solution.py:354
  46.7 6.2 %copy-start.1 = (bf16[2,1152,256]{2,1,0:T(8,128)(2,1)S(1)}, bf16[2,1152,256]{2,1,0:T(8,128)(2,1)}, u32[]{:S(2)}) copy-start(bf16[2,1152,256]{2,1,0:T(8,128)(2,1)} %get-tuple-element.81.total) | copy-start | bytes 3538948
  46.7 6.2 %copy-start.3 = (bf16[2,2,256,256]{3,2,1,0:T(8,128)(2,1)S(1)}, bf16[2,2,256,256]{3,2,1,0:T(8,128)(2,1)}, u32[]{:S(2)}) copy-start(bf16[2,2,256,256]{3,2,1,0:T(8,128)(2,1)} %get-tuple-element.82.kept) | copy-start | bytes 1572868
  49.3 9.2 %collective-permute-start.6 = (bf16[2,2,144,256]{3,2,1,0:T(8,128)(2,1)S(1)}, bf16[2,2,144,256]{3,2,1,0:T(8,128)(2,1)S(1)}, u32[]{:S(2)}, u32[]{:S(2)}) collective-permute-start(bf16[2,2,144,256]{3,2,1,0:T(8,128)(2,1)S(1)} %get-tuple-element.87), channel_id=1, source_target_pairs={{0,2},{2,0},{4,6},{6,4},{1,3},{3,1},{5,7},{7,5},{8,10},{10,8},{12,... | collective-permute-start | bytes 884744 | tf_op jit(solution)/shard_map/ppermute | solution.py:411
  50.8 9.6 %collective-permute-start.7 = (bf16[2,2,144,256]{3,2,1,0:T(8,128)(2,1)S(1)}, bf16[2,2,144,256]{3,2,1,0:T(8,128)(2,1)S(1)}, u32[]{:S(2)}, u32[]{:S(2)}) collective-permute-start(bf16[2,2,144,256]{3,2,1,0:T(8,128)(2,1)S(1)} %get-tuple-element.88), channel_id=1, source_target_pairs={{0,6},{2,4},{4,2},{6,0},{1,7},{3,5},{5,3},{7,1},{8,14},{10,12},{12... | collective-permute-start | bytes 884744 | tf_op jit(solution)/shard_map/ppermute | solution.py:411
  55.2 9.8 %collective-permute-start.10 = (bf16[2,2,144,256]{3,2,1,0:T(8,128)(2,1)S(1)}, bf16[2,2,144,256]{3,2,1,0:T(8,128)(2,1)S(1)}, u32[]{:S(2)}, u32[]{:S(2)}) collective-permute-start(bf16[2,2,144,256]{3,2,1,0:T(8,128)(2,1)S(1)} %get-tuple-element.93), channel_id=1, source_target_pairs={{0,2},{2,0},{4,6},{6,4},{1,3},{3,1},{5,7},{7,5},{8,10},{10,8},{12,... | collective-permute-start | bytes 884744 | tf_op jit(solution)/shard_map/ppermute | solution.py:411
  56.4 11.2 %collective-permute-start.11 = (bf16[2,2,144,256]{3,2,1,0:T(8,128)(2,1)S(1)}, bf16[2,2,144,256]{3,2,1,0:T(8,128)(2,1)S(1)}, u32[]{:S(2)}, u32[]{:S(2)}) collective-permute-start(bf16[2,2,144,256]{3,2,1,0:T(8,128)(2,1)S(1)} %get-tuple-element.94), channel_id=1, source_target_pairs={{0,6},{2,4},{4,2},{6,0},{1,7},{3,5},{5,3},{7,1},{8,14},{10,12},{12... | collective-permute-start | bytes 884744 | tf_op jit(solution)/shard_map/ppermute | solution.py:411
  60.5 9.3 %collective-permute-start.8 = (bf16[2,144,256]{2,1,0:T(8,128)(2,1)S(1)}, bf16[2,144,256]{2,1,0:T(8,128)(2,1)S(1)}, u32[]{:S(2)}, u32[]{:S(2)}) collective-permute-start(bf16[2,144,256]{2,1,0:T(8,128)(2,1)S(1)} %get-tuple-element.90), channel_id=1, source_target_pairs={{0,6},{2,4},{4,2},{6,0},{1,7},{3,5},{5,3},{7,1},{8,14},{10,12},{12... | collective-permute-start | bytes 442376 | tf_op jit(solution)/shard_map/ppermute | solution.py:425
  62.6 7.2 %collective-permute-start.9 = (bf16[2,144,256]{2,1,0:T(8,128)(2,1)S(1)}, bf16[2,144,256]{2,1,0:T(8,128)(2,1)S(1)}, u32[]{:S(2)}, u32[]{:S(2)}) collective-permute-start(bf16[2,144,256]{2,1,0:T(8,128)(2,1)S(1)} %get-tuple-element.91), channel_id=1, source_target_pairs={{0,2},{2,0},{4,6},{6,4},{1,3},{3,1},{5,7},{7,5},{8,10},{10,8},{12,... | collective-permute-start | bytes 442376 | tf_op jit(solution)/shard_map/ppermute | solution.py:425
  67.6 6.9 %collective-permute-start.12 = (bf16[2,144,256]{2,1,0:T(8,128)(2,1)S(1)}, bf16[2,144,256]{2,1,0:T(8,128)(2,1)S(1)}, u32[]{:S(2)}, u32[]{:S(2)}) collective-permute-start(bf16[2,144,256]{2,1,0:T(8,128)(2,1)S(1)} %get-tuple-element.98), channel_id=1, source_target_pairs={{0,6},{2,4},{4,2},{6,0},{1,7},{3,5},{5,3},{7,1},{8,14},{10,12},{12... | collective-permute-start | bytes 442376 | tf_op jit(solution)/shard_map/ppermute | solution.py:425
  69.8 5.1 %collective-permute-start.13 = (bf16[2,144,256]{2,1,0:T(8,128)(2,1)S(1)}, bf16[2,144,256]{2,1,0:T(8,128)(2,1)S(1)}, u32[]{:S(2)}, u32[]{:S(2)}) collective-permute-start(bf16[2,144,256]{2,1,0:T(8,128)(2,1)S(1)} %get-tuple-element.99), channel_id=1, source_target_pairs={{0,2},{2,0},{4,6},{6,4},{1,3},{3,1},{5,7},{7,5},{8,10},{10,8},{12,... | collective-permute-start | bytes 442376 | tf_op jit(solution)/shard_map/ppermute | solution.py:425
  69.9 15.2 %collective-permute-start.14 = (bf16[2,144,256]{2,1,0:T(8,128)(2,1)S(1)}, bf16[2,144,256]{2,1,0:T(8,128)(2,1)S(1)}, u32[]{:S(2)}, u32[]{:S(2)}) collective-permute-start(bf16[2,144,256]{2,1,0:T(8,128)(2,1)S(1)} %get-tuple-element.102), channel_id=1, source_target_pairs={{0,1},{1,0},{2,3},{3,2},{4,5},{5,4},{6,7},{7,6},{8,9},{9,8},{10,11... | collective-permute-start | bytes 442376 | tf_op jit(solution)/shard_map/ppermute | solution.py:436
  75.6 11.8 %collective-permute-start.15 = (bf16[2,144,256]{2,1,0:T(8,128)(2,1)S(1)}, bf16[2,144,256]{2,1,0:T(8,128)(2,1)S(1)}, u32[]{:S(2)}, u32[]{:S(2)}) collective-permute-start(bf16[2,144,256]{2,1,0:T(8,128)(2,1)S(1)} %get-tuple-element.103), channel_id=1, source_target_pairs={{0,1},{1,0},{2,3},{3,2},{4,5},{5,4},{6,7},{7,6},{8,9},{9,8},{10,11... | collective-permute-start | bytes 442376 | tf_op jit(solution)/shard_map/ppermute | solution.py:436

commit v4 on v3

--- a/solution.py
+++ b/solution.py
@@ -157,42 +157,35 @@
     return list(copies)
 
 
+def kernel_copies(half, width, kernels, held, sems):
+    wide = pl.ds(half * width, width)
+    return [
+        pltpu.make_async_copy(kernels.at[branch, :, wide], held.at[branch], sems.at[branch])
+        for branch in range(2)
+    ]
+
+
 def early_tick(tick, half, width, *refs):
     groups = width // GW
-    made, kept, turn, following = None, None, None, None
-    loads, outgoing = {}, []
+    loads, outgoing = [], []
     if tick == 0:
-        if half == 0:
-            states, kernels, earlier, made, kept, turn, following, stored, *refs = refs
-            sent, next_sems, out_sems, state_sem, stored_sems, held, sems = refs
-        else:
-            states, kernels, held, store_next, earlier, made, kept, turn, following, stored, *refs = refs
-            sent, next_sems, out_sems, state_sem, stored_sems = refs
-        wide = pl.ds(half * width, width)
-        (state_load,) = started(pltpu.make_async_copy(states.at[:, :, wide], made, state_sem))
-        if half == 0:
-            for branch in (1, 0):
-                (loads[branch],) = started(
-                    pltpu.make_async_copy(
-                        kernels.at[branch, :, wide], held.at[branch], sems.at[branch]
-                    )
-                )
-            later = pl.ds(width, width)
-            sources = [kernels.at[branch, :, later] for branch in range(2)]
-        else:
-            sources = [store_next.at[branch] for branch in range(2)]
-            for branch in (1, 0):
-                outgoing += started(
-                    pltpu.make_async_copy(held.at[branch], stored.at[branch], stored_sems.at[branch])
-                )
+        states, kernels, *refs = refs
+        if half:
+            held, *refs = refs
+        earlier, made, kept, turn, following, sent, out_sems, state_sem, next_sems, *refs = refs
+        (state_load,) = started(
+            pltpu.make_async_copy(states.at[:, :, pl.ds(half * width, width)], made, state_sem)
+        )
+        if not half:
+            held, sems = refs
+            loads = kernel_copies(half, width, kernels, held, sems)
+            started(*loads[::-1])
     else:
-        received, top, store_next, held, earlier, made, kept, turn, following, *refs = refs
-        sent, next_sems, out_sems, top_sem = refs
-        sources = [store_next.at[branch] for branch in range(2)]
-    for branch in (1, 0):
-        outgoing += started(
-            pltpu.make_async_copy(sources[branch], following.at[branch], next_sems.at[branch])
-        )
+        received, top, kernels, held, earlier, made, kept, turn, following, *refs = refs
+        sent, out_sems, top_sem, next_sems = refs
+    outgoing += started(
+        *kernel_copies((half + 1) % HALVES, width, kernels, following, next_sems)[::-1]
+    )
     turn[...] = jnp.zeros_like(turn)
     if tick:
         take_state(tick, half, width, received, top, made, top_sem)
@@ -200,13 +193,8 @@
         state_load.wait()
 
     def weights(group, branch):
-        if group == 0 and branch in loads:
+        if group == 0 and loads:
             loads[branch].wait()
-            outgoing.extend(
-                started(
-                    pltpu.make_async_copy(held.at[branch], stored.at[branch], stored_sems.at[branch])
-                )
-            )
         return taps_by_row(held, branch, group_lanes(group))
 
     def keep(group, branch, columns, rows):
@@ -264,7 +252,7 @@
         copy.wait()
 
 
-def last_tick(half, width, received, top, store_next, held, total, kept, earlier, *rest):
+def last_tick(half, width, received, top, kernels, held, total, kept, earlier, *rest):
     if half:
         rest = rest[1:]
     made, final, mine, *rest = rest
@@ -274,12 +262,7 @@
     turn, *rest = rest
     if half + 1 < HALVES:
         following, summed, top_sem, final_sem, next_sems = rest
-        for branch in (1, 0):
-            copies += started(
-                pltpu.make_async_copy(
-                    store_next.at[branch], following.at[branch], next_sems.at[branch]
-                )
-            )
+        copies += started(*kernel_copies(half + 1, width, kernels, following, next_sems)[::-1])
     else:
         summed, top_sem, final_sem = rest
     turn[...] = jnp.zeros_like(turn)
@@ -460,8 +443,7 @@
     dma = pltpu.SemaphoreType.DMA
     kept_scratch = pltpu.VMEM((2, 2, CELLS, width), jnp.bfloat16)
     turn = jnp.zeros((8, 128), jnp.float32)
-    held, stored = None, []
-    stored_type = pltpu.HBM((2, ROWS, width), jnp.bfloat16)
+    held = None
     made, kept = [None] * HALVES, [[] for _ in range(HALVES)]
     for tick in range(TICKS - 1):
         for half in range(HALVES):
@@ -485,35 +467,28 @@
                     name="early_terms",
                 )(*[in_hbm(plane) for side in kept for plane in side], turn)
             aliases = {}
-            outs = [state_type, kept_type, turn_type, held_type]
-            out_specs = [VMEM_REF, ANY_REF, VMEM_REF, VMEM_REF]
-            scratch = [kept_scratch, dma((2,)), dma((2,)), dma(())]
+            scratch = [kept_scratch, dma((2,)), dma(()), dma((2,))]
             if tick:
-                operands = [in_vmem(made[half]), top, stored[1 - half], held, turn]
+                operands = [in_vmem(made[half]), top, kernels, held, turn]
                 specs = [VMEM_REF, ANY_REF, ANY_REF, VMEM_REF, ANY_REF]
                 aliases = {0: 0}
+            elif half:
+                operands = [states, kernels, held, turn]
+                specs = [ANY_REF, ANY_REF, VMEM_REF, ANY_REF]
             else:
-                outs.append(stored_type)
-                out_specs.append(ANY_REF)
-                scratch.append(dma((2,)))
-                if half:
-                    operands = [states, kernels, held, stored[0], turn]
-                    specs = [ANY_REF, ANY_REF, VMEM_REF, ANY_REF, ANY_REF]
-                else:
-                    operands, specs = [states, kernels, turn], [ANY_REF] * 3
-                    scratch += [held_type, dma((2,))]
-            out, fields, turn, following, *rest = pl.pallas_call(
+                operands, specs = [states, kernels, turn], [ANY_REF] * 3
+                scratch += [held_type, dma((2,))]
+            out, fields, turn, following = pl.pallas_call(
                 functools.partial(early_tick, tick, half, width),
-                out_shape=tuple(outs),
+                out_shape=(state_type, kept_type, turn_type, held_type),
                 in_specs=specs,
-                out_specs=tuple(out_specs),
+                out_specs=(VMEM_REF, ANY_REF, VMEM_REF, VMEM_REF),
                 scratch_shapes=scratch,
                 input_output_aliases=aliases,
                 compiler_params=params(),
                 cost_estimate=cost(4, width),
                 name=f"tick_{tick}_{half}",
             )(*operands)
-            stored += [in_hbm(copy) for copy in rest]
             held = in_vmem(following)
             made[half] = passed_down(out)
             kept[half].append(fields)
@@ -522,7 +497,7 @@
     mine, theirs = [None] * HALVES, [None] * HALVES
     theirs_type = pltpu.VMEM((2, 2, SHARE, width), jnp.bfloat16)
     for half in range(HALVES):
-        operands = [in_vmem(made[half]), top, stored[1], held, total[half], kept[half][FIRST], turn]
+        operands = [in_vmem(made[half]), top, kernels, held, total[half], kept[half][FIRST], turn]
         specs = [VMEM_REF, ANY_REF, ANY_REF, VMEM_REF, VMEM_REF, VMEM_REF, ANY_REF]
         aliases = {0: 0}
         if half:

time: 88.7 us -> 88.6 us (level)
  no operation moved by 1% of the time
where the time goes in v4:
time: 88.6 us; the launch traced here: 88.2 us
  starting transfers between devices  46.6 us (53%)
  Pallas kernels  23.8 us (27%)
  waiting for transfers between devices  17 us (19%)
    ppermute x6, starting transfers between devices, passed_down(): lax.ppermute(value, 'section', [(source, source - 1) for source in range(...  26.4 us
    pallas_call x6, Pallas kernels, on_device(): pl.pallas_call(functools.partial(early_tick, tick, half, width), out_shap...  12.8 us
    ppermute x2, starting transfers between devices, summed_shares(): came_last.append(lax.ppermute(across, 'dp_1', [(0, 1), (1, 0)]))  9.07 us
    ppermute x2, waiting for transfers between devices, summed_shares(): came_last.append(lax.ppermute(across, 'dp_1', [(0, 1), (1, 0)]))  7.39 us
    ppermute x4, waiting for transfers between devices, summed_shares(): lax.ppermute(theirs[half][b], 'dp_0', pairs[b][0])  6.8 us
    ppermute x4, starting transfers between devices, summed_shares(): lax.ppermute(theirs[half][b], 'dp_0', pairs[b][0])  6.75 us
    pallas_call x2, Pallas kernels, on_device(): pl.pallas_call(functools.partial(last_tick, half, width), out_shape=(stat...  4.86 us
    ppermute x4, starting transfers between devices, summed_shares(): lax.ppermute(passed[b], 'dp_0', pairs[b][1])  4.37 us
  transfers between devices with their start and end apart: 16, of which 8 were waited for; matrix products, arithmetic and copies ran while one was open for 0% of the time, Pallas kernels for 22%

profile of v4, /device:TPU:24, one launch (start us, length us, event | category | flops | bytes accessed | tf_op | source)
XLA Modules:
  0.0 88.2 jit_solution(5173541981589676981)
XLA Ops:
  0.6 3.6 %tick_0_0.1 = (bf16[4,256,256]{2,1,0:T(8,128)(2,1)S(1)}, bf16[2,2,256,256]{3,2,1,0:T(8,128)(2,1)}, f32[8,128]{1,0:T(8,128)S(1)}, bf16[2,1152,256]{2,1,0:T(8,128)(2,1)S(1)}) custom-call(bf16[4,256,512]{2,1,0:T(8,128)(2,1)} %bitcast.21, bf16[2,1152,512]{2,1,0:T(8,128)(2,1)} %bitcast.7, f32[8,128]{1,0:T(8,128)S(1)} %broadcast_in_dim.6.refs_2_), custom_call_target="tpu_custom_call" | custom-call | flops 603979776 | bytes 1048576 | tf_op jit(solution)/shard_map/tick_0_0/pallas_call | solution.py:481
  4.2 6.2 %collective-permute-start.1 = (bf16[4,256,256]{2,1,0:T(8,128)(2,1)S(1)}, bf16[4,256,256]{2,1,0:T(8,128)(2,1)S(1)}, u32[]{:S(2)}, u32[]{:S(2)}) collective-permute-start(bf16[4,256,256]{2,1,0:T(8,128)(2,1)S(1)} %get-tuple-element.54), channel_id=1, source_target_pairs={{8,0},{16,8},{24,16},{32,24},{40,32},{48,40},{56,48},{64,56},{72,6... | collective-permute-start | bytes 1572872 | tf_op jit(solution)/shard_map/ppermute | solution.py:337
  10.4 2.7 %tick_0_1.1 = (bf16[4,256,256]{2,1,0:T(8,128)(2,1)S(1)}, bf16[2,2,256,256]{3,2,1,0:T(8,128)(2,1)}, f32[8,128]{1,0:T(8,128)S(1)}, bf16[2,1152,256]{2,1,0:T(8,128)(2,1)S(1)}) custom-call(bf16[4,256,512]{2,1,0:T(8,128)(2,1)} %bitcast.22, bf16[2,1152,512]{2,1,0:T(8,128)(2,1)} %bitcast.8, bf16[2,1152,256]{2,1,0:T(8,128)(2,1)S(1)} %get-tuple-element.51.refs_2_, ...), custom_call_target="tpu_custom_call" | custom-call | flops 603979776 | bytes 1048576 | tf_op jit(solution)/shard_map/tick_0_1/pallas_call | solution.py:481
  13.1 2.6 %collective-permute-start = (bf16[4,256,256]{2,1,0:T(8,128)(2,1)S(1)}, bf16[4,256,256]{2,1,0:T(8,128)(2,1)S(1)}, u32[]{:S(2)}, u32[]{:S(2)}) collective-permute-start(bf16[4,256,256]{2,1,0:T(8,128)(2,1)S(1)} %get-tuple-element.53), channel_id=1, source_target_pairs={{8,0},{16,8},{24,16},{32,24},{40,32},{48,40},{56,48},{64,56},{72,6... | collective-permute-start | bytes 1572872 | tf_op jit(solution)/shard_map/ppermute | solution.py:337
  15.7 1.3 %collective-permute-done.1.refs_0_ = bf16[4,256,256]{2,1,0:T(8,128)(2,1)S(1)} collective-permute-done((bf16[4,256,256]{2,1,0:T(8,128)(2,1)S(1)}, bf16[4,256,256]{2,1,0:T(8,128)(2,1)S(1)}, u32[]{:S(2)}, u32[]{:S(2)}) %collective-permute-start.1) | collective-permute-done | bytes 524320 | tf_op jit(solution)/shard_map/ppermute | solution.py:337
  17.1 1.6 %tick_1_0.1 = (bf16[4,256,256]{2,1,0:T(8,128)(2,1)S(1)}, bf16[2,2,256,256]{3,2,1,0:T(8,128)(2,1)}, f32[8,128]{1,0:T(8,128)S(1)}, bf16[2,1152,256]{2,1,0:T(8,128)(2,1)S(1)}) custom-call(bf16[4,256,256]{2,1,0:T(8,128)(2,1)S(1)} %collective-permute-done.1.refs_0_, bf16[3,4,256,512]{3,2,1,0:T(8,128)(2,1)} %bitcast.15, ...), custom_call_target="tpu_custom_call", output_to_operand_aliasing={{0}: (0, {})} | custom-call | flops 603979776 | bytes 1048576 | tf_op jit(solution)/shard_map/tick_1_0/pallas_call | solution.py:481
  18.7 6.5 %collective-permute-start.3 = (bf16[4,256,256]{2,1,0:T(8,128)(2,1)S(1)}, bf16[4,256,256]{2,1,0:T(8,128)(2,1)S(1)}, u32[]{:S(2)}, u32[]{:S(2)}) collective-permute-start(bf16[4,256,256]{2,1,0:T(8,128)(2,1)S(1)} %get-tuple-element.60), channel_id=1, source_target_pairs={{8,0},{16,8},{24,16},{32,24},{40,32},{48,40},{56,48},{64,56},{72,6... | collective-permute-start | bytes 1572872 | tf_op jit(solution)/shard_map/ppermute | solution.py:337
  25.2 0.0 collective-permute-done.refs_0_
  25.2 1.6 %tick_1_1.1 = (bf16[4,256,256]{2,1,0:T(8,128)(2,1)S(1)}, bf16[2,2,256,256]{3,2,1,0:T(8,128)(2,1)}, f32[8,128]{1,0:T(8,128)S(1)}, bf16[2,1152,256]{2,1,0:T(8,128)(2,1)S(1)}) custom-call(bf16[4,256,256]{2,1,0:T(8,128)(2,1)S(1)} %collective-permute-done.refs_0_, bf16[3,4,256,512]{3,2,1,0:T(8,128)(2,1)} %bitcast.16, ...), custom_call_target="tpu_custom_call", output_to_operand_aliasing={{0}: (0, {})} | custom-call | flops 603979776 | bytes 1048576 | tf_op jit(solution)/shard_map/tick_1_1/pallas_call | solution.py:481
  26.9 4.0 %collective-permute-start.2 = (bf16[4,256,256]{2,1,0:T(8,128)(2,1)S(1)}, bf16[4,256,256]{2,1,0:T(8,128)(2,1)S(1)}, u32[]{:S(2)}, u32[]{:S(2)}) collective-permute-start(bf16[4,256,256]{2,1,0:T(8,128)(2,1)S(1)} %get-tuple-element.59), channel_id=1, source_target_pairs={{8,0},{16,8},{24,16},{32,24},{40,32},{48,40},{56,48},{64,56},{72,6... | collective-permute-start | bytes 1572872 | tf_op jit(solution)/shard_map/ppermute | solution.py:337
  30.8 4.3 %early_terms.1 = (bf16[2,1152,256]{2,1,0:T(8,128)(2,1)}, bf16[2,1152,256]{2,1,0:T(8,128)(2,1)}, f32[8,128]{1,0:T(8,128)S(1)}) custom-call(bf16[2,2,256,256]{3,2,1,0:T(8,128)(2,1)} %get-tuple-element.62.refs_0_, bf16[2,2,256,256]{3,2,1,0:T(8,128)(2,1)} %get-tuple-element.63.refs_1_, bf16[2,2,256,256]{3,2,1,0:T(8,128)(2,1)} %get-tuple-element.64.refs_2_, ...), custom_call_target="tpu_custom_call" | custom-call | flops 1207959552 | bytes 1048576 | tf_op jit(solution)/shard_map/early_terms/pallas_call | solution.py:451
  35.2 0.0 collective-permute-done.3.refs_0_
  35.2 1.6 %tick_2_0.1 = (bf16[4,256,256]{2,1,0:T(8,128)(2,1)S(1)}, bf16[2,2,256,256]{3,2,1,0:T(8,128)(2,1)}, f32[8,128]{1,0:T(8,128)S(1)}, bf16[2,1152,256]{2,1,0:T(8,128)(2,1)S(1)}) custom-call(bf16[4,256,256]{2,1,0:T(8,128)(2,1)S(1)} %collective-permute-done.3.refs_0_, bf16[3,4,256,512]{3,2,1,0:T(8,128)(2,1)} %bitcast.17, ...), custom_call_target="tpu_custom_call", output_to_operand_aliasing={{0}: (0, {})} | custom-call | flops 603979776 | bytes 1048576 | tf_op jit(solution)/shard_map/tick_2_0/pallas_call | solution.py:481
  36.8 3.2 %collective-permute-start.5 = (bf16[4,256,256]{2,1,0:T(8,128)(2,1)S(1)}, bf16[4,256,256]{2,1,0:T(8,128)(2,1)S(1)}, u32[]{:S(2)}, u32[]{:S(2)}) collective-permute-start(bf16[4,256,256]{2,1,0:T(8,128)(2,1)S(1)} %get-tuple-element.71), channel_id=1, source_target_pairs={{8,0},{16,8},{24,16},{32,24},{40,32},{48,40},{56,48},{64,56},{72,6... | collective-permute-start | bytes 1572872 | tf_op jit(solution)/shard_map/ppermute | solution.py:337
  40.0 0.0 collective-permute-done.2.refs_0_
  40.0 0.0 copy-start.1
  40.0 0.0 copy-start.3
  40.1 1.6 %tick_2_1.1 = (bf16[4,256,256]{2,1,0:T(8,128)(2,1)S(1)}, bf16[2,2,256,256]{3,2,1,0:T(8,128)(2,1)}, f32[8,128]{1,0:T(8,128)S(1)}, bf16[2,1152,256]{2,1,0:T(8,128)(2,1)S(1)}) custom-call(bf16[4,256,256]{2,1,0:T(8,128)(2,1)S(1)} %collective-permute-done.2.refs_0_, bf16[3,4,256,512]{3,2,1,0:T(8,128)(2,1)} %bitcast.18, ...), custom_call_target="tpu_custom_call", output_to_operand_aliasing={{0}: (0, {})} | custom-call | flops 603979776 | bytes 1048576 | tf_op jit(solution)/shard_map/tick_2_1/pallas_call | solution.py:481
  41.7 4.0 %collective-permute-start.4 = (bf16[4,256,256]{2,1,0:T(8,128)(2,1)S(1)}, bf16[4,256,256]{2,1,0:T(8,128)(2,1)S(1)}, u32[]{:S(2)}, u32[]{:S(2)}) collective-permute-start(bf16[4,256,256]{2,1,0:T(8,128)(2,1)S(1)} %get-tuple-element.70), channel_id=1, source_target_pairs={{8,0},{16,8},{24,16},{32,24},{40,32},{48,40},{56,48},{64,56},{72,6... | collective-permute-start | bytes 1572872 | tf_op jit(solution)/shard_map/ppermute | solution.py:337
  45.7 1.0 %collective-permute-done.5.received = bf16[4,256,256]{2,1,0:T(8,128)(2,1)S(1)} collective-permute-done((bf16[4,256,256]{2,1,0:T(8,128)(2,1)S(1)}, bf16[4,256,256]{2,1,0:T(8,128)(2,1)S(1)}, u32[]{:S(2)}, u32[]{:S(2)}) %collective-permute-start.5) | collective-permute-done | bytes 524320 | tf_op jit(solution)/shard_map/ppermute | solution.py:337
  46.7 0.0 copy-done.1
  46.7 0.0 copy-done.3
  46.7 0.0 copy-start
  46.7 0.0 copy-start.2
  46.7 2.5 %last_tick_0.1 = (bf16[4,256,256]{2,1,0:T(8,128)(2,1)S(1)}, bf16[4,256,512]{2,1,0:T(8,128)(2,1)}, bf16[2,2,2,144,256]{4,3,2,1,0:T(8,128)(2,1)S(1)}, bf16[2,2,144...) custom-call(bf16[4,256,256]{2,1,0:T(8,128)(2,1)S(1)} %collective-per, ...), custom_call_target="tpu_custom_call", output_to_operand_aliasing={{0}: (0, {})} | custom-call | flops 905969664 | bytes 1048576 | tf_op jit(solution)/shard_map/last_tick_0/pallas_call | solution.py:508
  49.2 1.6 %collective-permute-start.6 = (bf16[2,2,144,256]{3,2,1,0:T(8,128)(2,1)S(1)}, bf16[2,2,144,256]{3,2,1,0:T(8,128)(2,1)S(1)}, u32[]{:S(2)}, u32[]{:S(2)}) collective-permute-start(bf16[2,2,144,256]{3,2,1,0:T(8,128)(2,1)S(1)} %get-tuple-element.83), channel_id=1, source_target_pairs={{0,2},{2,0},{4,6},{6,4},{1,3},{3,1},{5,7},{7,5},{8,10},{10,8},{12,... | collective-permute-start | bytes 884744 | tf_op jit(solution)/shard_map/ppermute | solution.py:394
  50.8 2.1 %collective-permute-start.7 = (bf16[2,2,144,256]{3,2,1,0:T(8,128)(2,1)S(1)}, bf16[2,2,144,256]{3,2,1,0:T(8,128)(2,1)S(1)}, u32[]{:S(2)}, u32[]{:S(2)}) collective-permute-start(bf16[2,2,144,256]{3,2,1,0:T(8,128)(2,1)S(1)} %get-tuple-element.84), channel_id=1, source_target_pairs={{0,6},{2,4},{4,2},{6,0},{1,7},{3,5},{5,3},{7,1},{8,14},{10,12},{12... | collective-permute-start | bytes 884744 | tf_op jit(solution)/shard_map/ppermute | solution.py:394
  52.9 0.0 collective-permute-done.4.received
  52.9 0.0 copy-done
  52.9 0.0 copy-done.2
  52.9 2.3 %last_tick_1.1 = (bf16[4,256,256]{2,1,0:T(8,128)(2,1)S(1)}, bf16[4,256,512]{2,1,0:T(8,128)(2,1)}, bf16[2,2,2,144,256]{4,3,2,1,0:T(8,128)(2,1)S(1)}, bf16[2,2,144...) custom-call(bf16[4,256,256]{2,1,0:T(8,128)(2,1)S(1)} %collective-per, ...), custom_call_target="tpu_custom_call", output_to_operand_aliasing={{0}: (0, {}), {1}: (7, {})} | custom-call | flops 905969664 | bytes 1048576 | tf_op jit(solution)/shard_map/last_tick_1/pallas_call | solution.py:508
  55.3 1.0 %collective-permute-start.10 = (bf16[2,2,144,256]{3,2,1,0:T(8,128)(2,1)S(1)}, bf16[2,2,144,256]{3,2,1,0:T(8,128)(2,1)S(1)}, u32[]{:S(2)}, u32[]{:S(2)}) collective-permute-start(bf16[2,2,144,256]{3,2,1,0:T(8,128)(2,1)S(1)} %get-tuple-element.89), channel_id=1, source_target_pairs={{0,2},{2,0},{4,6},{6,4},{1,3},{3,1},{5,7},{7,5},{8,10},{10,8},{12,... | collective-permute-start | bytes 884744 | tf_op jit(solution)/shard_map/ppermute | solution.py:394
  56.3 2.1 %collective-permute-start.11 = (bf16[2,2,144,256]{3,2,1,0:T(8,128)(2,1)S(1)}, bf16[2,2,144,256]{3,2,1,0:T(8,128)(2,1)S(1)}, u32[]{:S(2)}, u32[]{:S(2)}) collective-permute-start(bf16[2,2,144,256]{3,2,1,0:T(8,128)(2,1)S(1)} %get-tuple-element.90), channel_id=1, source_target_pairs={{0,6},{2,4},{4,2},{6,0},{1,7},{3,5},{5,3},{7,1},{8,14},{10,12},{12... | collective-permute-start | bytes 884744 | tf_op jit(solution)/shard_map/ppermute | solution.py:394
  58.3 0.0 collective-permute-done.6.refs_0_
  58.4 2.2 %collective-permute-done.7.refs_1_ = bf16[2,2,144,256]{3,2,1,0:T(8,128)(2,1)S(1)} collective-permute-done((bf16[2,2,144,256]{3,2,1,0:T(8,128)(2,1)S(1)}, bf16[2,2,144,256]{3,2,1,0:T(8,128)(2,1)S(1)}, u32[]{:S(2)}, u32[]{:S(2)}) %collective-permute-start.7) | collective-permute-done | bytes 294944 | tf_op jit(solution)/shard_map/ppermute | solution.py:394
  60.6 0.1 first_sum_0.1
  60.6 2.2 %collective-permute-start.8 = (bf16[2,144,256]{2,1,0:T(8,128)(2,1)S(1)}, bf16[2,144,256]{2,1,0:T(8,128)(2,1)S(1)}, u32[]{:S(2)}, u32[]{:S(2)}) collective-permute-start(bf16[2,144,256]{2,1,0:T(8,128)(2,1)S(1)} %get-tuple-element.86), channel_id=1, source_target_pairs={{0,6},{2,4},{4,2},{6,0},{1,7},{3,5},{5,3},{7,1},{8,14},{10,12},{12... | collective-permute-start | bytes 442376 | tf_op jit(solution)/shard_map/ppermute | solution.py:408
  62.8 0.0 collective-permute-start.9
  62.8 2.2 %collective-permute-done.10.refs_0_ = bf16[2,2,144,256]{3,2,1,0:T(8,128)(2,1)S(1)} collective-permute-done((bf16[2,2,144,256]{3,2,1,0:T(8,128)(2,1)S(1)}, bf16[2,2,144,256]{3,2,1,0:T(8,128)(2,1)S(1)}, u32[]{:S(2)}, u32[]{:S(2)}) %collective-permute-start.10) | collective-permute-done | bytes 294944 | tf_op jit(solution)/shard_map/ppermute | solution.py:394
  65.0 2.4 %collective-permute-done.11.refs_1_ = bf16[2,2,144,256]{3,2,1,0:T(8,128)(2,1)S(1)} collective-permute-done((bf16[2,2,144,256]{3,2,1,0:T(8,128)(2,1)S(1)}, bf16[2,2,144,256]{3,2,1,0:T(8,128)(2,1)S(1)}, u32[]{:S(2)}, u32[]{:S(2)}) %collective-permute-start.11) | collective-permute-done | bytes 294944 | tf_op jit(solution)/shard_map/ppermute | solution.py:394
  67.4 0.1 first_sum_1.1
  67.5 2.2 %collective-permute-start.12 = (bf16[2,144,256]{2,1,0:T(8,128)(2,1)S(1)}, bf16[2,144,256]{2,1,0:T(8,128)(2,1)S(1)}, u32[]{:S(2)}, u32[]{:S(2)}) collective-permute-start(bf16[2,144,256]{2,1,0:T(8,128)(2,1)S(1)} %get-tuple-element.94), channel_id=1, source_target_pairs={{0,6},{2,4},{4,2},{6,0},{1,7},{3,5},{5,3},{7,1},{8,14},{10,12},{12... | collective-permute-start | bytes 442376 | tf_op jit(solution)/shard_map/ppermute | solution.py:408
  69.7 0.0 collective-permute-start.13
  69.7 0.0 collective-permute-done.8.refs_2_
  69.7 0.0 collective-permute-done.9.refs_3_
  69.7 0.1 second_sum_0.1
  69.8 4.6 %collective-permute-start.14 = (bf16[2,144,256]{2,1,0:T(8,128)(2,1)S(1)}, bf16[2,144,256]{2,1,0:T(8,128)(2,1)S(1)}, u32[]{:S(2)}, u32[]{:S(2)}) collective-permute-start(bf16[2,144,256]{2,1,0:T(8,128)(2,1)S(1)} %get-tuple-element.98), channel_id=1, source_target_pairs={{0,1},{1,0},{2,3},{3,2},{4,5},{5,4},{6,7},{7,6},{8,9},{9,8},{10,11... | collective-permute-start | bytes 442376 | tf_op jit(solution)/shard_map/ppermute | solution.py:419
  74.4 0.0 collective-permute-done.12.refs_2_
  74.4 0.4 collective-permute-done.13.refs_3_
  74.8 0.6 second_sum_1.1
  75.5 4.5 %collective-permute-start.15 = (bf16[2,144,256]{2,1,0:T(8,128)(2,1)S(1)}, bf16[2,144,256]{2,1,0:T(8,128)(2,1)S(1)}, u32[]{:S(2)}, u32[]{:S(2)}) collective-permute-start(bf16[2,144,256]{2,1,0:T(8,128)(2,1)S(1)} %get-tuple-element.99), channel_id=1, source_target_pairs={{0,1},{1,0},{2,3},{3,2},{4,5},{5,4},{6,7},{7,6},{8,9},{9,8},{10,11... | collective-permute-start | bytes 442376 | tf_op jit(solution)/shard_map/ppermute | solution.py:419
  79.9 5.2 %collective-permute-done.14.refs_2_ = bf16[2,144,256]{2,1,0:T(8,128)(2,1)S(1)} collective-permute-done((bf16[2,144,256]{2,1,0:T(8,128)(2,1)S(1)}, bf16[2,144,256]{2,1,0:T(8,128)(2,1)S(1)}, u32[]{:S(2)}, u32[]{:S(2)}) %collective-permute-start.14) | collective-permute-done | bytes 147488 | tf_op jit(solution)/shard_map/ppermute | solution.py:419
  85.1 2.2 %collective-permute-done.15.refs_3_ = bf16[2,144,256]{2,1,0:T(8,128)(2,1)S(1)} collective-permute-done((bf16[2,144,256]{2,1,0:T(8,128)(2,1)S(1)}, bf16[2,144,256]{2,1,0:T(8,128)(2,1)S(1)}, u32[]{:S(2)}, u32[]{:S(2)}) %collective-permute-start.15) | collective-permute-done | bytes 147488 | tf_op jit(solution)/shard_map/ppermute | solution.py:419
  87.3 0.9 last_sum.1
  (1 shorter events, 0.0 us)
Async XLA Ops:
  4.2 12.8 %collective-permute-start.1 = (bf16[4,256,256]{2,1,0:T(8,128)(2,1)S(1)}, bf16[4,256,256]{2,1,0:T(8,128)(2,1)S(1)}, u32[]{:S(2)}, u32[]{:S(2)}) collective-permute-start(bf16[4,256,256]{2,1,0:T(8,128)(2,1)S(1)} %get-tuple-element.54), channel_id=1, source_target_pairs={{8,0},{16,8},{24,16},{32,24},{40,32},{48,40},{56,48},{64,56},{72,6... | collective-permute-start | bytes 1572872 | tf_op jit(solution)/shard_map/ppermute | solution.py:337
  13.1 12.1 %collective-permute-start = (bf16[4,256,256]{2,1,0:T(8,128)(2,1)S(1)}, bf16[4,256,256]{2,1,0:T(8,128)(2,1)S(1)}, u32[]{:S(2)}, u32[]{:S(2)}) collective-permute-start(bf16[4,256,256]{2,1,0:T(8,128)(2,1)S(1)} %get-tuple-element.53), channel_id=1, source_target_pairs={{8,0},{16,8},{24,16},{32,24},{40,32},{48,40},{56,48},{64,56},{72,6... | collective-permute-start | bytes 1572872 | tf_op jit(solution)/shard_map/ppermute | solution.py:337
  18.7 16.5 %collective-permute-start.3 = (bf16[4,256,256]{2,1,0:T(8,128)(2,1)S(1)}, bf16[4,256,256]{2,1,0:T(8,128)(2,1)S(1)}, u32[]{:S(2)}, u32[]{:S(2)}) collective-permute-start(bf16[4,256,256]{2,1,0:T(8,128)(2,1)S(1)} %get-tuple-element.60), channel_id=1, source_target_pairs={{8,0},{16,8},{24,16},{32,24},{40,32},{48,40},{56,48},{64,56},{72,6... | collective-permute-start | bytes 1572872 | tf_op jit(solution)/shard_map/ppermute | solution.py:337
  26.9 13.2 %collective-permute-start.2 = (bf16[4,256,256]{2,1,0:T(8,128)(2,1)S(1)}, bf16[4,256,256]{2,1,0:T(8,128)(2,1)S(1)}, u32[]{:S(2)}, u32[]{:S(2)}) collective-permute-start(bf16[4,256,256]{2,1,0:T(8,128)(2,1)S(1)} %get-tuple-element.59), channel_id=1, source_target_pairs={{8,0},{16,8},{24,16},{32,24},{40,32},{48,40},{56,48},{64,56},{72,6... | collective-permute-start | bytes 1572872 | tf_op jit(solution)/shard_map/ppermute | solution.py:337
  36.8 9.9 %collective-permute-start.5 = (bf16[4,256,256]{2,1,0:T(8,128)(2,1)S(1)}, bf16[4,256,256]{2,1,0:T(8,128)(2,1)S(1)}, u32[]{:S(2)}, u32[]{:S(2)}) collective-permute-start(bf16[4,256,256]{2,1,0:T(8,128)(2,1)S(1)} %get-tuple-element.71), channel_id=1, source_target_pairs={{8,0},{16,8},{24,16},{32,24},{40,32},{48,40},{56,48},{64,56},{72,6... | collective-permute-start | bytes 1572872 | tf_op jit(solution)/shard_map/ppermute | solution.py:337
  40.0 6.7 %copy-start.1 = (bf16[2,1152,256]{2,1,0:T(8,128)(2,1)S(1)}, bf16[2,1152,256]{2,1,0:T(8,128)(2,1)}, u32[]{:S(2)}) copy-start(bf16[2,1152,256]{2,1,0:T(8,128)(2,1)} %get-tuple-element.73.total) | copy-start | bytes 3538948
  40.0 6.7 %copy-start.3 = (bf16[2,2,256,256]{3,2,1,0:T(8,128)(2,1)S(1)}, bf16[2,2,256,256]{3,2,1,0:T(8,128)(2,1)}, u32[]{:S(2)}) copy-start(bf16[2,2,256,256]{3,2,1,0:T(8,128)(2,1)} %get-tuple-element.74.kept) | copy-start | bytes 1572868
  41.7 11.2 %collective-permute-start.4 = (bf16[4,256,256]{2,1,0:T(8,128)(2,1)S(1)}, bf16[4,256,256]{2,1,0:T(8,128)(2,1)S(1)}, u32[]{:S(2)}, u32[]{:S(2)}) collective-permute-start(bf16[4,256,256]{2,1,0:T(8,128)(2,1)S(1)} %get-tuple-element.70), channel_id=1, source_target_pairs={{8,0},{16,8},{24,16},{32,24},{40,32},{48,40},{56,48},{64,56},{72,6... | collective-permute-start | bytes 1572872 | tf_op jit(solution)/shard_map/ppermute | solution.py:337
  46.7 6.2 %copy-start = (bf16[2,1152,256]{2,1,0:T(8,128)(2,1)S(1)}, bf16[2,1152,256]{2,1,0:T(8,128)(2,1)}, u32[]{:S(2)}) copy-start(bf16[2,1152,256]{2,1,0:T(8,128)(2,1)} %get-tuple-element.77.total) | copy-start | bytes 3538948
  46.7 6.2 %copy-start.2 = (bf16[2,2,256,256]{3,2,1,0:T(8,128)(2,1)S(1)}, bf16[2,2,256,256]{3,2,1,0:T(8,128)(2,1)}, u32[]{:S(2)}) copy-start(bf16[2,2,256,256]{3,2,1,0:T(8,128)(2,1)} %get-tuple-element.78.kept) | copy-start | bytes 1572868
  49.2 9.1 %collective-permute-start.6 = (bf16[2,2,144,256]{3,2,1,0:T(8,128)(2,1)S(1)}, bf16[2,2,144,256]{3,2,1,0:T(8,128)(2,1)S(1)}, u32[]{:S(2)}, u32[]{:S(2)}) collective-permute-start(bf16[2,2,144,256]{3,2,1,0:T(8,128)(2,1)S(1)} %get-tuple-element.83), channel_id=1, source_target_pairs={{0,2},{2,0},{4,6},{6,4},{1,3},{3,1},{5,7},{7,5},{8,10},{10,8},{12,... | collective-permute-start | bytes 884744 | tf_op jit(solution)/shard_map/ppermute | solution.py:394
  50.8 9.7 %collective-permute-start.7 = (bf16[2,2,144,256]{3,2,1,0:T(8,128)(2,1)S(1)}, bf16[2,2,144,256]{3,2,1,0:T(8,128)(2,1)S(1)}, u32[]{:S(2)}, u32[]{:S(2)}) collective-permute-start(bf16[2,2,144,256]{3,2,1,0:T(8,128)(2,1)S(1)} %get-tuple-element.84), channel_id=1, source_target_pairs={{0,6},{2,4},{4,2},{6,0},{1,7},{3,5},{5,3},{7,1},{8,14},{10,12},{12... | collective-permute-start | bytes 884744 | tf_op jit(solution)/shard_map/ppermute | solution.py:394
  55.3 9.8 %collective-permute-start.10 = (bf16[2,2,144,256]{3,2,1,0:T(8,128)(2,1)S(1)}, bf16[2,2,144,256]{3,2,1,0:T(8,128)(2,1)S(1)}, u32[]{:S(2)}, u32[]{:S(2)}) collective-permute-start(bf16[2,2,144,256]{3,2,1,0:T(8,128)(2,1)S(1)} %get-tuple-element.89), channel_id=1, source_target_pairs={{0,2},{2,0},{4,6},{6,4},{1,3},{3,1},{5,7},{7,5},{8,10},{10,8},{12,... | collective-permute-start | bytes 884744 | tf_op jit(solution)/shard_map/ppermute | solution.py:394
  56.3 11.2 %collective-permute-start.11 = (bf16[2,2,144,256]{3,2,1,0:T(8,128)(2,1)S(1)}, bf16[2,2,144,256]{3,2,1,0:T(8,128)(2,1)S(1)}, u32[]{:S(2)}, u32[]{:S(2)}) collective-permute-start(bf16[2,2,144,256]{3,2,1,0:T(8,128)(2,1)S(1)} %get-tuple-element.90), channel_id=1, source_target_pairs={{0,6},{2,4},{4,2},{6,0},{1,7},{3,5},{5,3},{7,1},{8,14},{10,12},{12... | collective-permute-start | bytes 884744 | tf_op jit(solution)/shard_map/ppermute | solution.py:394
  60.6 9.0 %collective-permute-start.8 = (bf16[2,144,256]{2,1,0:T(8,128)(2,1)S(1)}, bf16[2,144,256]{2,1,0:T(8,128)(2,1)S(1)}, u32[]{:S(2)}, u32[]{:S(2)}) collective-permute-start(bf16[2,144,256]{2,1,0:T(8,128)(2,1)S(1)} %get-tuple-element.86), channel_id=1, source_target_pairs={{0,6},{2,4},{4,2},{6,0},{1,7},{3,5},{5,3},{7,1},{8,14},{10,12},{12... | collective-permute-start | bytes 442376 | tf_op jit(solution)/shard_map/ppermute | solution.py:408
  62.8 6.9 %collective-permute-start.9 = (bf16[2,144,256]{2,1,0:T(8,128)(2,1)S(1)}, bf16[2,144,256]{2,1,0:T(8,128)(2,1)S(1)}, u32[]{:S(2)}, u32[]{:S(2)}) collective-permute-start(bf16[2,144,256]{2,1,0:T(8,128)(2,1)S(1)} %get-tuple-element.87), channel_id=1, source_target_pairs={{0,2},{2,0},{4,6},{6,4},{1,3},{3,1},{5,7},{7,5},{8,10},{10,8},{12,... | collective-permute-start | bytes 442376 | tf_op jit(solution)/shard_map/ppermute | solution.py:408
  67.5 6.9 %collective-permute-start.12 = (bf16[2,144,256]{2,1,0:T(8,128)(2,1)S(1)}, bf16[2,144,256]{2,1,0:T(8,128)(2,1)S(1)}, u32[]{:S(2)}, u32[]{:S(2)}) collective-permute-start(bf16[2,144,256]{2,1,0:T(8,128)(2,1)S(1)} %get-tuple-element.94), channel_id=1, source_target_pairs={{0,6},{2,4},{4,2},{6,0},{1,7},{3,5},{5,3},{7,1},{8,14},{10,12},{12... | collective-permute-start | bytes 442376 | tf_op jit(solution)/shard_map/ppermute | solution.py:408
  69.7 5.1 %collective-permute-start.13 = (bf16[2,144,256]{2,1,0:T(8,128)(2,1)S(1)}, bf16[2,144,256]{2,1,0:T(8,128)(2,1)S(1)}, u32[]{:S(2)}, u32[]{:S(2)}) collective-permute-start(bf16[2,144,256]{2,1,0:T(8,128)(2,1)S(1)} %get-tuple-element.95), channel_id=1, source_target_pairs={{0,2},{2,0},{4,6},{6,4},{1,3},{3,1},{5,7},{7,5},{8,10},{10,8},{12,... | collective-permute-start | bytes 442376 | tf_op jit(solution)/shard_map/ppermute | solution.py:408
  69.8 15.3 %collective-permute-start.14 = (bf16[2,144,256]{2,1,0:T(8,128)(2,1)S(1)}, bf16[2,144,256]{2,1,0:T(8,128)(2,1)S(1)}, u32[]{:S(2)}, u32[]{:S(2)}) collective-permute-start(bf16[2,144,256]{2,1,0:T(8,128)(2,1)S(1)} %get-tuple-element.98), channel_id=1, source_target_pairs={{0,1},{1,0},{2,3},{3,2},{4,5},{5,4},{6,7},{7,6},{8,9},{9,8},{10,11... | collective-permute-start | bytes 442376 | tf_op jit(solution)/shard_map/ppermute | solution.py:419
  75.5 11.9 %collective-permute-start.15 = (bf16[2,144,256]{2,1,0:T(8,128)(2,1)S(1)}, bf16[2,144,256]{2,1,0:T(8,128)(2,1)S(1)}, u32[]{:S(2)}, u32[]{:S(2)}) collective-permute-start(bf16[2,144,256]{2,1,0:T(8,128)(2,1)S(1)} %get-tuple-element.99), channel_id=1, source_target_pairs={{0,1},{1,0},{2,3},{3,2},{4,5},{5,4},{6,7},{7,6},{8,9},{9,8},{10,11... | collective-permute-start | bytes 442376 | tf_op jit(solution)/shard_map/ppermute | solution.py:419

commit v5 on v4

--- a/solution.py
+++ b/solution.py
@@ -372,13 +372,12 @@
         across[branch] = total[1].astype(jnp.bfloat16)
 
 
-def last_sum(*refs):
-    kept, came, out = refs[:HALVES], refs[HALVES:-1], refs[-1]
-    for half in range(HALVES):
-        width = kept[half].shape[-1]
-        out[:, :, pl.ds(half * width, width)] = (
-            kept[half][...] + came[half][...].astype(jnp.float32)
-        ) * (1.0 / (HW * HW))
+def last_sum(half, kept, came, before, out, total, sem):
+    width = kept.shape[-1]
+    total[...] = (kept[...] + came[...].astype(jnp.float32)) * (1.0 / (HW * HW))
+    copy = pltpu.make_async_copy(total, out.at[:, :, pl.ds(half * width, width)], sem)
+    copy.start()
+    copy.wait()
 
 
 def summed_shares(mine, theirs, turn):
@@ -418,14 +417,22 @@
         )(mine[half], *came[half], *came_next[half], turn)
         came_last.append(lax.ppermute(across, "dp_1", [(0, 1), (1, 0)]))
         kept.append(own)
-    return pl.pallas_call(
-        last_sum,
-        out_shape=jax.ShapeDtypeStruct((2, SHARE, width * HALVES), jnp.float32),
-        in_specs=[VMEM_REF] * (2 * HALVES),
-        out_specs=VMEM_REF,
-        compiler_params=params(),
-        name="last_sum",
-    )(*[in_vmem(own) for own in kept], *[in_vmem(part) for part in came_last])
+    out = turn
+    for half in halves:
+        out = pl.pallas_call(
+            functools.partial(last_sum, half),
+            out_shape=pltpu.HBM((2, SHARE, width * HALVES), jnp.float32),
+            in_specs=[VMEM_REF, VMEM_REF, ANY_REF],
+            out_specs=ANY_REF,
+            scratch_shapes=[
+                pltpu.VMEM((2, SHARE, width), jnp.float32),
+                pltpu.SemaphoreType.DMA(()),
+            ],
+            input_output_aliases={2: 0} if half else {},
+            compiler_params=params(),
+            name=f"last_sum_{half}",
+        )(in_vmem(kept[half]), in_vmem(came_last[half]), in_hbm(out) if half else out)
+    return out
 
 
 def on_device(section_states, conv_kernels, top_feed):

time: 88.6 us -> 88.7 us (level)
  no operation moved by 1% of the time
where the time goes in v5:
time: 88.7 us; the launch traced here: 88.3 us
  starting transfers between devices  46.7 us (53%)
  Pallas kernels  23.9 us (27%)
  waiting for transfers between devices  16.7 us (19%)
  between operations  1 us (1%)
    ppermute x6, starting transfers between devices, passed_down(): lax.ppermute(value, 'section', [(source, source - 1) for source in range(...  26.4 us
    pallas_call x6, Pallas kernels, on_device(): pl.pallas_call(functools.partial(early_tick, tick, half, width), out_shap...  12.8 us
    ppermute x2, starting transfers between devices, summed_shares(): came_last.append(lax.ppermute(across, 'dp_1', [(0, 1), (1, 0)]))  9.15 us
    ppermute x2, waiting for transfers between devices, summed_shares(): came_last.append(lax.ppermute(across, 'dp_1', [(0, 1), (1, 0)]))  7.07 us
    ppermute x4, waiting for transfers between devices, summed_shares(): lax.ppermute(theirs[half][b], 'dp_0', pairs[b][0])  6.8 us
    ppermute x4, starting transfers between devices, summed_shares(): lax.ppermute(theirs[half][b], 'dp_0', pairs[b][0])  6.75 us
    pallas_call x2, Pallas kernels, on_device(): pl.pallas_call(functools.partial(last_tick, half, width), out_shape=(stat...  4.86 us
    ppermute x4, starting transfers between devices, summed_shares(): lax.ppermute(passed[b], 'dp_0', pairs[b][1])  4.37 us
  transfers between devices with their start and end apart: 16, of which 8 were waited for; matrix products, arithmetic and copies ran while one was open for 0% of the time, Pallas kernels for 22%

profile of v5, /device:TPU:24, one launch (start us, length us, event | category | flops | bytes accessed | tf_op | source)
XLA Modules:
  0.0 88.3 jit_solution(2034137080943170134)
XLA Ops:
  0.6 3.6 %tick_0_0.1 = (bf16[4,256,256]{2,1,0:T(8,128)(2,1)S(1)}, bf16[2,2,256,256]{3,2,1,0:T(8,128)(2,1)}, f32[8,128]{1,0:T(8,128)S(1)}, bf16[2,1152,256]{2,1,0:T(8,128)(2,1)S(1)}) custom-call(bf16[4,256,512]{2,1,0:T(8,128)(2,1)} %bitcast.21, bf16[2,1152,512]{2,1,0:T(8,128)(2,1)} %bitcast.7, f32[8,128]{1,0:T(8,128)S(1)} %broadcast_in_dim.6.refs_2_), custom_call_target="tpu_custom_call" | custom-call | flops 603979776 | bytes 1048576 | tf_op jit(solution)/shard_map/tick_0_0/pallas_call | solution.py:488
  4.2 6.2 %collective-permute-start.1 = (bf16[4,256,256]{2,1,0:T(8,128)(2,1)S(1)}, bf16[4,256,256]{2,1,0:T(8,128)(2,1)S(1)}, u32[]{:S(2)}, u32[]{:S(2)}) collective-permute-start(bf16[4,256,256]{2,1,0:T(8,128)(2,1)S(1)} %get-tuple-element.55), channel_id=1, source_target_pairs={{8,0},{16,8},{24,16},{32,24},{40,32},{48,40},{56,48},{64,56},{72,6... | collective-permute-start | bytes 1572872 | tf_op jit(solution)/shard_map/ppermute | solution.py:337
  10.4 2.7 %tick_0_1.1 = (bf16[4,256,256]{2,1,0:T(8,128)(2,1)S(1)}, bf16[2,2,256,256]{3,2,1,0:T(8,128)(2,1)}, f32[8,128]{1,0:T(8,128)S(1)}, bf16[2,1152,256]{2,1,0:T(8,128)(2,1)S(1)}) custom-call(bf16[4,256,512]{2,1,0:T(8,128)(2,1)} %bitcast.22, bf16[2,1152,512]{2,1,0:T(8,128)(2,1)} %bitcast.8, bf16[2,1152,256]{2,1,0:T(8,128)(2,1)S(1)} %get-tuple-element.52.refs_2_, ...), custom_call_target="tpu_custom_call" | custom-call | flops 603979776 | bytes 1048576 | tf_op jit(solution)/shard_map/tick_0_1/pallas_call | solution.py:488
  13.1 2.6 %collective-permute-start = (bf16[4,256,256]{2,1,0:T(8,128)(2,1)S(1)}, bf16[4,256,256]{2,1,0:T(8,128)(2,1)S(1)}, u32[]{:S(2)}, u32[]{:S(2)}) collective-permute-start(bf16[4,256,256]{2,1,0:T(8,128)(2,1)S(1)} %get-tuple-element.54), channel_id=1, source_target_pairs={{8,0},{16,8},{24,16},{32,24},{40,32},{48,40},{56,48},{64,56},{72,6... | collective-permute-start | bytes 1572872 | tf_op jit(solution)/shard_map/ppermute | solution.py:337
  15.7 1.3 %collective-permute-done.1.refs_0_ = bf16[4,256,256]{2,1,0:T(8,128)(2,1)S(1)} collective-permute-done((bf16[4,256,256]{2,1,0:T(8,128)(2,1)S(1)}, bf16[4,256,256]{2,1,0:T(8,128)(2,1)S(1)}, u32[]{:S(2)}, u32[]{:S(2)}) %collective-permute-start.1) | collective-permute-done | bytes 524320 | tf_op jit(solution)/shard_map/ppermute | solution.py:337
  17.1 1.6 %tick_1_0.1 = (bf16[4,256,256]{2,1,0:T(8,128)(2,1)S(1)}, bf16[2,2,256,256]{3,2,1,0:T(8,128)(2,1)}, f32[8,128]{1,0:T(8,128)S(1)}, bf16[2,1152,256]{2,1,0:T(8,128)(2,1)S(1)}) custom-call(bf16[4,256,256]{2,1,0:T(8,128)(2,1)S(1)} %collective-permute-done.1.refs_0_, bf16[3,4,256,512]{3,2,1,0:T(8,128)(2,1)} %bitcast.15, ...), custom_call_target="tpu_custom_call", output_to_operand_aliasing={{0}: (0, {})} | custom-call | flops 603979776 | bytes 1048576 | tf_op jit(solution)/shard_map/tick_1_0/pallas_call | solution.py:488
  18.7 6.5 %collective-permute-start.3 = (bf16[4,256,256]{2,1,0:T(8,128)(2,1)S(1)}, bf16[4,256,256]{2,1,0:T(8,128)(2,1)S(1)}, u32[]{:S(2)}, u32[]{:S(2)}) collective-permute-start(bf16[4,256,256]{2,1,0:T(8,128)(2,1)S(1)} %get-tuple-element.61), channel_id=1, source_target_pairs={{8,0},{16,8},{24,16},{32,24},{40,32},{48,40},{56,48},{64,56},{72,6... | collective-permute-start | bytes 1572872 | tf_op jit(solution)/shard_map/ppermute | solution.py:337
  25.2 0.0 collective-permute-done.refs_0_
  25.2 1.6 %tick_1_1.1 = (bf16[4,256,256]{2,1,0:T(8,128)(2,1)S(1)}, bf16[2,2,256,256]{3,2,1,0:T(8,128)(2,1)}, f32[8,128]{1,0:T(8,128)S(1)}, bf16[2,1152,256]{2,1,0:T(8,128)(2,1)S(1)}) custom-call(bf16[4,256,256]{2,1,0:T(8,128)(2,1)S(1)} %collective-permute-done.refs_0_, bf16[3,4,256,512]{3,2,1,0:T(8,128)(2,1)} %bitcast.16, ...), custom_call_target="tpu_custom_call", output_to_operand_aliasing={{0}: (0, {})} | custom-call | flops 603979776 | bytes 1048576 | tf_op jit(solution)/shard_map/tick_1_1/pallas_call | solution.py:488
  26.9 4.0 %collective-permute-start.2 = (bf16[4,256,256]{2,1,0:T(8,128)(2,1)S(1)}, bf16[4,256,256]{2,1,0:T(8,128)(2,1)S(1)}, u32[]{:S(2)}, u32[]{:S(2)}) collective-permute-start(bf16[4,256,256]{2,1,0:T(8,128)(2,1)S(1)} %get-tuple-element.60), channel_id=1, source_target_pairs={{8,0},{16,8},{24,16},{32,24},{40,32},{48,40},{56,48},{64,56},{72,6... | collective-permute-start | bytes 1572872 | tf_op jit(solution)/shard_map/ppermute | solution.py:337
  30.8 4.3 %early_terms.1 = (bf16[2,1152,256]{2,1,0:T(8,128)(2,1)}, bf16[2,1152,256]{2,1,0:T(8,128)(2,1)}, f32[8,128]{1,0:T(8,128)S(1)}) custom-call(bf16[2,2,256,256]{3,2,1,0:T(8,128)(2,1)} %get-tuple-element.63.refs_0_, bf16[2,2,256,256]{3,2,1,0:T(8,128)(2,1)} %get-tuple-element.64.refs_1_, bf16[2,2,256,256]{3,2,1,0:T(8,128)(2,1)} %get-tuple-element.65.refs_2_, ...), custom_call_target="tpu_custom_call" | custom-call | flops 1207959552 | bytes 1048576 | tf_op jit(solution)/shard_map/early_terms/pallas_call | solution.py:458
  35.2 0.0 collective-permute-done.3.refs_0_
  35.2 1.6 %tick_2_0.1 = (bf16[4,256,256]{2,1,0:T(8,128)(2,1)S(1)}, bf16[2,2,256,256]{3,2,1,0:T(8,128)(2,1)}, f32[8,128]{1,0:T(8,128)S(1)}, bf16[2,1152,256]{2,1,0:T(8,128)(2,1)S(1)}) custom-call(bf16[4,256,256]{2,1,0:T(8,128)(2,1)S(1)} %collective-permute-done.3.refs_0_, bf16[3,4,256,512]{3,2,1,0:T(8,128)(2,1)} %bitcast.17, ...), custom_call_target="tpu_custom_call", output_to_operand_aliasing={{0}: (0, {})} | custom-call | flops 603979776 | bytes 1048576 | tf_op jit(solution)/shard_map/tick_2_0/pallas_call | solution.py:488
  36.8 3.2 %collective-permute-start.5 = (bf16[4,256,256]{2,1,0:T(8,128)(2,1)S(1)}, bf16[4,256,256]{2,1,0:T(8,128)(2,1)S(1)}, u32[]{:S(2)}, u32[]{:S(2)}) collective-permute-start(bf16[4,256,256]{2,1,0:T(8,128)(2,1)S(1)} %get-tuple-element.72), channel_id=1, source_target_pairs={{8,0},{16,8},{24,16},{32,24},{40,32},{48,40},{56,48},{64,56},{72,6... | collective-permute-start | bytes 1572872 | tf_op jit(solution)/shard_map/ppermute | solution.py:337
  40.0 0.0 collective-permute-done.2.refs_0_
  40.0 0.0 copy-start.1
  40.0 0.0 copy-start.3
  40.1 1.6 %tick_2_1.1 = (bf16[4,256,256]{2,1,0:T(8,128)(2,1)S(1)}, bf16[2,2,256,256]{3,2,1,0:T(8,128)(2,1)}, f32[8,128]{1,0:T(8,128)S(1)}, bf16[2,1152,256]{2,1,0:T(8,128)(2,1)S(1)}) custom-call(bf16[4,256,256]{2,1,0:T(8,128)(2,1)S(1)} %collective-permute-done.2.refs_0_, bf16[3,4,256,512]{3,2,1,0:T(8,128)(2,1)} %bitcast.18, ...), custom_call_target="tpu_custom_call", output_to_operand_aliasing={{0}: (0, {})} | custom-call | flops 603979776 | bytes 1048576 | tf_op jit(solution)/shard_map/tick_2_1/pallas_call | solution.py:488
  41.7 4.0 %collective-permute-start.4 = (bf16[4,256,256]{2,1,0:T(8,128)(2,1)S(1)}, bf16[4,256,256]{2,1,0:T(8,128)(2,1)S(1)}, u32[]{:S(2)}, u32[]{:S(2)}) collective-permute-start(bf16[4,256,256]{2,1,0:T(8,128)(2,1)S(1)} %get-tuple-element.71), channel_id=1, source_target_pairs={{8,0},{16,8},{24,16},{32,24},{40,32},{48,40},{56,48},{64,56},{72,6... | collective-permute-start | bytes 1572872 | tf_op jit(solution)/shard_map/ppermute | solution.py:337
  45.7 1.0 %collective-permute-done.5.received = bf16[4,256,256]{2,1,0:T(8,128)(2,1)S(1)} collective-permute-done((bf16[4,256,256]{2,1,0:T(8,128)(2,1)S(1)}, bf16[4,256,256]{2,1,0:T(8,128)(2,1)S(1)}, u32[]{:S(2)}, u32[]{:S(2)}) %collective-permute-start.5) | collective-permute-done | bytes 524320 | tf_op jit(solution)/shard_map/ppermute | solution.py:337
  46.7 0.0 copy-done.1
  46.7 0.0 copy-done.3
  46.7 0.0 copy-start
  46.7 0.0 copy-start.2
  46.7 2.5 %last_tick_0.1 = (bf16[4,256,256]{2,1,0:T(8,128)(2,1)S(1)}, bf16[4,256,512]{2,1,0:T(8,128)(2,1)}, bf16[2,2,2,144,256]{4,3,2,1,0:T(8,128)(2,1)S(1)}, bf16[2,2,144...) custom-call(bf16[4,256,256]{2,1,0:T(8,128)(2,1)S(1)} %collective-per, ...), custom_call_target="tpu_custom_call", output_to_operand_aliasing={{0}: (0, {})} | custom-call | flops 905969664 | bytes 1048576 | tf_op jit(solution)/shard_map/last_tick_0/pallas_call | solution.py:515
  49.2 1.6 %collective-permute-start.8 = (bf16[2,2,144,256]{3,2,1,0:T(8,128)(2,1)S(1)}, bf16[2,2,144,256]{3,2,1,0:T(8,128)(2,1)S(1)}, u32[]{:S(2)}, u32[]{:S(2)}) collective-permute-start(bf16[2,2,144,256]{3,2,1,0:T(8,128)(2,1)S(1)} %get-tuple-element.87), channel_id=1, source_target_pairs={{0,2},{2,0},{4,6},{6,4},{1,3},{3,1},{5,7},{7,5},{8,10},{10,8},{12,... | collective-permute-start | bytes 884744 | tf_op jit(solution)/shard_map/ppermute | solution.py:393
  50.8 2.1 %collective-permute-start.9 = (bf16[2,2,144,256]{3,2,1,0:T(8,128)(2,1)S(1)}, bf16[2,2,144,256]{3,2,1,0:T(8,128)(2,1)S(1)}, u32[]{:S(2)}, u32[]{:S(2)}) collective-permute-start(bf16[2,2,144,256]{3,2,1,0:T(8,128)(2,1)S(1)} %get-tuple-element.88), channel_id=1, source_target_pairs={{0,6},{2,4},{4,2},{6,0},{1,7},{3,5},{5,3},{7,1},{8,14},{10,12},{12... | collective-permute-start | bytes 884744 | tf_op jit(solution)/shard_map/ppermute | solution.py:393
  52.9 0.0 collective-permute-done.4.received
  52.9 0.0 copy-done
  52.9 0.0 copy-done.2
  52.9 2.3 %last_tick_1.1 = (bf16[4,256,256]{2,1,0:T(8,128)(2,1)S(1)}, bf16[4,256,512]{2,1,0:T(8,128)(2,1)}, bf16[2,2,2,144,256]{4,3,2,1,0:T(8,128)(2,1)S(1)}, bf16[2,2,144...) custom-call(bf16[4,256,256]{2,1,0:T(8,128)(2,1)S(1)} %collective-per, ...), custom_call_target="tpu_custom_call", output_to_operand_aliasing={{0}: (0, {}), {1}: (7, {})} | custom-call | flops 905969664 | bytes 1048576 | tf_op jit(solution)/shard_map/last_tick_1/pallas_call | solution.py:515
  55.3 1.0 %collective-permute-start.6 = (bf16[2,2,144,256]{3,2,1,0:T(8,128)(2,1)S(1)}, bf16[2,2,144,256]{3,2,1,0:T(8,128)(2,1)S(1)}, u32[]{:S(2)}, u32[]{:S(2)}) collective-permute-start(bf16[2,2,144,256]{3,2,1,0:T(8,128)(2,1)S(1)} %get-tuple-element.84), channel_id=1, source_target_pairs={{0,2},{2,0},{4,6},{6,4},{1,3},{3,1},{5,7},{7,5},{8,10},{10,8},{12,... | collective-permute-start | bytes 884744 | tf_op jit(solution)/shard_map/ppermute | solution.py:393
  56.3 2.1 %collective-permute-start.7 = (bf16[2,2,144,256]{3,2,1,0:T(8,128)(2,1)S(1)}, bf16[2,2,144,256]{3,2,1,0:T(8,128)(2,1)S(1)}, u32[]{:S(2)}, u32[]{:S(2)}) collective-permute-start(bf16[2,2,144,256]{3,2,1,0:T(8,128)(2,1)S(1)} %get-tuple-element.85), channel_id=1, source_target_pairs={{0,6},{2,4},{4,2},{6,0},{1,7},{3,5},{5,3},{7,1},{8,14},{10,12},{12... | collective-permute-start | bytes 884744 | tf_op jit(solution)/shard_map/ppermute | solution.py:393
  58.3 0.0 collective-permute-done.8.refs_0_
  58.4 2.2 %collective-permute-done.9.refs_1_ = bf16[2,2,144,256]{3,2,1,0:T(8,128)(2,1)S(1)} collective-permute-done((bf16[2,2,144,256]{3,2,1,0:T(8,128)(2,1)S(1)}, bf16[2,2,144,256]{3,2,1,0:T(8,128)(2,1)S(1)}, u32[]{:S(2)}, u32[]{:S(2)}) %collective-permute-start.9) | collective-permute-done | bytes 294944 | tf_op jit(solution)/shard_map/ppermute | solution.py:393
  60.6 0.1 first_sum_0.1
  60.6 2.2 %collective-permute-start.12 = (bf16[2,144,256]{2,1,0:T(8,128)(2,1)S(1)}, bf16[2,144,256]{2,1,0:T(8,128)(2,1)S(1)}, u32[]{:S(2)}, u32[]{:S(2)}) collective-permute-start(bf16[2,144,256]{2,1,0:T(8,128)(2,1)S(1)} %get-tuple-element.93), channel_id=1, source_target_pairs={{0,6},{2,4},{4,2},{6,0},{1,7},{3,5},{5,3},{7,1},{8,14},{10,12},{12... | collective-permute-start | bytes 442376 | tf_op jit(solution)/shard_map/ppermute | solution.py:407
  62.8 0.0 collective-permute-start.13
  62.8 2.2 %collective-permute-done.6.refs_0_ = bf16[2,2,144,256]{3,2,1,0:T(8,128)(2,1)S(1)} collective-permute-done((bf16[2,2,144,256]{3,2,1,0:T(8,128)(2,1)S(1)}, bf16[2,2,144,256]{3,2,1,0:T(8,128)(2,1)S(1)}, u32[]{:S(2)}, u32[]{:S(2)}) %collective-permute-start.6) | collective-permute-done | bytes 294944 | tf_op jit(solution)/shard_map/ppermute | solution.py:393
  65.0 2.4 %collective-permute-done.7.refs_1_ = bf16[2,2,144,256]{3,2,1,0:T(8,128)(2,1)S(1)} collective-permute-done((bf16[2,2,144,256]{3,2,1,0:T(8,128)(2,1)S(1)}, bf16[2,2,144,256]{3,2,1,0:T(8,128)(2,1)S(1)}, u32[]{:S(2)}, u32[]{:S(2)}) %collective-permute-start.7) | collective-permute-done | bytes 294944 | tf_op jit(solution)/shard_map/ppermute | solution.py:393
  67.4 0.1 first_sum_1.1
  67.5 2.2 %collective-permute-start.10 = (bf16[2,144,256]{2,1,0:T(8,128)(2,1)S(1)}, bf16[2,144,256]{2,1,0:T(8,128)(2,1)S(1)}, u32[]{:S(2)}, u32[]{:S(2)}) collective-permute-start(bf16[2,144,256]{2,1,0:T(8,128)(2,1)S(1)} %get-tuple-element.91), channel_id=1, source_target_pairs={{0,6},{2,4},{4,2},{6,0},{1,7},{3,5},{5,3},{7,1},{8,14},{10,12},{12... | collective-permute-start | bytes 442376 | tf_op jit(solution)/shard_map/ppermute | solution.py:407
  69.7 0.0 collective-permute-start.11
  69.7 0.0 collective-permute-done.12.refs_2_
  69.7 0.0 collective-permute-done.13.refs_3_
  69.7 0.1 second_sum_0.1
  69.8 4.6 %collective-permute-start.15 = (bf16[2,144,256]{2,1,0:T(8,128)(2,1)S(1)}, bf16[2,144,256]{2,1,0:T(8,128)(2,1)S(1)}, u32[]{:S(2)}, u32[]{:S(2)}) collective-permute-start(bf16[2,144,256]{2,1,0:T(8,128)(2,1)S(1)} %get-tuple-element.100), channel_id=1, source_target_pairs={{0,1},{1,0},{2,3},{3,2},{4,5},{5,4},{6,7},{7,6},{8,9},{9,8},{10,11... | collective-permute-start | bytes 442376 | tf_op jit(solution)/shard_map/ppermute | solution.py:418
  74.4 0.0 collective-permute-done.10.refs_2_
  74.4 0.4 collective-permute-done.11.refs_3_
  74.8 0.1 second_sum_1.1
  74.9 4.6 %collective-permute-start.14 = (bf16[2,144,256]{2,1,0:T(8,128)(2,1)S(1)}, bf16[2,144,256]{2,1,0:T(8,128)(2,1)S(1)}, u32[]{:S(2)}, u32[]{:S(2)}) collective-permute-start(bf16[2,144,256]{2,1,0:T(8,128)(2,1)S(1)} %get-tuple-element.98), channel_id=1, source_target_pairs={{0,1},{1,0},{2,3},{3,2},{4,5},{5,4},{6,7},{7,6},{8,9},{9,8},{10,11... | collective-permute-start | bytes 442376 | tf_op jit(solution)/shard_map/ppermute | solution.py:418
  79.5 6.3 %collective-permute-done.15.came = bf16[2,144,256]{2,1,0:T(8,128)(2,1)S(1)} collective-permute-done((bf16[2,144,256]{2,1,0:T(8,128)(2,1)S(1)}, bf16[2,144,256]{2,1,0:T(8,128)(2,1)S(1)}, u32[]{:S(2)}, u32[]{:S(2)}) %collective-permute-start.15) | collective-permute-done | bytes 147488 | tf_op jit(solution)/shard_map/ppermute | solution.py:418
  85.8 0.8 last_sum_0.1.before
  86.5 0.8 collective-permute-done.14.came
  87.3 0.8 last_sum_1.1
  (1 shorter events, 0.0 us)
Async XLA Ops:
  4.2 12.8 %collective-permute-start.1 = (bf16[4,256,256]{2,1,0:T(8,128)(2,1)S(1)}, bf16[4,256,256]{2,1,0:T(8,128)(2,1)S(1)}, u32[]{:S(2)}, u32[]{:S(2)}) collective-permute-start(bf16[4,256,256]{2,1,0:T(8,128)(2,1)S(1)} %get-tuple-element.55), channel_id=1, source_target_pairs={{8,0},{16,8},{24,16},{32,24},{40,32},{48,40},{56,48},{64,56},{72,6... | collective-permute-start | bytes 1572872 | tf_op jit(solution)/shard_map/ppermute | solution.py:337
  13.1 12.1 %collective-permute-start = (bf16[4,256,256]{2,1,0:T(8,128)(2,1)S(1)}, bf16[4,256,256]{2,1,0:T(8,128)(2,1)S(1)}, u32[]{:S(2)}, u32[]{:S(2)}) collective-permute-start(bf16[4,256,256]{2,1,0:T(8,128)(2,1)S(1)} %get-tuple-element.54), channel_id=1, source_target_pairs={{8,0},{16,8},{24,16},{32,24},{40,32},{48,40},{56,48},{64,56},{72,6... | collective-permute-start | bytes 1572872 | tf_op jit(solution)/shard_map/ppermute | solution.py:337
  18.7 16.5 %collective-permute-start.3 = (bf16[4,256,256]{2,1,0:T(8,128)(2,1)S(1)}, bf16[4,256,256]{2,1,0:T(8,128)(2,1)S(1)}, u32[]{:S(2)}, u32[]{:S(2)}) collective-permute-start(bf16[4,256,256]{2,1,0:T(8,128)(2,1)S(1)} %get-tuple-element.61), channel_id=1, source_target_pairs={{8,0},{16,8},{24,16},{32,24},{40,32},{48,40},{56,48},{64,56},{72,6... | collective-permute-start | bytes 1572872 | tf_op jit(solution)/shard_map/ppermute | solution.py:337
  26.9 13.2 %collective-permute-start.2 = (bf16[4,256,256]{2,1,0:T(8,128)(2,1)S(1)}, bf16[4,256,256]{2,1,0:T(8,128)(2,1)S(1)}, u32[]{:S(2)}, u32[]{:S(2)}) collective-permute-start(bf16[4,256,256]{2,1,0:T(8,128)(2,1)S(1)} %get-tuple-element.60), channel_id=1, source_target_pairs={{8,0},{16,8},{24,16},{32,24},{40,32},{48,40},{56,48},{64,56},{72,6... | collective-permute-start | bytes 1572872 | tf_op jit(solution)/shard_map/ppermute | solution.py:337
  36.8 9.9 %collective-permute-start.5 = (bf16[4,256,256]{2,1,0:T(8,128)(2,1)S(1)}, bf16[4,256,256]{2,1,0:T(8,128)(2,1)S(1)}, u32[]{:S(2)}, u32[]{:S(2)}) collective-permute-start(bf16[4,256,256]{2,1,0:T(8,128)(2,1)S(1)} %get-tuple-element.72), channel_id=1, source_target_pairs={{8,0},{16,8},{24,16},{32,24},{40,32},{48,40},{56,48},{64,56},{72,6... | collective-permute-start | bytes 1572872 | tf_op jit(solution)/shard_map/ppermute | solution.py:337
  40.0 6.7 %copy-start.1 = (bf16[2,1152,256]{2,1,0:T(8,128)(2,1)S(1)}, bf16[2,1152,256]{2,1,0:T(8,128)(2,1)}, u32[]{:S(2)}) copy-start(bf16[2,1152,256]{2,1,0:T(8,128)(2,1)} %get-tuple-element.74.total) | copy-start | bytes 3538948
  40.0 6.7 %copy-start.3 = (bf16[2,2,256,256]{3,2,1,0:T(8,128)(2,1)S(1)}, bf16[2,2,256,256]{3,2,1,0:T(8,128)(2,1)}, u32[]{:S(2)}) copy-start(bf16[2,2,256,256]{3,2,1,0:T(8,128)(2,1)} %get-tuple-element.75.kept) | copy-start | bytes 1572868
  41.7 11.2 %collective-permute-start.4 = (bf16[4,256,256]{2,1,0:T(8,128)(2,1)S(1)}, bf16[4,256,256]{2,1,0:T(8,128)(2,1)S(1)}, u32[]{:S(2)}, u32[]{:S(2)}) collective-permute-start(bf16[4,256,256]{2,1,0:T(8,128)(2,1)S(1)} %get-tuple-element.71), channel_id=1, source_target_pairs={{8,0},{16,8},{24,16},{32,24},{40,32},{48,40},{56,48},{64,56},{72,6... | collective-permute-start | bytes 1572872 | tf_op jit(solution)/shard_map/ppermute | solution.py:337
  46.7 6.2 %copy-start = (bf16[2,1152,256]{2,1,0:T(8,128)(2,1)S(1)}, bf16[2,1152,256]{2,1,0:T(8,128)(2,1)}, u32[]{:S(2)}) copy-start(bf16[2,1152,256]{2,1,0:T(8,128)(2,1)} %get-tuple-element.78.total) | copy-start | bytes 3538948
  46.7 6.2 %copy-start.2 = (bf16[2,2,256,256]{3,2,1,0:T(8,128)(2,1)S(1)}, bf16[2,2,256,256]{3,2,1,0:T(8,128)(2,1)}, u32[]{:S(2)}) copy-start(bf16[2,2,256,256]{3,2,1,0:T(8,128)(2,1)} %get-tuple-element.79.kept) | copy-start | bytes 1572868
  49.2 9.1 %collective-permute-start.8 = (bf16[2,2,144,256]{3,2,1,0:T(8,128)(2,1)S(1)}, bf16[2,2,144,256]{3,2,1,0:T(8,128)(2,1)S(1)}, u32[]{:S(2)}, u32[]{:S(2)}) collective-permute-start(bf16[2,2,144,256]{3,2,1,0:T(8,128)(2,1)S(1)} %get-tuple-element.87), channel_id=1, source_target_pairs={{0,2},{2,0},{4,6},{6,4},{1,3},{3,1},{5,7},{7,5},{8,10},{10,8},{12,... | collective-permute-start | bytes 884744 | tf_op jit(solution)/shard_map/ppermute | solution.py:393
  50.8 9.7 %collective-permute-start.9 = (bf16[2,2,144,256]{3,2,1,0:T(8,128)(2,1)S(1)}, bf16[2,2,144,256]{3,2,1,0:T(8,128)(2,1)S(1)}, u32[]{:S(2)}, u32[]{:S(2)}) collective-permute-start(bf16[2,2,144,256]{3,2,1,0:T(8,128)(2,1)S(1)} %get-tuple-element.88), channel_id=1, source_target_pairs={{0,6},{2,4},{4,2},{6,0},{1,7},{3,5},{5,3},{7,1},{8,14},{10,12},{12... | collective-permute-start | bytes 884744 | tf_op jit(solution)/shard_map/ppermute | solution.py:393
  55.3 9.8 %collective-permute-start.6 = (bf16[2,2,144,256]{3,2,1,0:T(8,128)(2,1)S(1)}, bf16[2,2,144,256]{3,2,1,0:T(8,128)(2,1)S(1)}, u32[]{:S(2)}, u32[]{:S(2)}) collective-permute-start(bf16[2,2,144,256]{3,2,1,0:T(8,128)(2,1)S(1)} %get-tuple-element.84), channel_id=1, source_target_pairs={{0,2},{2,0},{4,6},{6,4},{1,3},{3,1},{5,7},{7,5},{8,10},{10,8},{12,... | collective-permute-start | bytes 884744 | tf_op jit(solution)/shard_map/ppermute | solution.py:393
  56.3 11.2 %collective-permute-start.7 = (bf16[2,2,144,256]{3,2,1,0:T(8,128)(2,1)S(1)}, bf16[2,2,144,256]{3,2,1,0:T(8,128)(2,1)S(1)}, u32[]{:S(2)}, u32[]{:S(2)}) collective-permute-start(bf16[2,2,144,256]{3,2,1,0:T(8,128)(2,1)S(1)} %get-tuple-element.85), channel_id=1, source_target_pairs={{0,6},{2,4},{4,2},{6,0},{1,7},{3,5},{5,3},{7,1},{8,14},{10,12},{12... | collective-permute-start | bytes 884744 | tf_op jit(solution)/shard_map/ppermute | solution.py:393
  60.6 9.0 %collective-permute-start.12 = (bf16[2,144,256]{2,1,0:T(8,128)(2,1)S(1)}, bf16[2,144,256]{2,1,0:T(8,128)(2,1)S(1)}, u32[]{:S(2)}, u32[]{:S(2)}) collective-permute-start(bf16[2,144,256]{2,1,0:T(8,128)(2,1)S(1)} %get-tuple-element.93), channel_id=1, source_target_pairs={{0,6},{2,4},{4,2},{6,0},{1,7},{3,5},{5,3},{7,1},{8,14},{10,12},{12... | collective-permute-start | bytes 442376 | tf_op jit(solution)/shard_map/ppermute | solution.py:407
  62.8 6.9 %collective-permute-start.13 = (bf16[2,144,256]{2,1,0:T(8,128)(2,1)S(1)}, bf16[2,144,256]{2,1,0:T(8,128)(2,1)S(1)}, u32[]{:S(2)}, u32[]{:S(2)}) collective-permute-start(bf16[2,144,256]{2,1,0:T(8,128)(2,1)S(1)} %get-tuple-element.94), channel_id=1, source_target_pairs={{0,2},{2,0},{4,6},{6,4},{1,3},{3,1},{5,7},{7,5},{8,10},{10,8},{12,... | collective-permute-start | bytes 442376 | tf_op jit(solution)/shard_map/ppermute | solution.py:407
  67.5 6.9 %collective-permute-start.10 = (bf16[2,144,256]{2,1,0:T(8,128)(2,1)S(1)}, bf16[2,144,256]{2,1,0:T(8,128)(2,1)S(1)}, u32[]{:S(2)}, u32[]{:S(2)}) collective-permute-start(bf16[2,144,256]{2,1,0:T(8,128)(2,1)S(1)} %get-tuple-element.91), channel_id=1, source_target_pairs={{0,6},{2,4},{4,2},{6,0},{1,7},{3,5},{5,3},{7,1},{8,14},{10,12},{12... | collective-permute-start | bytes 442376 | tf_op jit(solution)/shard_map/ppermute | solution.py:407
  69.7 5.1 %collective-permute-start.11 = (bf16[2,144,256]{2,1,0:T(8,128)(2,1)S(1)}, bf16[2,144,256]{2,1,0:T(8,128)(2,1)S(1)}, u32[]{:S(2)}, u32[]{:S(2)}) collective-permute-start(bf16[2,144,256]{2,1,0:T(8,128)(2,1)S(1)} %get-tuple-element.92), channel_id=1, source_target_pairs={{0,2},{2,0},{4,6},{6,4},{1,3},{3,1},{5,7},{7,5},{8,10},{10,8},{12,... | collective-permute-start | bytes 442376 | tf_op jit(solution)/shard_map/ppermute | solution.py:407
  69.8 16.0 %collective-permute-start.15 = (bf16[2,144,256]{2,1,0:T(8,128)(2,1)S(1)}, bf16[2,144,256]{2,1,0:T(8,128)(2,1)S(1)}, u32[]{:S(2)}, u32[]{:S(2)}) collective-permute-start(bf16[2,144,256]{2,1,0:T(8,128)(2,1)S(1)} %get-tuple-element.100), channel_id=1, source_target_pairs={{0,1},{1,0},{2,3},{3,2},{4,5},{5,4},{6,7},{7,6},{8,9},{9,8},{10,11... | collective-permute-start | bytes 442376 | tf_op jit(solution)/shard_map/ppermute | solution.py:418
  74.9 12.4 %collective-permute-start.14 = (bf16[2,144,256]{2,1,0:T(8,128)(2,1)S(1)}, bf16[2,144,256]{2,1,0:T(8,128)(2,1)S(1)}, u32[]{:S(2)}, u32[]{:S(2)}) collective-permute-start(bf16[2,144,256]{2,1,0:T(8,128)(2,1)S(1)} %get-tuple-element.98), channel_id=1, source_target_pairs={{0,1},{1,0},{2,3},{3,2},{4,5},{5,4},{6,7},{7,6},{8,9},{9,8},{10,11... | collective-permute-start | bytes 442376 | tf_op jit(solution)/shard_map/ppermute | solution.py:418
